TPU v7x, 32 devices: a whole 2x2x4 slice. The times are simulated.
32 devices in a mesh: seq: 8 (over z, x), kv: 4 (over y, core).
Axes of the slice: x: 2, y: 2, z: 4, core: 2. Of those that a mesh axis runs over, the one named last changes fastest.
Arguments:
- queries: bfloat16 [4096, 1024], P('seq'), may hold values from -88 to 88
- keys: bfloat16 [64, 64, 1024], P('seq', 'kv'), may hold values from -4 to 4
- values: bfloat16 [64, 64, 1024], P('seq', 'kv'), may hold values from -6 to 6
- layout: int32 [64, 15], replicated, may hold values from -1 to 63, as said below
- grad_out: bfloat16 [4096, 1024], P('seq'), may hold values from -6 to 6
Outputs:
- attended: bfloat16 [4096, 1024], P('seq')
- grad_q: bfloat16 [4096, 1024], P('seq')
- grad_k: bfloat16 [64, 64, 1024], P('seq', 'kv')
- grad_v: bfloat16 [64, 64, 1024], P('seq', 'kv')
Inputs may be any that keep to these rules, and one draw needn't show every extreme that they name: `layout`: write query block b as 8 w + i with 0 <= i < 8. Row b lists the summary block of each window 0 .. w - 1 in order of windows, then the blocks 8 w .. 8 w + i in order, then -1 in the remaining entries. The summary block of window u is one of the blocks 8 u .. 8 u + 7 and is the same in every row.
All inputs are finite; a program needn't handle non-finite values.
Results may differ from a plain program's by a relative error of at most 0.038.
Values may be sent and summed in bfloat16 or wider, within the bound.
No kernel may reach another device: no remote copies, remote signals or barrier semaphores. Data moves between devices by JAX's collectives and lax.ppermute only.
A program may use at most 128 MiB of HBM per device.

v0:
```python
import functools
import math

import jax
import jax.numpy as jnp
from jax import lax
from jax.experimental import pallas as pl
from jax.experimental.pallas import tpu as pltpu
from jax.sharding import PartitionSpec as P

HEADS = 8
COLUMNS = 2
CORES = 2
GROUP = 2
SMALL = pl.CostEstimate(flops=0, bytes_accessed=0, transcendentals=0)
HIDDEN = -1e30
NT = (((1,), (1,)), ((), ()))
NN = (((1,), (0,)), ((), ()))
TN = (((0,), (0,)), ((), ()))
IN_HBM = pl.BlockSpec(memory_space=pltpu.HBM)
WHOLE = pl.BlockSpec(memory_space=pltpu.VMEM)
LIMIT = pltpu.CompilerParams(vmem_limit_bytes=12 * 1024 * 1024)


def dot(a, b, dims):
    return lax.dot_general(a, b, dims, preferred_element_type=jnp.float32)


def wide(rows, width):
    return jnp.concatenate([rows] * (width // rows.shape[1]), axis=1)


def base2_scale(head_dim):
    return math.log2(math.e) / math.sqrt(head_dim)


def pick_kernel(table_hbm, keys_hbm, values_hbm, mine_ref, theirs_ref, pair_ref, sent_ref, block_ref, table_ref, sems):
    window = lax.axis_index("seq")
    core = lax.axis_index("kv") % CORES
    _, blocks, part_tok, half = mine_ref.shape
    copies = [pltpu.make_async_copy(table_hbm, table_ref, sems.at[0])]
    for which, ref in enumerate((keys_hbm, values_hbm)):
        for side, out_ref in enumerate((mine_ref, theirs_ref)):
            cols = pl.ds(pl.multiple_of((core ^ side) * half, half), half)
            copies.append(
                pltpu.make_async_copy(ref.at[:, :, cols], out_ref.at[which], sems.at[len(copies)])
            )
    for copy in copies:
        copy.start()
    copies[0].wait()
    pick = jnp.minimum(window, lax.axis_size("seq") - 2)
    entry = lax.broadcasted_iota(jnp.int32, table_ref.shape, 0)
    row = lax.broadcasted_iota(jnp.int32, table_ref.shape, 1)
    here = (entry == pick) & (row == table_ref.shape[1] - 1)
    named = jnp.where(here, table_ref[...].astype(jnp.float32), -1.0)
    named = jnp.max(jnp.max(named, axis=1, keepdims=True), axis=0, keepdims=True)
    block = jnp.clip(named - (window * blocks).astype(jnp.float32), 0.0, blocks - 1.0)
    block_ref[...] = jnp.broadcast_to(block, block_ref.shape)
    block = jnp.broadcast_to(block, (part_tok, half))
    for copy in copies[1:]:
        copy.wait()
    for ref, out_ref in ((mine_ref, pair_ref), (theirs_ref, sent_ref)):
        for which in range(2):
            chosen = ref[which, 0].astype(jnp.float32)
            for b in range(1, blocks):
                chosen = jnp.where(block == b, ref[which, b].astype(jnp.float32), chosen)
            out_ref[which] = chosen.astype(out_ref.dtype)


def pick_pair(table, keys, values):
    blocks, part_tok, feat_width = keys.shape
    half = feat_width // CORES
    operands = [pltpu.with_memory_space_constraint(a, pltpu.HBM) for a in (table, keys, values)]
    return pl.pallas_call(
        pick_kernel,
        in_specs=[IN_HBM] * 3,
        out_specs=[WHOLE] * 5,
        out_shape=[pltpu.VMEM((2, blocks, part_tok, half), keys.dtype)] * 2
        + [pltpu.VMEM((2, part_tok, half), keys.dtype)] * 2
        + [pltpu.VMEM((8, 128), jnp.float32)],
        scratch_shapes=[pltpu.VMEM(table.shape, table.dtype), pltpu.SemaphoreType.DMA((5,))],
    )(*operands)


def join_kernel(att_ref, att_far, sent_ref, sent_far, kept_ref, att_out, gq_out, gk_out, gv_out, sems):
    core = lax.axis_index("kv") % CORES
    rows, half = att_ref.shape
    near = gk_out.shape[0]
    own, gk, gv = pl.ds(0, rows), pl.ds(rows, near), pl.ds(rows + near, near)
    copies = []
    for out_ref, sides in (
        (att_out, (att_ref, att_far)),
        (gq_out, (sent_ref.at[own], sent_far.at[own])),
        (gk_out, (kept_ref.at[pl.ds(0, near)], sent_far.at[gk])),
        (gv_out, (kept_ref.at[pl.ds(near, near)], sent_far.at[gv])),
    ):
        for side, ref in enumerate(sides):
            cols = pl.ds(pl.multiple_of((core ^ side) * half, half), half)
            copies.append(pltpu.make_async_copy(ref, out_ref.at[:, cols], sems.at[len(copies)]))
    for copy in copies:
        copy.start()
    for copy in copies:
        copy.wait()


def join(operands, shapes):
    return pl.pallas_call(
        join_kernel,
        in_specs=[WHOLE] * len(operands),
        out_specs=[IN_HBM] * len(shapes),
        out_shape=[pltpu.HBM(shape, jnp.bfloat16) for shape in shapes],
        scratch_shapes=[pltpu.SemaphoreType.DMA((2 * len(shapes),))],
        cost_estimate=SMALL,
    )(*operands)


def finish_kernel(block_ref, near_ref, near_far_ref, far_ref, *refs):
    arrived, outs, rows_ref, sems = refs[:-6], refs[-4:-2], refs[-2], refs[-1]
    core = lax.axis_index("kv") % CORES
    part_tok, half = far_ref.shape[1:]
    block = jnp.max(block_ref[...]).astype(jnp.int32)
    here = pl.ds(pl.multiple_of(block * part_tok, part_tok), part_tok)
    near = near_ref.shape[1]
    first = near_far_ref.shape[0] - 2 * near
    mine = pl.ds(pl.multiple_of(core * half, half), half)
    theirs = pl.ds(pl.multiple_of((core ^ 1) * half, half), half)
    copies = []
    for which, out_ref in enumerate(outs):
        total = near_ref[which, here]
        for ref in arrived:
            total += ref[0, which].astype(jnp.float32)
        rows_ref[which, :, mine] = total.astype(rows_ref.dtype)
        there = first + which * near + block * part_tok
        there = pl.ds(pl.multiple_of(there, part_tok), part_tok)
        total = near_far_ref[there, :].astype(jnp.float32) + far_ref[which].astype(jnp.float32)
        rows_ref[which, :, theirs] = total.astype(rows_ref.dtype)
        copies.append(pltpu.make_async_copy(rows_ref.at[which], out_ref.at[here], sems.at[which]))
        copies[-1].start()
    for copy in copies:
        copy.wait()


def finish(operands, outs):
    part_tok, half = operands[3].shape[1:]
    operands = [pltpu.with_memory_space_constraint(a, pltpu.VMEM) for a in operands]
    outs = [pltpu.with_memory_space_constraint(a, pltpu.HBM) for a in outs]
    return pl.pallas_call(
        finish_kernel,
        in_specs=[WHOLE] * len(operands) + [IN_HBM] * 2,
        out_specs=[IN_HBM] * 2,
        out_shape=[pltpu.HBM(a.shape, a.dtype) for a in outs],
        input_output_aliases={len(operands): 0, len(operands) + 1: 1},
        scratch_shapes=[
            pltpu.VMEM((2, part_tok, half * CORES), jnp.bfloat16),
            pltpu.SemaphoreType.DMA((2,)),
        ],
        cost_estimate=SMALL,
    )(*operands, *outs)


def near_tiles(rows, near):
    half = rows // 2
    return [(0, half, near // 2), (half, half, near)]


def fill_mask(members, near, blk_len, part_tok, bias_ref):
    member = lax.axis_index("kv")
    shift = part_tok.bit_length() - 1
    for start, count, used in near_tiles(bias_ref.shape[0], near):
        row = start + lax.broadcasted_iota(jnp.int32, (count, 1), 0)
        col = lax.broadcasted_iota(jnp.int32, (1, used), 1)
        key_tok = (col >> shift) * blk_len + (col & (part_tok - 1))
        for j in range(members):
            key_pos = key_tok + (member ^ j) * part_tok
            bias_ref[start : start + count, j * used : (j + 1) * used] = jnp.where(
                key_pos <= row, 0.0, HIDDEN
            )


def head_columns(head, head_dim):
    return pl.ds(pl.multiple_of(head * head_dim, head_dim), head_dim)


def near_rows(parts, which, used, cols):
    return jnp.concatenate([ref[which, :used, cols] for ref in parts], axis=0)


def near_forward_kernel(members, blk_len, part_tok, head_dim, q_hbm, g_hbm, *refs):
    parts, outs = refs[:members], refs[members:]
    out_ref, stat_ref, bias_ref, q_ref, g_ref, sems = outs
    rows, half = q_ref.shape
    near = parts[0].shape[1]
    slab = GROUP * head_dim
    core = lax.axis_index("kv") % CORES

    def fetch(group):
        there = pl.ds(pl.multiple_of(core * half + group * slab, slab), slab)
        here = pl.ds(pl.multiple_of(group * slab, slab), slab)
        return pltpu.make_async_copy(q_hbm.at[:, there], q_ref.at[:, here], sems.at[group])

    there = pl.ds(pl.multiple_of(core * half, half), half)
    last = pltpu.make_async_copy(g_hbm.at[:, there], g_ref, sems.at[half // slab])
    for group in range(half // slab):
        fetch(group).start()
    last.start()
    fill_mask(members, near, blk_len, part_tok, bias_ref)

    @pl.loop(0, half // slab)
    def _(group):
        fetch(group).wait()
        units = [
            (head_columns(group * GROUP + i, head_dim), pl.ds(start, count), used)
            for i in range(GROUP)
            for start, count, used in near_tiles(rows, near)
        ]
        raws = [
            dot(q_ref[here, cols], near_rows(parts, 0, used, cols), NT) * base2_scale(head_dim)
            + bias_ref[here, : members * used]
            for cols, here, used in units
        ]
        peaks = [jnp.max(raw, axis=1, keepdims=True) for raw in raws]
        weights = [jnp.exp2(raw - peak) for raw, peak in zip(raws, peaks)]
        totals = [jnp.sum(weight, axis=1, keepdims=True) for weight in weights]
        sums = [
            dot(weight.astype(jnp.bfloat16), near_rows(parts, 1, used, cols), NN)
            for weight, (cols, here, used) in zip(weights, units)
        ]
        for (cols, here, used), peak, total, summed in zip(units, peaks, totals, sums):
            level = peak + jnp.log2(total)
            stat_ref[here, cols] = jnp.broadcast_to(level, summed.shape)
            out_ref[here, cols] = summed * (1.0 / total)

    last.wait()


def far_rows(parts, which, cols):
    rows = []
    for pair_ref, column_ref in zip(parts[0::2], parts[1::2]):
        steps, cores, _, part_tok, _ = column_ref.shape
        rows.append(pair_ref[:, which, :, cols].reshape(cores * part_tok, cols.size))
        rows.append(column_ref[:, :, which, :, cols].reshape(steps * cores * part_tok, cols.size))
    return jnp.concatenate(rows, axis=0)


def far_kernel(groups, steps, head_dim, tile, heads, batch, q_ref, g_ref, sum_ref, stat_ref, *refs):
    parts = refs[: 2 * COLUMNS * groups]
    att_ref, gq_ref, level_ref, drift_ref, *grad_refs = refs[2 * COLUMNS * groups :]
    _, cores, _, part_tok, _ = grad_refs[0].shape
    rows, half = q_ref.shape
    span = steps * cores * part_tok
    width = COLUMNS * span
    score_scale = 1.0 / math.sqrt(head_dim)
    window = lax.axis_index("seq")
    level, side = window // COLUMNS, window % COLUMNS
    step = lax.broadcasted_iota(jnp.int32, (1, span), 1) >> ((cores * part_tok).bit_length() - 1)
    valid = [(step >= 1) & (step <= level), (step >= 1 - side) & (step <= level)]
    bias = jnp.concatenate([jnp.where(ok, 0.0, HIDDEN) for ok in valid] * groups, axis=1)
    total_width = groups * width

    def work(units, keys, values, key_grads, value_grads):
        raws = [
            dot(q_ref[here, cols], keys[i], NT) * base2_scale(head_dim) + bias
            for i, cols, here in units
        ]
        grad_probs = [dot(g_ref[here, cols], values[i], NT) for i, cols, here in units]
        near_levels = [stat_ref[here, cols] for i, cols, here in units]
        peaks = [
            jnp.maximum(near_level, jnp.max(raw, axis=1, keepdims=True))
            for near_level, raw in zip(near_levels, raws)
        ]
        near_weights = [jnp.exp2(near_level - peak) for near_level, peak in zip(near_levels, peaks)]
        weights = [jnp.exp2(raw - wide(peak, total_width)) for raw, peak in zip(raws, peaks)]
        totals = [
            near_weight + jnp.sum(weight, axis=1, keepdims=True)
            for near_weight, weight in zip(near_weights, weights)
        ]
        inverses = [1.0 / total for total in totals]
        sums = [
            dot(weight.astype(jnp.bfloat16), values[i], NN)
            for weight, (i, cols, here) in zip(weights, units)
        ]
        drifts = []
        for u, (i, cols, here) in enumerate(units):
            summed = sum_ref[here, cols] * near_weights[u] + sums[u]
            attended = (summed * inverses[u]).astype(jnp.bfloat16)
            att_ref[here, cols] = attended
            product = g_ref[here, cols].astype(jnp.float32) * attended.astype(jnp.float32)
            drift = jnp.broadcast_to(jnp.sum(product, axis=1, keepdims=True), product.shape)
            drifts.append(drift)
            level_ref[here, cols] = peaks[u] + jnp.log2(totals[u])
            drift_ref[here, cols] = drift
        moved = [
            weight * (grad_prob - wide(drift, total_width))
            for weight, grad_prob, drift in zip(weights, grad_probs, drifts)
        ]
        factors = [inverse * score_scale for inverse in inverses]
        own_scores = [
            (part[:, :width] * wide(factor, width)).astype(jnp.bfloat16)
            for part, factor in zip(moved, factors)
        ]
        own_probs = [
            (weight[:, :width] * wide(inverse, width)).astype(jnp.bfloat16)
            for weight, inverse in zip(weights, inverses)
        ]
        for u, (i, cols, here) in enumerate(units):
            gq_ref[here, cols] = dot(moved[u].astype(jnp.bfloat16), keys[i], NN) * factors[u]
        for u, (i, cols, here) in enumerate(units):
            key_grads[i].append(dot(own_scores[u], q_ref[here, cols], TN))
            value_grads[i].append(dot(own_probs[u], g_ref[here, cols], TN))

    @pl.loop(0, half // (heads * head_dim))
    def _(group):
        columns = [head_columns(group * heads + i, head_dim) for i in range(heads)]
        units = [
            (i, cols, pl.ds(r, tile)) for i, cols in enumerate(columns) for r in range(0, rows, tile)
        ]
        keys = [far_rows(parts, 0, cols) for cols in columns]
        values = [far_rows(parts, 1, cols) for cols in columns]
        grads = [[[] for _ in columns] for _ in range(2)]
        for first in range(0, len(units), batch):
            work(units[first : first + batch], keys, values, *grads)
        for which, per_head in enumerate(grads):
            for cols, terms in zip(columns, per_head):
                total = functools.reduce(lambda a, b: a + b, terms).astype(jnp.bfloat16)
                start = 0
                for ref in grad_refs:
                    shape = ref.shape[:2] + (part_tok, head_dim)
                    count = math.prod(shape[:3])
                    ref[:, :, which, :, cols] = total[start : start + count].reshape(shape)
                    start += count


def near_backward_kernel(members, head_dim, bias_ref, q_ref, g_ref, level_ref, drift_ref, far_gq_ref, *refs):
    parts, outs = refs[:members], refs[members:]
    own_ref, kept_ref, sent_ref = outs
    rows, half = q_ref.shape
    near = parts[0].shape[1]
    score_scale = 1.0 / math.sqrt(head_dim)

    @pl.loop(0, half // (GROUP * head_dim))
    def _(group):
        units = [
            (head_columns(group * GROUP + i, head_dim), pl.ds(start, count), used)
            for i in range(GROUP)
            for start, count, used in near_tiles(rows, near)
        ]
        keys = [near_rows(parts, 0, used, cols) for cols, here, used in units]
        values = [near_rows(parts, 1, used, cols) for cols, here, used in units]
        raws = [
            dot(q_ref[here, cols], key, NT) * base2_scale(head_dim)
            + bias_ref[here, : members * used]
            for (cols, here, used), key in zip(units, keys)
        ]
        grad_probs = [
            dot(g_ref[here, cols], value, NT) for (cols, here, used), value in zip(units, values)
        ]
        probs = [
            jnp.exp2(raw - wide(level_ref[here, cols], raw.shape[1]))
            for raw, (cols, here, used) in zip(raws, units)
        ]
        moved = [
            prob * (grad_prob - wide(drift_ref[here, cols], prob.shape[1]))
            for prob, grad_prob, (cols, here, used) in zip(probs, grad_probs, units)
        ]
        for (cols, here, used), part, key in zip(units, moved, keys):
            sent_ref[here, cols] = (
                dot(part.astype(jnp.bfloat16), key, NN) * score_scale + far_gq_ref[here, cols]
            ).astype(jnp.bfloat16)
        grads = []
        for (cols, here, used), part, prob in zip(units, moved, probs):
            own_score = (part[:, : CORES * used] * score_scale).astype(jnp.bfloat16)
            own_prob = prob[:, : CORES * used].astype(jnp.bfloat16)
            grads.append((dot(own_score, q_ref[here, cols], TN), dot(own_prob, g_ref[here, cols], TN)))
        low = near // 2
        for (cols, _, _), early, late in zip(units[0::2], grads[0::2], grads[1::2]):
            for which in range(2):
                for core in range(CORES):
                    top = late[which][core * near : core * near + low]
                    top += early[which][core * low : (core + 1) * low]
                    bottom = late[which][core * near + low : (core + 1) * near]
                    if core == 0:
                        own_ref[which, :low, cols] = top
                        own_ref[which, low:, cols] = bottom
                    ref, first = ((kept_ref, 0), (sent_ref, rows))[core]
                    first += which * near
                    ref[first : first + low, cols] = top.astype(ref.dtype)
                    ref[first + low : first + near, cols] = bottom.astype(ref.dtype)


def call(kernel, operands, outs, pairs, products, head_dim, in_specs=None, scratch=()):
    moved_bytes = sum(a.size * a.dtype.itemsize for a in operands)
    return pl.pallas_call(
        kernel,
        in_specs=in_specs or [WHOLE] * len(operands),
        out_specs=[WHOLE] * len(outs),
        out_shape=outs,
        scratch_shapes=scratch,
        compiler_params=LIMIT,
        cost_estimate=pl.CostEstimate(
            flops=4 * products * pairs * head_dim, bytes_accessed=moved_bytes, transcendentals=pairs
        ),
    )(*operands)


def shards(queries, keys, values, layout, grad_out):
    seq_count = lax.axis_size("seq")
    members = lax.axis_size("kv")
    tok_rows, feat_width = queries.shape
    blocks, part_tok = (keys.shape[0], keys.shape[1])
    blk_len = part_tok * members
    near = blocks * part_tok
    head_dim = feat_width // HEADS
    half = feat_width // CORES
    levels = seq_count // COLUMNS
    groups = members // CORES

    def hop(part, column_step, member_step):
        pairs = [
            (s * members + m, (s ^ column_step) * members + (m ^ member_step))
            for s in range(seq_count)
            for m in range(members)
        ]
        return lax.ppermute(part, ("seq", "kv"), pairs)

    def climb(part, d):
        return lax.ppermute(
            part, "seq", [(s, s + COLUMNS * d) for s in range(seq_count - COLUMNS * d)]
        )

    def sink(part, d):
        return lax.ppermute(
            part, "seq", [(s, s - COLUMNS * d) for s in range(COLUMNS * d, seq_count)]
        )

    mine, theirs, pair_mine, pair_theirs, block = pick_pair(layout.T, keys, values)
    own_pair = jnp.stack([pair_mine, hop(pair_theirs, 0, 1)])
    climbed = [climb(own_pair, d) for d in range(1, levels)]
    column = jnp.stack(climbed)
    chip_parts = [mine, hop(theirs, 0, 1)]
    near_parts = list(chip_parts)
    for group in range(1, groups):
        near_parts += [hop(part, 0, CORES * group) for part in chip_parts]
    sent_pair, _ = lax.optimization_barrier((own_pair, chip_parts[1]))
    cross_pairs = [hop(sent_pair, 1, CORES * group) for group in range(groups)]
    column, near_parts = lax.optimization_barrier((column, near_parts))
    near_parts = [part.reshape(2, near, half) for part in near_parts]
    crossing = [
        [column if (c, group) == (0, 0) else hop(column, c, CORES * group) for c in range(COLUMNS)]
        for group in range(groups)
    ]

    def rows_out(dtype):
        return pltpu.VMEM((tok_rows, half), dtype)

    def far_out(count):
        return pltpu.VMEM((count,) + own_pair.shape, jnp.bfloat16)

    low = (levels + 1) // 2
    near_pairs = HEADS // CORES * tok_rows * members * near
    far_width = members * seq_count * part_tok
    far_pairs = HEADS // CORES * tok_rows * far_width
    roomy = far_width <= 512
    far_plan = (tok_rows // 2, GROUP, 2 * GROUP) if roomy else (tok_rows // 8, 1, 1)

    near_sum, near_stat, bias, queries, grad_out = call(
        functools.partial(near_forward_kernel, members, blk_len, part_tok, head_dim),
        [pltpu.with_memory_space_constraint(a, pltpu.HBM) for a in (queries, grad_out)] + near_parts,
        [rows_out(jnp.float32)] * 2
        + [pltpu.VMEM((tok_rows, members * near), jnp.float32)]
        + [rows_out(jnp.bfloat16)] * 2,
        near_pairs,
        2,
        head_dim,
        [IN_HBM, IN_HBM] + [WHOLE] * members,
        [pltpu.SemaphoreType.DMA((half // (GROUP * head_dim) + 1,))],
    )
    far_parts = []
    for group, cross_pair in zip(crossing, cross_pairs):
        (same, other), _ = lax.optimization_barrier((group, near_stat))
        far_parts += [own_pair, same, cross_pair, other]
    attended, far_gq, level, drift, own_low, own_high, cross_low, cross_high = call(
        functools.partial(far_kernel, groups, levels, head_dim, *far_plan),
        [queries, grad_out, near_sum, near_stat] + far_parts,
        [rows_out(jnp.bfloat16)]
        + [rows_out(jnp.float32)] * 3
        + [far_out(low), far_out(levels - low)] * COLUMNS,
        far_pairs,
        5,
        head_dim,
    )

    def add(own, cross):
        return (own.astype(jnp.float32) + cross.astype(jnp.float32)).astype(jnp.bfloat16)

    high = hop(cross_high, 1, 0)
    near_own, near_kept, sent = call(
        functools.partial(near_backward_kernel, members, head_dim),
        [bias, queries, grad_out, level, drift, far_gq] + near_parts,
        [
            pltpu.VMEM((2, near, half), jnp.float32),
            pltpu.VMEM((2 * near, half), jnp.bfloat16),
            pltpu.VMEM((tok_rows + 2 * near, half), jnp.bfloat16),
        ],
        near_pairs,
        4,
        head_dim,
    )
    high, _ = lax.optimization_barrier((high, sent))
    sums = [add(own_high[d - low], high[d - low]) for d in range(low, levels)]
    cross_low, sent_mine, _ = lax.optimization_barrier((cross_low, sent, sums))
    crossed = hop(cross_low, 1, 0)
    sent_far = hop(sent_mine, 0, 1)
    att_far = hop(attended, 0, 1)
    sums = [add(own_low[d], crossed[d]) for d in range(1, low)] + sums
    returned = [sink(part, d) for d, part in enumerate(sums, 1)] + [crossed[0]]
    attended, grad_q, grad_k, grad_v = join(
        [attended, att_far, sent, sent_far, near_kept],
        [(tok_rows, feat_width)] * 2 + [(near, feat_width)] * 2,
    )
    returned, grad_k, grad_v = lax.optimization_barrier((returned, grad_k, grad_v))
    far_sent = sum(part[1].astype(jnp.float32) for part in returned).astype(jnp.bfloat16)
    grad_k, grad_v = finish(
        [block, near_own, sent_far, hop(far_sent, 0, 1)] + returned, [grad_k, grad_v]
    )
    return (attended, grad_q, grad_k.reshape(keys.shape), grad_v.reshape(values.shape))


def solution(mesh):
    return jax.shard_map(
        shards,
        mesh=mesh,
        in_specs=(P("seq", None), P("seq", "kv", None), P("seq", "kv", None), P(), P("seq", None)),
        out_specs=(P("seq", None), P("seq", None), P("seq", "kv", None), P("seq", "kv", None)),
        check_vma=False,
    )
```

profile of v0, /device:TPU:0, one launch (start us, length us, event | category | flops | bytes accessed | tf_op | source)
XLA Modules:
  0.0 58.0 jit_solution(8658073379290581279)
XLA Ops:
  0.6 1.2 %shard_map.84 = (bf16[2,8,16,512]{3,2,1,0:T(8,128)(2,1)S(1)}, bf16[2,8,16,512]{3,2,1,0:T(8,128)(2,1)S(1)}, bf16[2,16,512]{2,1,0:T(8,128)(2,1)S(1)}, bf16[2,16,512]{2,1,0:T(8,128)(2,1)S(1)}, f32[8,128]{1,0:T(8,128)S(1)}) custom-call(s32[15,64]{1,0:T(8,128)} %bitcast.37, bf16[8,16,1024]{2,1,0:T(8,128)(2,1)} %keys_hbm.1, bf16[8,16,1024]{2,1,0:T(8,128)(2,1)} %values_hbm.1), custom_call_target="tpu_custom_call" | custom-call | tf_op jit(solution)/shard_map/pallas_call | solution.py:74
  1.9 0.5 collective-permute-start.4
  2.5 2.9 %collective-permute-start.5 = (bf16[2,8,16,512]{3,2,1,0:T(8,128)(2,1)S(1)}, bf16[2,8,16,512]{3,2,1,0:T(8,128)(2,1)S(1)}, u32[]{:S(2)}, u32[]{:S(2)}) collective-permute-start(bf16[2,8,16,512]{3,2,1,0:T(8,128)(2,1)S(1)} %get-tuple-element.54), channel_id=1, source_target_pairs={{0,2},{1,3},{2,0},{3,1},{4,6},{5,7},{6,4},{7,5},{8,10},{9,11},{10,... | collective-permute-start | bytes 786440 | tf_op jit(solution)/shard_map/ppermute | solution.py:423
  5.4 1.0 %collective-permute-start.6 = (bf16[2,8,16,512]{3,2,1,0:T(8,128)(2,1)S(1)}, bf16[2,8,16,512]{3,2,1,0:T(8,128)(2,1)S(1)}, u32[]{:S(2)}, u32[]{:S(2)}) collective-permute-start(bf16[2,8,16,512]{3,2,1,0:T(8,128)(2,1)S(1)} %collective-permute-done.4), channel_id=1, source_target_pairs={{0,2},{1,3},{2,0},{3,1},{4,6},{5,7},{6,4},{7,5},{8,10},{9,11},{10,... | collective-permute-start | bytes 786440 | tf_op jit(solution)/shard_map/ppermute | solution.py:423
  6.4 5.5 %collective-permute-start.3 = (bf16[2,2,16,512]{3,2,1,0:T(8,128)(2,1)S(1)}, bf16[2,2,16,512]{3,2,1,0:T(8,128)(2,1)S(1)}, u32[]{:S(2)}, u32[]{:S(2)}) collective-permute-start(bf16[2,2,16,512]{3,2,1,0:T(8,128)(2,1)S(1)} %pad_maximum_fusion.1.refs_0_.refs_4_), channel_id=1, source_target_pairs={{0,24},{4,28},{1,25},{5,29},{2,26},{6,30},{3,27},{7,31}} | collective-permute-start | bytes 196616 | tf_op jit(solution)/shard_map/ppermute | solution.py:426
  12.0 1.3 %collective-permute-start.2 = (bf16[2,2,16,512]{3,2,1,0:T(8,128)(2,1)S(1)}, bf16[2,2,16,512]{3,2,1,0:T(8,128)(2,1)S(1)}, u32[]{:S(2)}, u32[]{:S(2)}) collective-permute-start(bf16[2,2,16,512]{3,2,1,0:T(8,128)(2,1)S(1)} %pad_maximum_fusion.1.refs_0_.refs_4_), channel_id=1, source_target_pairs={{0,16},{4,20},{8,24},{12,28},{1,17},{5,21},{9,25},{13,29},{2,18},{... | collective-permute-start | bytes 196616 | tf_op jit(solution)/shard_map/ppermute | solution.py:426
  13.3 2.5 %collective-permute-start.1 = (bf16[2,2,16,512]{3,2,1,0:T(8,128)(2,1)S(1)}, bf16[2,2,16,512]{3,2,1,0:T(8,128)(2,1)S(1)}, u32[]{:S(2)}, u32[]{:S(2)}) collective-permute-start(bf16[2,2,16,512]{3,2,1,0:T(8,128)(2,1)S(1)} %pad_maximum_fusion.1.refs_0_.refs_4_), channel_id=1, source_target_pairs={{0,8},{4,12},{8,16},{12,20},{16,24},{20,28},{1,9},{5,13},{9,17},{1... | collective-permute-start | bytes 196616 | tf_op jit(solution)/shard_map/ppermute | solution.py:426
  15.8 1.9 %collective-permute-done.1 = bf16[2,2,16,512]{3,2,1,0:T(8,128)(2,1)S(1)} collective-permute-done((bf16[2,2,16,512]{3,2,1,0:T(8,128)(2,1)S(1)}, bf16[2,2,16,512]{3,2,1,0:T(8,128)(2,1)S(1)}, u32[]{:S(2)}, u32[]{:S(2)}) %collective-permute-start.1) | collective-permute-done | bytes 65568 | tf_op jit(solution)/shard_map/ppermute | solution.py:426
  17.7 2.6 %collective-permute-start.10 = (bf16[3,2,2,16,512]{4,3,2,1,0:T(8,128)(2,1)S(1)}, bf16[3,2,2,16,512]{4,3,2,1,0:T(8,128)(2,1)S(1)}, u32[]{:S(2)}, u32[]{:S(2)}) collective-permute-start(bf16[3,2,2,16,512]{4,3,2,1,0:T(8,128)(2,1)S(1)} %pad_maximum_fusion.refs_1_), channel_id=1, source_target_pairs={{0,6},{1,7},{2,4},{3,5},{4,2},{5,3},{6,0},{7,1},{8,14},{9,15},{10,... | collective-permute-start | bytes 589832 | tf_op jit(solution)/shard_map/ppermute | solution.py:423
  21.2 2.5 %collective-permute-start.11 = (bf16[2,2,16,512]{3,2,1,0:T(8,128)(2,1)S(1)}, bf16[2,2,16,512]{3,2,1,0:T(8,128)(2,1)S(1)}, u32[]{:S(2)}, u32[]{:S(2)}) collective-permute-start(bf16[2,2,16,512]{3,2,1,0:T(8,128)(2,1)S(1)} %pad_maximum_fusion.1.refs_0_.refs_4_), channel_id=1, source_target_pairs={{0,6},{1,7},{2,4},{3,5},{4,2},{5,3},{6,0},{7,1},{8,14},{9,15},{10,... | collective-permute-start | bytes 196616 | tf_op jit(solution)/shard_map/ppermute | solution.py:423
  23.7 0.5 collective-permute-start.8
  24.3 2.7 %shard_map.85 = (f32[512,512]{1,0:T(8,128)S(1)}, f32[512,512]{1,0:T(8,128)S(1)}, f32[512,512]{1,0:T(8,128)S(1)}, bf16[512,512]{1,0:T(8,128)(2,1)S(1)}, bf16[512,512]{1,0:T(8,128)(2,1)S(1)}) custom-call(bf16[512,1024]{1,0:T(8,128)(2,1)} %q_hbm.1, bf16[512,1024]{1,0:T(8,128)(2,1)} %g_hbm.1, bf16[2,128,512]{2,1,0:T(8,128)(2,1)S(1)} %bitcast.23, ...), custom_call_target="tpu_custom_call" | custom-call | flops 1073741824 | bytes 3145728 | tf_op jit(solution)/shard_map/pallas_call | solution.py:392
  27.0 2.7 %collective-permute-done.9.refs_5_ = bf16[3,2,2,16,512]{4,3,2,1,0:T(8,128)(2,1)S(1)} collective-permute-done((bf16[3,2,2,16,512]{4,3,2,1,0:T(8,128)(2,1)S(1)}, bf16[3,2,2,16,512]{4,3,2,1,0:T(8,128)(2,1)S(1)}, u32[]{:S(2)}, u32[]{:S(2)}) %collective-permute-start.9) | collective-permute-done | bytes 196640 | tf_op jit(solution)/shard_map/ppermute | solution.py:423
  29.7 0.7 %collective-permute-done.7.refs_3_ = bf16[3,2,2,16,512]{4,3,2,1,0:T(8,128)(2,1)S(1)} collective-permute-done((bf16[3,2,2,16,512]{4,3,2,1,0:T(8,128)(2,1)S(1)}, bf16[3,2,2,16,512]{4,3,2,1,0:T(8,128)(2,1)S(1)}, u32[]{:S(2)}, u32[]{:S(2)}) %collective-permute-start.7) | collective-permute-done | bytes 196640 | tf_op jit(solution)/shard_map/ppermute | solution.py:423
  30.5 0.7 %collective-permute-done.11.refs_6_ = bf16[2,2,16,512]{3,2,1,0:T(8,128)(2,1)S(1)} collective-permute-done((bf16[2,2,16,512]{3,2,1,0:T(8,128)(2,1)S(1)}, bf16[2,2,16,512]{3,2,1,0:T(8,128)(2,1)S(1)}, u32[]{:S(2)}, u32[]{:S(2)}) %collective-permute-start.11) | collective-permute-done | bytes 65568 | tf_op jit(solution)/shard_map/ppermute | solution.py:423
  31.2 0.7 %collective-permute-done.8.refs_2_ = bf16[2,2,16,512]{3,2,1,0:T(8,128)(2,1)S(1)} collective-permute-done((bf16[2,2,16,512]{3,2,1,0:T(8,128)(2,1)S(1)}, bf16[2,2,16,512]{3,2,1,0:T(8,128)(2,1)S(1)}, u32[]{:S(2)}, u32[]{:S(2)}) %collective-permute-start.8) | collective-permute-done | bytes 65568 | tf_op jit(solution)/shard_map/ppermute | solution.py:423
  31.9 4.5 %shard_map.86 = (bf16[512,512]{1,0:T(8,128)(2,1)S(1)}, f32[512,512]{1,0:T(8,128)S(1)}, f32[512,512]{1,0:T(8,128)S(1)}, f32[512,512]{1,0:T(8,128)S(1)}, bf16[2,2,...) custom-call(bf16[512,512]{1,0:T(8,128)(2,1)S(1)} %get-tuple-element., ...), custom_call_target="tpu_custom_call" | custom-call | flops 2684354560 | bytes 4194304 | tf_op jit(solution)/shard_map/pallas_call | solution.py:392
  36.4 1.6 %collective-permute-start.13 = (bf16[2,2,2,16,512]{4,3,2,1,0:T(8,128)(2,1)S(1)}, bf16[2,2,2,16,512]{4,3,2,1,0:T(8,128)(2,1)S(1)}, u32[]{:S(2)}, u32[]{:S(2)}) collective-permute-start(bf16[2,2,2,16,512]{4,3,2,1,0:T(8,128)(2,1)S(1)} %get-tuple-element.76), channel_id=1, source_target_pairs={{0,4},{1,5},{2,6},{3,7},{4,0},{5,1},{6,2},{7,3},{8,12},{9,13},{10,... | collective-permute-start | bytes 393224 | tf_op jit(solution)/shard_map/ppermute | solution.py:423
  38.0 2.4 %shard_map.87 = (f32[2,128,512]{2,1,0:T(8,128)S(1)}, bf16[256,512]{1,0:T(8,128)(2,1)S(1)}, bf16[768,512]{1,0:T(8,128)(2,1)S(1)}) custom-call(f32[512,512]{1,0:T(8,128)S(1)} %get-tuple-element.69.bias_ref, bf16[512,512]{1,0:T(8,128)(2,1)S(1)} %get-tuple-element.58.q_ref, bf16[512,512]{1,0:T(8,128)(2,1)S(1)} %get-tuple-element.59.g_ref, ...), custom_call_target="tpu_custom_call" | custom-call | flops 2147483648 | bytes 6291456 | tf_op jit(solution)/shard_map/pallas_call | solution.py:392
  40.4 1.0 %collective-permute-done.13 = bf16[2,2,2,16,512]{4,3,2,1,0:T(8,128)(2,1)S(1)} collective-permute-done((bf16[2,2,2,16,512]{4,3,2,1,0:T(8,128)(2,1)S(1)}, bf16[2,2,2,16,512]{4,3,2,1,0:T(8,128)(2,1)S(1)}, u32[]{:S(2)}, u32[]{:S(2)}) %collective-permute-start.13) | collective-permute-done | bytes 131104 | tf_op jit(solution)/shard_map/ppermute | solution.py:423
  41.6 1.6 %collective-permute-start.15 = (bf16[2,2,2,16,512]{4,3,2,1,0:T(8,128)(2,1)S(1)}, bf16[2,2,2,16,512]{4,3,2,1,0:T(8,128)(2,1)S(1)}, u32[]{:S(2)}, u32[]{:S(2)}) collective-permute-start(bf16[2,2,2,16,512]{4,3,2,1,0:T(8,128)(2,1)S(1)} %get-tuple-element.85), channel_id=1, source_target_pairs={{0,4},{1,5},{2,6},{3,7},{4,0},{5,1},{6,2},{7,3},{8,12},{9,13},{10,... | collective-permute-start | bytes 393224 | tf_op jit(solution)/shard_map/ppermute | solution.py:423
  43.3 1.3 %collective-permute-start.18 = (bf16[2,2,16,512]{3,2,1,0:T(8,128)(2,1)S(1)}, bf16[2,2,16,512]{3,2,1,0:T(8,128)(2,1)S(1)}, u32[]{:S(2)}, u32[]{:S(2)}) collective-permute-start(bf16[2,2,16,512]{3,2,1,0:T(8,128)(2,1)S(1)} %get-tuple-element.96), channel_id=1, source_target_pairs={{24,0},{28,4},{25,1},{29,5},{26,2},{30,6},{27,3},{31,7}} | collective-permute-start | bytes 196616 | tf_op jit(solution)/shard_map/ppermute | solution.py:431
  44.6 1.3 %collective-permute-start.17 = (bf16[2,2,16,512]{3,2,1,0:T(8,128)(2,1)S(1)}, bf16[2,2,16,512]{3,2,1,0:T(8,128)(2,1)S(1)}, u32[]{:S(2)}, u32[]{:S(2)}) collective-permute-start(bf16[2,2,16,512]{3,2,1,0:T(8,128)(2,1)S(1)} %get-tuple-element.97), channel_id=1, source_target_pairs={{16,0},{20,4},{24,8},{28,12},{17,1},{21,5},{25,9},{29,13},{18,2},{... | collective-permute-start | bytes 196616 | tf_op jit(solution)/shard_map/ppermute | solution.py:431
  45.9 1.6 %collective-permute-done.15 = bf16[2,2,2,16,512]{4,3,2,1,0:T(8,128)(2,1)S(1)} collective-permute-done((bf16[2,2,2,16,512]{4,3,2,1,0:T(8,128)(2,1)S(1)}, bf16[2,2,2,16,512]{4,3,2,1,0:T(8,128)(2,1)S(1)}, u32[]{:S(2)}, u32[]{:S(2)}) %collective-permute-start.15) | collective-permute-done | bytes 131104 | tf_op jit(solution)/shard_map/ppermute | solution.py:423
  47.5 1.3 %collective-permute-start.16 = (bf16[2,2,16,512]{3,2,1,0:T(8,128)(2,1)S(1)}, bf16[2,2,16,512]{3,2,1,0:T(8,128)(2,1)S(1)}, u32[]{:S(2)}, u32[]{:S(2)}) collective-permute-start(bf16[2,2,16,512]{3,2,1,0:T(8,128)(2,1)S(1)} %fusion.2), channel_id=1, source_target_pairs={{8,0},{12,4},{16,8},{20,12},{24,16},{28,20},{9,1},{13,5},{17,9},{2... | collective-permute-start | bytes 196616 | tf_op jit(solution)/shard_map/ppermute | solution.py:431
  48.9 0.8 %copy-done.5 = bf16[512,512]{1,0:T(8,128)(2,1)} copy-done((bf16[512,512]{1,0:T(8,128)(2,1)}, bf16[512,512]{1,0:T(8,128)(2,1)S(1)}, u32[]{:S(2)}) %copy-start.5) | copy-done | bytes 524312
  49.7 0.9 %copy-done = bf16[768,512]{1,0:T(8,128)(2,1)} copy-done((bf16[768,512]{1,0:T(8,128)(2,1)}, bf16[768,512]{1,0:T(8,128)(2,1)S(1)}, u32[]{:S(2)}) %copy-start) | copy-done | bytes 786456
  50.6 3.3 %shard_map.88 = (bf16[512,1024]{1,0:T(8,128)(2,1)}, bf16[512,1024]{1,0:T(8,128)(2,1)}, bf16[128,1024]{1,0:T(8,128)(2,1)}, bf16[128,1024]{1,0:T(8,128)(2,1)}) custom-call(bf16[512,512]{1,0:T(8,128)(2,1)} %copy-done.3, bf16[512,512]{1,0:T(8,128)(2,1)} %copy-done.5, bf16[768,512]{1,0:T(8,128)(2,1)} %copy-done.2, bf16[768,512]{1,0:T(8,128)(2,1)} %copy-done, ...), custom_call_target="tpu_custom_call" | custom-call | tf_op jit(solution)/shard_map/pallas_call | solution.py:107
  54.2 0.6 %collective-permute-done.16.refs_0_ = bf16[2,2,16,512]{3,2,1,0:T(8,128)(2,1)S(1)} collective-permute-done((bf16[2,2,16,512]{3,2,1,0:T(8,128)(2,1)S(1)}, bf16[2,2,16,512]{3,2,1,0:T(8,128)(2,1)S(1)}, u32[]{:S(2)}, u32[]{:S(2)}) %collective-permute-start.16) | collective-permute-done | bytes 65568 | tf_op jit(solution)/shard_map/ppermute | solution.py:431
  54.9 1.2 %collective-permute-done.19.far_ref = bf16[2,16,512]{2,1,0:T(8,128)(2,1)S(1)} collective-permute-done((bf16[2,16,512]{2,1,0:T(8,128)(2,1)S(1)}, bf16[2,16,512]{2,1,0:T(8,128)(2,1)S(1)}, u32[]{:S(2)}, u32[]{:S(2)}) %collective-permute-start.19) | collective-permute-done | bytes 32800 | tf_op jit(solution)/shard_map/ppermute | solution.py:423
  56.1 1.1 %copy-done.1 = bf16[768,512]{1,0:T(8,128)(2,1)S(1)} copy-done((bf16[768,512]{1,0:T(8,128)(2,1)S(1)}, bf16[768,512]{1,0:T(8,128)(2,1)}, u32[]{:S(2)}) %copy-start.1) | copy-done | bytes 786456
  57.3 0.8 %shard_map.89 = (bf16[128,1024]{1,0:T(8,128)(2,1)}, bf16[128,1024]{1,0:T(8,128)(2,1)}) custom-call(f32[8,128]{1,0:T(8,128)S(1)} %get-tuple-element.82.block_ref, f32[2,128,512]{2,1,0:T(8,128)S(1)} %get-tuple-element.83.near_ref, bf16[768,512]{1,0:T(8,128)(2,1)S(1)} %copy-done.1, ...), custom_call_target="tpu_custom_call", output_to_operand_aliasing={{0}: (8, {}), {1}: (9, {})} | custom-call | tf_op jit(solution)/shard_map/pallas_call | solution.py:147
  (32 shorter events, 1.9 us)
Async XLA Ops:
  1.9 3.5 %collective-permute-start.4 = (bf16[2,8,16,512]{3,2,1,0:T(8,128)(2,1)S(1)}, bf16[2,8,16,512]{3,2,1,0:T(8,128)(2,1)S(1)}, u32[]{:S(2)}, u32[]{:S(2)}) collective-permute-start(bf16[2,8,16,512]{3,2,1,0:T(8,128)(2,1)S(1)} %get-tuple-element.53), channel_id=1, source_target_pairs={{0,1},{1,0},{2,3},{3,2},{4,5},{5,4},{6,7},{7,6},{8,9},{9,8},{10,11... | collective-permute-start | bytes 786440 | tf_op jit(solution)/shard_map/ppermute | solution.py:423
  2.4 4.1 %collective-permute-start = (bf16[2,16,512]{2,1,0:T(8,128)(2,1)S(1)}, bf16[2,16,512]{2,1,0:T(8,128)(2,1)S(1)}, u32[]{:S(2)}, u32[]{:S(2)}) collective-permute-start(bf16[2,16,512]{2,1,0:T(8,128)(2,1)S(1)} %get-tuple-element.51), channel_id=1, source_target_pairs={{0,1},{1,0},{2,3},{3,2},{4,5},{5,4},{6,7},{7,6},{8,9},{9,8},{10,11... | collective-permute-start | bytes 98312 | tf_op jit(solution)/shard_map/ppermute | solution.py:423
  2.5 15.2 %collective-permute-start.5 = (bf16[2,8,16,512]{3,2,1,0:T(8,128)(2,1)S(1)}, bf16[2,8,16,512]{3,2,1,0:T(8,128)(2,1)S(1)}, u32[]{:S(2)}, u32[]{:S(2)}) collective-permute-start(bf16[2,8,16,512]{3,2,1,0:T(8,128)(2,1)S(1)} %get-tuple-element.54), channel_id=1, source_target_pairs={{0,2},{1,3},{2,0},{3,1},{4,6},{5,7},{6,4},{7,5},{8,10},{9,11},{10,... | collective-permute-start | bytes 786440 | tf_op jit(solution)/shard_map/ppermute | solution.py:423
  5.4 12.3 %collective-permute-start.6 = (bf16[2,8,16,512]{3,2,1,0:T(8,128)(2,1)S(1)}, bf16[2,8,16,512]{3,2,1,0:T(8,128)(2,1)S(1)}, u32[]{:S(2)}, u32[]{:S(2)}) collective-permute-start(bf16[2,8,16,512]{3,2,1,0:T(8,128)(2,1)S(1)} %collective-permute-done.4), channel_id=1, source_target_pairs={{0,2},{1,3},{2,0},{3,1},{4,6},{5,7},{6,4},{7,5},{8,10},{9,11},{10,... | collective-permute-start | bytes 786440 | tf_op jit(solution)/shard_map/ppermute | solution.py:423
  6.4 9.3 %collective-permute-start.3 = (bf16[2,2,16,512]{3,2,1,0:T(8,128)(2,1)S(1)}, bf16[2,2,16,512]{3,2,1,0:T(8,128)(2,1)S(1)}, u32[]{:S(2)}, u32[]{:S(2)}) collective-permute-start(bf16[2,2,16,512]{3,2,1,0:T(8,128)(2,1)S(1)} %pad_maximum_fusion.1.refs_0_.refs_4_), channel_id=1, source_target_pairs={{0,24},{4,28},{1,25},{5,29},{2,26},{6,30},{3,27},{7,31}} | collective-permute-start | bytes 196616 | tf_op jit(solution)/shard_map/ppermute | solution.py:426
  12.0 3.8 %collective-permute-start.2 = (bf16[2,2,16,512]{3,2,1,0:T(8,128)(2,1)S(1)}, bf16[2,2,16,512]{3,2,1,0:T(8,128)(2,1)S(1)}, u32[]{:S(2)}, u32[]{:S(2)}) collective-permute-start(bf16[2,2,16,512]{3,2,1,0:T(8,128)(2,1)S(1)} %pad_maximum_fusion.1.refs_0_.refs_4_), channel_id=1, source_target_pairs={{0,16},{4,20},{8,24},{12,28},{1,17},{5,21},{9,25},{13,29},{2,18},{... | collective-permute-start | bytes 196616 | tf_op jit(solution)/shard_map/ppermute | solution.py:426
  13.3 4.4 %collective-permute-start.1 = (bf16[2,2,16,512]{3,2,1,0:T(8,128)(2,1)S(1)}, bf16[2,2,16,512]{3,2,1,0:T(8,128)(2,1)S(1)}, u32[]{:S(2)}, u32[]{:S(2)}) collective-permute-start(bf16[2,2,16,512]{3,2,1,0:T(8,128)(2,1)S(1)} %pad_maximum_fusion.1.refs_0_.refs_4_), channel_id=1, source_target_pairs={{0,8},{4,12},{8,16},{12,20},{16,24},{20,28},{1,9},{5,13},{9,17},{1... | collective-permute-start | bytes 196616 | tf_op jit(solution)/shard_map/ppermute | solution.py:426
  17.7 9.3 %collective-permute-start.10 = (bf16[3,2,2,16,512]{4,3,2,1,0:T(8,128)(2,1)S(1)}, bf16[3,2,2,16,512]{4,3,2,1,0:T(8,128)(2,1)S(1)}, u32[]{:S(2)}, u32[]{:S(2)}) collective-permute-start(bf16[3,2,2,16,512]{4,3,2,1,0:T(8,128)(2,1)S(1)} %pad_maximum_fusion.refs_1_), channel_id=1, source_target_pairs={{0,6},{1,7},{2,4},{3,5},{4,2},{5,3},{6,0},{7,1},{8,14},{9,15},{10,... | collective-permute-start | bytes 589832 | tf_op jit(solution)/shard_map/ppermute | solution.py:423
  20.2 9.5 %collective-permute-start.9 = (bf16[3,2,2,16,512]{4,3,2,1,0:T(8,128)(2,1)S(1)}, bf16[3,2,2,16,512]{4,3,2,1,0:T(8,128)(2,1)S(1)}, u32[]{:S(2)}, u32[]{:S(2)}) collective-permute-start(bf16[3,2,2,16,512]{4,3,2,1,0:T(8,128)(2,1)S(1)} %pad_maximum_fusion.refs_1_), channel_id=1, source_target_pairs={{0,2},{1,3},{2,0},{3,1},{4,6},{5,7},{6,4},{7,5},{8,10},{9,11},{10,... | collective-permute-start | bytes 589832 | tf_op jit(solution)/shard_map/ppermute | solution.py:423
  20.7 9.7 %collective-permute-start.7 = (bf16[3,2,2,16,512]{4,3,2,1,0:T(8,128)(2,1)S(1)}, bf16[3,2,2,16,512]{4,3,2,1,0:T(8,128)(2,1)S(1)}, u32[]{:S(2)}, u32[]{:S(2)}) collective-permute-start(bf16[3,2,2,16,512]{4,3,2,1,0:T(8,128)(2,1)S(1)} %pad_maximum_fusion.refs_1_), channel_id=1, source_target_pairs={{0,4},{1,5},{2,6},{3,7},{4,0},{5,1},{6,2},{7,3},{8,12},{9,13},{10,... | collective-permute-start | bytes 589832 | tf_op jit(solution)/shard_map/ppermute | solution.py:423
  21.2 9.9 %collective-permute-start.11 = (bf16[2,2,16,512]{3,2,1,0:T(8,128)(2,1)S(1)}, bf16[2,2,16,512]{3,2,1,0:T(8,128)(2,1)S(1)}, u32[]{:S(2)}, u32[]{:S(2)}) collective-permute-start(bf16[2,2,16,512]{3,2,1,0:T(8,128)(2,1)S(1)} %pad_maximum_fusion.1.refs_0_.refs_4_), channel_id=1, source_target_pairs={{0,6},{1,7},{2,4},{3,5},{4,2},{5,3},{6,0},{7,1},{8,14},{9,15},{10,... | collective-permute-start | bytes 196616 | tf_op jit(solution)/shard_map/ppermute | solution.py:423
  23.7 8.1 %collective-permute-start.8 = (bf16[2,2,16,512]{3,2,1,0:T(8,128)(2,1)S(1)}, bf16[2,2,16,512]{3,2,1,0:T(8,128)(2,1)S(1)}, u32[]{:S(2)}, u32[]{:S(2)}) collective-permute-start(bf16[2,2,16,512]{3,2,1,0:T(8,128)(2,1)S(1)} %pad_maximum_fusion.1.refs_0_.refs_4_), channel_id=1, source_target_pairs={{0,4},{1,5},{2,6},{3,7},{4,0},{5,1},{6,2},{7,3},{8,12},{9,13},{10,... | collective-permute-start | bytes 196616 | tf_op jit(solution)/shard_map/ppermute | solution.py:423
  36.4 6.7 %copy-start.3 = (bf16[512,512]{1,0:T(8,128)(2,1)}, bf16[512,512]{1,0:T(8,128)(2,1)S(1)}, u32[]{:S(2)}) copy-start(bf16[512,512]{1,0:T(8,128)(2,1)S(1)} %get-tuple-element.68.att_ref) | copy-start | bytes 1572868
  36.4 5.0 %collective-permute-start.13 = (bf16[2,2,2,16,512]{4,3,2,1,0:T(8,128)(2,1)S(1)}, bf16[2,2,2,16,512]{4,3,2,1,0:T(8,128)(2,1)S(1)}, u32[]{:S(2)}, u32[]{:S(2)}) collective-permute-start(bf16[2,2,2,16,512]{4,3,2,1,0:T(8,128)(2,1)S(1)} %get-tuple-element.76), channel_id=1, source_target_pairs={{0,4},{1,5},{2,6},{3,7},{4,0},{5,1},{6,2},{7,3},{8,12},{9,13},{10,... | collective-permute-start | bytes 393224 | tf_op jit(solution)/shard_map/ppermute | solution.py:423
  40.4 7.1 %copy-start.4 = (bf16[256,512]{1,0:T(8,128)(2,1)}, bf16[256,512]{1,0:T(8,128)(2,1)S(1)}, u32[]{:S(2)}) copy-start(bf16[256,512]{1,0:T(8,128)(2,1)S(1)} %get-tuple-element.79.kept_ref) | copy-start | bytes 786436
  40.4 9.2 %copy-start.2 = (bf16[768,512]{1,0:T(8,128)(2,1)}, bf16[768,512]{1,0:T(8,128)(2,1)S(1)}, u32[]{:S(2)}) copy-start(bf16[768,512]{1,0:T(8,128)(2,1)S(1)} %get-tuple-element.78.sent_ref) | copy-start | bytes 2359300
  41.5 7.4 %collective-permute-start.14 = (bf16[768,512]{1,0:T(8,128)(2,1)S(1)}, bf16[768,512]{1,0:T(8,128)(2,1)S(1)}, u32[]{:S(2)}, u32[]{:S(2)}) collective-permute-start(bf16[768,512]{1,0:T(8,128)(2,1)S(1)} %get-tuple-element.78.sent_ref), channel_id=1, source_target_pairs={{0,1},{1,0},{2,3},{3,2},{4,5},{5,4},{6,7},{7,6},{8,9},{9,8},{10,11... | collective-permute-start | bytes 2359304 | tf_op jit(solution)/shard_map/ppermute | solution.py:423
  41.6 5.9 %collective-permute-start.15 = (bf16[2,2,2,16,512]{4,3,2,1,0:T(8,128)(2,1)S(1)}, bf16[2,2,2,16,512]{4,3,2,1,0:T(8,128)(2,1)S(1)}, u32[]{:S(2)}, u32[]{:S(2)}) collective-permute-start(bf16[2,2,2,16,512]{4,3,2,1,0:T(8,128)(2,1)S(1)} %get-tuple-element.85), channel_id=1, source_target_pairs={{0,4},{1,5},{2,6},{3,7},{4,0},{5,1},{6,2},{7,3},{8,12},{9,13},{10,... | collective-permute-start | bytes 393224 | tf_op jit(solution)/shard_map/ppermute | solution.py:423
  43.1 5.7 %collective-permute-start.12 = (bf16[512,512]{1,0:T(8,128)(2,1)S(1)}, bf16[512,512]{1,0:T(8,128)(2,1)S(1)}, u32[]{:S(2)}, u32[]{:S(2)}) collective-permute-start(bf16[512,512]{1,0:T(8,128)(2,1)S(1)} %get-tuple-element.68.att_ref), channel_id=1, source_target_pairs={{0,1},{1,0},{2,3},{3,2},{4,5},{5,4},{6,7},{7,6},{8,9},{9,8},{10,11... | collective-permute-start | bytes 1572872 | tf_op jit(solution)/shard_map/ppermute | solution.py:423
  43.3 10.6 %collective-permute-start.18 = (bf16[2,2,16,512]{3,2,1,0:T(8,128)(2,1)S(1)}, bf16[2,2,16,512]{3,2,1,0:T(8,128)(2,1)S(1)}, u32[]{:S(2)}, u32[]{:S(2)}) collective-permute-start(bf16[2,2,16,512]{3,2,1,0:T(8,128)(2,1)S(1)} %get-tuple-element.96), channel_id=1, source_target_pairs={{24,0},{28,4},{25,1},{29,5},{26,2},{30,6},{27,3},{31,7}} | collective-permute-start | bytes 196616 | tf_op jit(solution)/shard_map/ppermute | solution.py:431
  44.6 9.6 %collective-permute-start.17 = (bf16[2,2,16,512]{3,2,1,0:T(8,128)(2,1)S(1)}, bf16[2,2,16,512]{3,2,1,0:T(8,128)(2,1)S(1)}, u32[]{:S(2)}, u32[]{:S(2)}) collective-permute-start(bf16[2,2,16,512]{3,2,1,0:T(8,128)(2,1)S(1)} %get-tuple-element.97), channel_id=1, source_target_pairs={{16,0},{20,4},{24,8},{28,12},{17,1},{21,5},{25,9},{29,13},{18,2},{... | collective-permute-start | bytes 196616 | tf_op jit(solution)/shard_map/ppermute | solution.py:431
  47.5 7.3 %collective-permute-start.16 = (bf16[2,2,16,512]{3,2,1,0:T(8,128)(2,1)S(1)}, bf16[2,2,16,512]{3,2,1,0:T(8,128)(2,1)S(1)}, u32[]{:S(2)}, u32[]{:S(2)}) collective-permute-start(bf16[2,2,16,512]{3,2,1,0:T(8,128)(2,1)S(1)} %fusion.2), channel_id=1, source_target_pairs={{8,0},{12,4},{16,8},{20,12},{24,16},{28,20},{9,1},{13,5},{17,9},{2... | collective-permute-start | bytes 196616 | tf_op jit(solution)/shard_map/ppermute | solution.py:431
  48.8 0.8 %copy-start.5 = (bf16[512,512]{1,0:T(8,128)(2,1)}, bf16[512,512]{1,0:T(8,128)(2,1)S(1)}, u32[]{:S(2)}) copy-start(bf16[512,512]{1,0:T(8,128)(2,1)S(1)} %collective-permute-done.12.att_far) | copy-start | bytes 1572868
  49.6 0.9 %copy-start = (bf16[768,512]{1,0:T(8,128)(2,1)}, bf16[768,512]{1,0:T(8,128)(2,1)S(1)}, u32[]{:S(2)}) copy-start(bf16[768,512]{1,0:T(8,128)(2,1)S(1)} %collective-permute-done.14.sent_far.near_far_ref) | copy-start | bytes 2359300
  54.9 1.3 %collective-permute-start.19 = (bf16[2,16,512]{2,1,0:T(8,128)(2,1)S(1)}, bf16[2,16,512]{2,1,0:T(8,128)(2,1)S(1)}, u32[]{:S(2)}, u32[]{:S(2)}) collective-permute-start(bf16[2,16,512]{2,1,0:T(8,128)(2,1)S(1)} %fusion.3), channel_id=1, source_target_pairs={{0,1},{1,0},{2,3},{3,2},{4,5},{5,4},{6,7},{7,6},{8,9},{9,8},{10,11... | collective-permute-start | bytes 98312 | tf_op jit(solution)/shard_map/ppermute | solution.py:423
  56.1 1.1 %copy-start.1 = (bf16[768,512]{1,0:T(8,128)(2,1)S(1)}, bf16[768,512]{1,0:T(8,128)(2,1)}, u32[]{:S(2)}) copy-start(bf16[768,512]{1,0:T(8,128)(2,1)} %copy-done) | copy-start | bytes 2359300
where the time goes:
time: 58.4 us; the launch traced here: 58 us
  starting transfers between devices  27.7 us (47%)
  Pallas kernels  15 us (26%)
  waiting for transfers between devices  11.5 us (20%)
  local copies, waits for them, and re-layouts  2.87 us (5%)
  between operations  0.88 us (2%)
    ppermute x14, starting transfers between devices, hop(): return lax.ppermute(part, ('seq', 'kv'), pairs)  14.6 us
    pallas_call x3, Pallas kernels, call(): pl.pallas_call(kernel, in_specs=in_specs or [WHOLE] * len(operands), out_...  9.7 us
    ppermute x3, starting transfers between devices, climb(): lax.ppermute(part, 'seq', [(s, s + COLUMNS * d) for s in range(seq_count...  9.27 us
    ppermute x14, waiting for transfers between devices, hop(): return lax.ppermute(part, ('seq', 'kv'), pairs)  8.67 us
    ppermute x3, starting transfers between devices, sink(): lax.ppermute(part, 'seq', [(s, s - COLUMNS * d) for s in range(COLUMNS *...  3.86 us
    pallas_call x1, Pallas kernels, join(): pl.pallas_call(join_kernel, in_specs=[WHOLE] * len(operands), out_specs=[...  3.28 us
    unnamed x12, local copies, waits for them, and re-layouts  2.87 us
    ppermute x3, waiting for transfers between devices, climb(): lax.ppermute(part, 'seq', [(s, s + COLUMNS * d) for s in range(seq_count...  1.87 us
  transfers between devices with their start and end apart: 20, of which 10 were waited for; matrix products, arithmetic and copies ran while one was open for 0% of the time, Pallas kernels for 15%

commit v1 on v0

--- a/solution.py
+++ b/solution.py
@@ -104,6 +104,7 @@
 
 
 def join(operands, shapes):
+    operands = [pltpu.with_memory_space_constraint(a, pltpu.VMEM) for a in operands]
     return pl.pallas_call(
         join_kernel,
         in_specs=[WHOLE] * len(operands),
@@ -114,26 +115,21 @@
     )(*operands)
 
 
-def finish_kernel(block_ref, near_ref, near_far_ref, far_ref, *refs):
+def finish_kernel(block_ref, chosen_ref, far_ref, *refs):
     arrived, outs, rows_ref, sems = refs[:-6], refs[-4:-2], refs[-2], refs[-1]
     core = lax.axis_index("kv") % CORES
     part_tok, half = far_ref.shape[1:]
     block = jnp.max(block_ref[...]).astype(jnp.int32)
     here = pl.ds(pl.multiple_of(block * part_tok, part_tok), part_tok)
-    near = near_ref.shape[1]
-    first = near_far_ref.shape[0] - 2 * near
     mine = pl.ds(pl.multiple_of(core * half, half), half)
     theirs = pl.ds(pl.multiple_of((core ^ 1) * half, half), half)
     copies = []
     for which, out_ref in enumerate(outs):
-        total = near_ref[which, here]
+        total = chosen_ref[0, which]
         for ref in arrived:
             total += ref[0, which].astype(jnp.float32)
         rows_ref[which, :, mine] = total.astype(rows_ref.dtype)
-        there = first + which * near + block * part_tok
-        there = pl.ds(pl.multiple_of(there, part_tok), part_tok)
-        total = near_far_ref[there, :].astype(jnp.float32) + far_ref[which].astype(jnp.float32)
-        rows_ref[which, :, theirs] = total.astype(rows_ref.dtype)
+        rows_ref[which, :, theirs] = far_ref[which]
         copies.append(pltpu.make_async_copy(rows_ref.at[which], out_ref.at[here], sems.at[which]))
         copies[-1].start()
     for copy in copies:
@@ -141,7 +137,7 @@
 
 
 def finish(operands, outs):
-    part_tok, half = operands[3].shape[1:]
+    part_tok, half = operands[2].shape[1:]
     operands = [pltpu.with_memory_space_constraint(a, pltpu.VMEM) for a in operands]
     outs = [pltpu.with_memory_space_constraint(a, pltpu.HBM) for a in outs]
     return pl.pallas_call(
@@ -330,9 +326,9 @@
                     start += count
 
 
-def near_backward_kernel(members, head_dim, bias_ref, q_ref, g_ref, level_ref, drift_ref, far_gq_ref, *refs):
+def near_backward_kernel(members, head_dim, blocks, block_ref, bias_ref, q_ref, g_ref, level_ref, drift_ref, far_gq_ref, *refs):
     parts, outs = refs[:members], refs[members:]
-    own_ref, kept_ref, sent_ref = outs
+    chosen_ref, kept_ref, sent_ref, grad_ref = outs
     rows, half = q_ref.shape
     near = parts[0].shape[1]
     score_scale = 1.0 / math.sqrt(head_dim)
@@ -378,13 +374,22 @@
                     top = late[which][core * near : core * near + low]
                     top += early[which][core * low : (core + 1) * low]
                     bottom = late[which][core * near + low : (core + 1) * near]
-                    if core == 0:
-                        own_ref[which, :low, cols] = top
-                        own_ref[which, low:, cols] = bottom
+                    grad_ref[core, which, :low, cols] = top
+                    grad_ref[core, which, low:, cols] = bottom
                     ref, first = ((kept_ref, 0), (sent_ref, rows))[core]
                     first += which * near
                     ref[first : first + low, cols] = top.astype(ref.dtype)
                     ref[first + low : first + near, cols] = bottom.astype(ref.dtype)
+
+    part_tok = near // blocks
+    block = jnp.max(jnp.max(block_ref[...], axis=1, keepdims=True), axis=0, keepdims=True)
+    for core in range(CORES):
+        for which in range(2):
+            chosen = grad_ref[core, which, :part_tok]
+            for b in range(1, blocks):
+                rows_b = grad_ref[core, which, b * part_tok : (b + 1) * part_tok]
+                chosen = jnp.where(block == b, rows_b, chosen)
+            chosen_ref[core, which] = chosen
 
 
 def call(kernel, operands, outs, pairs, products, head_dim, in_specs=None, scratch=()):
@@ -493,17 +498,18 @@
         return (own.astype(jnp.float32) + cross.astype(jnp.float32)).astype(jnp.bfloat16)
 
     high = hop(cross_high, 1, 0)
-    near_own, near_kept, sent = call(
-        functools.partial(near_backward_kernel, members, head_dim),
-        [bias, queries, grad_out, level, drift, far_gq] + near_parts,
+    chosen, near_kept, sent = call(
+        functools.partial(near_backward_kernel, members, head_dim, blocks),
+        [block, bias, queries, grad_out, level, drift, far_gq] + near_parts,
         [
-            pltpu.VMEM((2, near, half), jnp.float32),
+            pltpu.VMEM((CORES, 2, part_tok, half), jnp.float32),
             pltpu.VMEM((2 * near, half), jnp.bfloat16),
             pltpu.VMEM((tok_rows + 2 * near, half), jnp.bfloat16),
         ],
         near_pairs,
         4,
         head_dim,
+        scratch=[pltpu.VMEM((CORES, 2, near, half), jnp.float32)],
     )
     high, _ = lax.optimization_barrier((high, sent))
     sums = [add(own_high[d - low], high[d - low]) for d in range(low, levels)]
@@ -518,9 +524,10 @@
         [(tok_rows, feat_width)] * 2 + [(near, feat_width)] * 2,
     )
     returned, grad_k, grad_v = lax.optimization_barrier((returned, grad_k, grad_v))
-    far_sent = sum(part[1].astype(jnp.float32) for part in returned).astype(jnp.bfloat16)
+    far_sent = chosen[1] + sum(part[1].astype(jnp.float32) for part in returned)
+    far_sent = far_sent.astype(jnp.bfloat16)
     grad_k, grad_v = finish(
-        [block, near_own, sent_far, hop(far_sent, 0, 1)] + returned, [grad_k, grad_v]
+        [block, chosen, hop(far_sent, 0, 1)] + returned, [grad_k, grad_v]
     )
     return (attended, grad_q, grad_k.reshape(keys.shape), grad_v.reshape(values.shape))
 

time: 58.4 us -> 58.1 us (level)
  Pallas kernels: 15 us -> 13.3 us
  local copies, waits for them, and re-layouts: 2.87 us -> 4.02 us
    pallas_call x1, Pallas kernels: 3.28 us -> 1.54 us  [join(): pl.pallas_call(join_kernel, in_specs=[WHOLE] * len(operands), out_specs=[...]
    unnamed x12 -> x8, local copies, waits for them, and re-layouts: 2.87 us -> 4.01 us
  transfers between devices with their start and end apart: 20 -> 20, of which waited for: 10 -> 10; matrix products, arithmetic and copies ran while one was open for 0% -> 0% of each run, Pallas kernels for 15% -> 12%
where the time goes in v1:
time: 58.1 us; the launch traced here: 57.7 us
  starting transfers between devices  27.7 us (48%)
  Pallas kernels  13.3 us (23%)
  waiting for transfers between devices  11.7 us (20%)
  local copies, waits for them, and re-layouts  4.02 us (7%)
  between operations  0.85 us (1%)
    ppermute x14, starting transfers between devices, hop(): return lax.ppermute(part, ('seq', 'kv'), pairs)  14.6 us
    pallas_call x3, Pallas kernels, call(): pl.pallas_call(kernel, in_specs=in_specs or [WHOLE] * len(operands), out_...  9.81 us
    ppermute x3, starting transfers between devices, climb(): lax.ppermute(part, 'seq', [(s, s + COLUMNS * d) for s in range(seq_count...  9.27 us
    ppermute x14, waiting for transfers between devices, hop(): return lax.ppermute(part, ('seq', 'kv'), pairs)  8.57 us
    unnamed x8, local copies, waits for them, and re-layouts  4.01 us
    ppermute x3, starting transfers between devices, sink(): lax.ppermute(part, 'seq', [(s, s - COLUMNS * d) for s in range(COLUMNS *...  3.86 us
    ppermute x3, waiting for transfers between devices, climb(): lax.ppermute(part, 'seq', [(s, s + COLUMNS * d) for s in range(seq_count...  1.87 us
    pallas_call x1, Pallas kernels, join(): pl.pallas_call(join_kernel, in_specs=[WHOLE] * len(operands), out_specs=[...  1.54 us
  transfers between devices with their start and end apart: 20, of which 10 were waited for; matrix products, arithmetic and copies ran while one was open for 0% of the time, Pallas kernels for 12%

profile of v1, /device:TPU:0, one launch (start us, length us, event | category | flops | bytes accessed | tf_op | source)
XLA Modules:
  0.0 57.7 jit_solution(17053618912156833282)
XLA Ops:
  0.6 1.2 %shard_map.84 = (bf16[2,8,16,512]{3,2,1,0:T(8,128)(2,1)S(1)}, bf16[2,8,16,512]{3,2,1,0:T(8,128)(2,1)S(1)}, bf16[2,16,512]{2,1,0:T(8,128)(2,1)S(1)}, bf16[2,16,512]{2,1,0:T(8,128)(2,1)S(1)}, f32[8,128]{1,0:T(8,128)S(1)}) custom-call(s32[15,64]{1,0:T(8,128)} %bitcast.37, bf16[8,16,1024]{2,1,0:T(8,128)(2,1)} %keys_hbm.1, bf16[8,16,1024]{2,1,0:T(8,128)(2,1)} %values_hbm.1), custom_call_target="tpu_custom_call" | custom-call | tf_op jit(solution)/shard_map/pallas_call | solution.py:74
  2.5 2.9 %collective-permute-start.5 = (bf16[2,8,16,512]{3,2,1,0:T(8,128)(2,1)S(1)}, bf16[2,8,16,512]{3,2,1,0:T(8,128)(2,1)S(1)}, u32[]{:S(2)}, u32[]{:S(2)}) collective-permute-start(bf16[2,8,16,512]{3,2,1,0:T(8,128)(2,1)S(1)} %get-tuple-element.54), channel_id=1, source_target_pairs={{0,2},{1,3},{2,0},{3,1},{4,6},{5,7},{6,4},{7,5},{8,10},{9,11},{10,... | collective-permute-start | bytes 786440 | tf_op jit(solution)/shard_map/ppermute | solution.py:428
  5.4 1.0 %collective-permute-start.6 = (bf16[2,8,16,512]{3,2,1,0:T(8,128)(2,1)S(1)}, bf16[2,8,16,512]{3,2,1,0:T(8,128)(2,1)S(1)}, u32[]{:S(2)}, u32[]{:S(2)}) collective-permute-start(bf16[2,8,16,512]{3,2,1,0:T(8,128)(2,1)S(1)} %collective-permute-done.4), channel_id=1, source_target_pairs={{0,2},{1,3},{2,0},{3,1},{4,6},{5,7},{6,4},{7,5},{8,10},{9,11},{10,... | collective-permute-start | bytes 786440 | tf_op jit(solution)/shard_map/ppermute | solution.py:428
  6.4 5.5 %collective-permute-start.3 = (bf16[2,2,16,512]{3,2,1,0:T(8,128)(2,1)S(1)}, bf16[2,2,16,512]{3,2,1,0:T(8,128)(2,1)S(1)}, u32[]{:S(2)}, u32[]{:S(2)}) collective-permute-start(bf16[2,2,16,512]{3,2,1,0:T(8,128)(2,1)S(1)} %pad_maximum_fusion.1.refs_0_.refs_4_), channel_id=1, source_target_pairs={{0,24},{4,28},{1,25},{5,29},{2,26},{6,30},{3,27},{7,31}} | collective-permute-start | bytes 196616 | tf_op jit(solution)/shard_map/ppermute | solution.py:431
  12.0 1.3 %collective-permute-start.2 = (bf16[2,2,16,512]{3,2,1,0:T(8,128)(2,1)S(1)}, bf16[2,2,16,512]{3,2,1,0:T(8,128)(2,1)S(1)}, u32[]{:S(2)}, u32[]{:S(2)}) collective-permute-start(bf16[2,2,16,512]{3,2,1,0:T(8,128)(2,1)S(1)} %pad_maximum_fusion.1.refs_0_.refs_4_), channel_id=1, source_target_pairs={{0,16},{4,20},{8,24},{12,28},{1,17},{5,21},{9,25},{13,29},{2,18},{... | collective-permute-start | bytes 196616 | tf_op jit(solution)/shard_map/ppermute | solution.py:431
  13.3 2.5 %collective-permute-start.1 = (bf16[2,2,16,512]{3,2,1,0:T(8,128)(2,1)S(1)}, bf16[2,2,16,512]{3,2,1,0:T(8,128)(2,1)S(1)}, u32[]{:S(2)}, u32[]{:S(2)}) collective-permute-start(bf16[2,2,16,512]{3,2,1,0:T(8,128)(2,1)S(1)} %pad_maximum_fusion.1.refs_0_.refs_4_), channel_id=1, source_target_pairs={{0,8},{4,12},{8,16},{12,20},{16,24},{20,28},{1,9},{5,13},{9,17},{1... | collective-permute-start | bytes 196616 | tf_op jit(solution)/shard_map/ppermute | solution.py:431
  15.8 1.9 %collective-permute-done.1 = bf16[2,2,16,512]{3,2,1,0:T(8,128)(2,1)S(1)} collective-permute-done((bf16[2,2,16,512]{3,2,1,0:T(8,128)(2,1)S(1)}, bf16[2,2,16,512]{3,2,1,0:T(8,128)(2,1)S(1)}, u32[]{:S(2)}, u32[]{:S(2)}) %collective-permute-start.1) | collective-permute-done | bytes 65568 | tf_op jit(solution)/shard_map/ppermute | solution.py:431
  17.7 2.6 %collective-permute-start.10 = (bf16[3,2,2,16,512]{4,3,2,1,0:T(8,128)(2,1)S(1)}, bf16[3,2,2,16,512]{4,3,2,1,0:T(8,128)(2,1)S(1)}, u32[]{:S(2)}, u32[]{:S(2)}) collective-permute-start(bf16[3,2,2,16,512]{4,3,2,1,0:T(8,128)(2,1)S(1)} %pad_maximum_fusion.refs_1_), channel_id=1, source_target_pairs={{0,6},{1,7},{2,4},{3,5},{4,2},{5,3},{6,0},{7,1},{8,14},{9,15},{10,... | collective-permute-start | bytes 589832 | tf_op jit(solution)/shard_map/ppermute | solution.py:428
  21.2 2.5 %collective-permute-start.11 = (bf16[2,2,16,512]{3,2,1,0:T(8,128)(2,1)S(1)}, bf16[2,2,16,512]{3,2,1,0:T(8,128)(2,1)S(1)}, u32[]{:S(2)}, u32[]{:S(2)}) collective-permute-start(bf16[2,2,16,512]{3,2,1,0:T(8,128)(2,1)S(1)} %pad_maximum_fusion.1.refs_0_.refs_4_), channel_id=1, source_target_pairs={{0,6},{1,7},{2,4},{3,5},{4,2},{5,3},{6,0},{7,1},{8,14},{9,15},{10,... | collective-permute-start | bytes 196616 | tf_op jit(solution)/shard_map/ppermute | solution.py:428
  24.3 2.7 %shard_map.85 = (f32[512,512]{1,0:T(8,128)S(1)}, f32[512,512]{1,0:T(8,128)S(1)}, f32[512,512]{1,0:T(8,128)S(1)}, bf16[512,512]{1,0:T(8,128)(2,1)S(1)}, bf16[512,512]{1,0:T(8,128)(2,1)S(1)}) custom-call(bf16[512,1024]{1,0:T(8,128)(2,1)} %q_hbm.1, bf16[512,1024]{1,0:T(8,128)(2,1)} %g_hbm.1, bf16[2,128,512]{2,1,0:T(8,128)(2,1)S(1)} %bitcast.23, ...), custom_call_target="tpu_custom_call" | custom-call | flops 1073741824 | bytes 3145728 | tf_op jit(solution)/shard_map/pallas_call | solution.py:397
  27.0 2.7 %collective-permute-done.9.refs_5_ = bf16[3,2,2,16,512]{4,3,2,1,0:T(8,128)(2,1)S(1)} collective-permute-done((bf16[3,2,2,16,512]{4,3,2,1,0:T(8,128)(2,1)S(1)}, bf16[3,2,2,16,512]{4,3,2,1,0:T(8,128)(2,1)S(1)}, u32[]{:S(2)}, u32[]{:S(2)}) %collective-permute-start.9) | collective-permute-done | bytes 196640 | tf_op jit(solution)/shard_map/ppermute | solution.py:428
  29.7 0.7 %collective-permute-done.7.refs_3_ = bf16[3,2,2,16,512]{4,3,2,1,0:T(8,128)(2,1)S(1)} collective-permute-done((bf16[3,2,2,16,512]{4,3,2,1,0:T(8,128)(2,1)S(1)}, bf16[3,2,2,16,512]{4,3,2,1,0:T(8,128)(2,1)S(1)}, u32[]{:S(2)}, u32[]{:S(2)}) %collective-permute-start.7) | collective-permute-done | bytes 196640 | tf_op jit(solution)/shard_map/ppermute | solution.py:428
  30.5 0.7 %collective-permute-done.11.refs_6_ = bf16[2,2,16,512]{3,2,1,0:T(8,128)(2,1)S(1)} collective-permute-done((bf16[2,2,16,512]{3,2,1,0:T(8,128)(2,1)S(1)}, bf16[2,2,16,512]{3,2,1,0:T(8,128)(2,1)S(1)}, u32[]{:S(2)}, u32[]{:S(2)}) %collective-permute-start.11) | collective-permute-done | bytes 65568 | tf_op jit(solution)/shard_map/ppermute | solution.py:428
  31.2 0.7 %collective-permute-done.8.refs_2_ = bf16[2,2,16,512]{3,2,1,0:T(8,128)(2,1)S(1)} collective-permute-done((bf16[2,2,16,512]{3,2,1,0:T(8,128)(2,1)S(1)}, bf16[2,2,16,512]{3,2,1,0:T(8,128)(2,1)S(1)}, u32[]{:S(2)}, u32[]{:S(2)}) %collective-permute-start.8) | collective-permute-done | bytes 65568 | tf_op jit(solution)/shard_map/ppermute | solution.py:428
  31.9 4.5 %shard_map.86 = (bf16[512,512]{1,0:T(8,128)(2,1)S(1)}, f32[512,512]{1,0:T(8,128)S(1)}, f32[512,512]{1,0:T(8,128)S(1)}, f32[512,512]{1,0:T(8,128)S(1)}, bf16[2,2,...) custom-call(bf16[512,512]{1,0:T(8,128)(2,1)S(1)} %get-tuple-element., ...), custom_call_target="tpu_custom_call" | custom-call | flops 2684354560 | bytes 4194304 | tf_op jit(solution)/shard_map/pallas_call | solution.py:397
  36.4 1.6 %collective-permute-start.13 = (bf16[2,2,2,16,512]{4,3,2,1,0:T(8,128)(2,1)S(1)}, bf16[2,2,2,16,512]{4,3,2,1,0:T(8,128)(2,1)S(1)}, u32[]{:S(2)}, u32[]{:S(2)}) collective-permute-start(bf16[2,2,2,16,512]{4,3,2,1,0:T(8,128)(2,1)S(1)} %get-tuple-element.77), channel_id=1, source_target_pairs={{0,4},{1,5},{2,6},{3,7},{4,0},{5,1},{6,2},{7,3},{8,12},{9,13},{10,... | collective-permute-start | bytes 393224 | tf_op jit(solution)/shard_map/ppermute | solution.py:428
  38.0 2.5 %shard_map.87 = (f32[2,2,16,512]{3,2,1,0:T(8,128)S(1)}, bf16[256,512]{1,0:T(8,128)(2,1)S(1)}, bf16[768,512]{1,0:T(8,128)(2,1)S(1)}) custom-call(f32[8,128]{1,0:T(8,128)S(1)} %get-tuple-element.69.block_ref, f32[512,512]{1,0:T(8,128)S(1)} %get-tuple-element.70.bias_ref, bf16[512,512]{1,0:T(8,128)(2,1)S(1)} %get-tuple-element.58.q_ref, ...), custom_call_target="tpu_custom_call" | custom-call | flops 2147483648 | bytes 6295552 | tf_op jit(solution)/shard_map/pallas_call | solution.py:397
  40.5 0.9 %collective-permute-done.13 = bf16[2,2,2,16,512]{4,3,2,1,0:T(8,128)(2,1)S(1)} collective-permute-done((bf16[2,2,2,16,512]{4,3,2,1,0:T(8,128)(2,1)S(1)}, bf16[2,2,2,16,512]{4,3,2,1,0:T(8,128)(2,1)S(1)}, u32[]{:S(2)}, u32[]{:S(2)}) %collective-permute-start.13) | collective-permute-done | bytes 131104 | tf_op jit(solution)/shard_map/ppermute | solution.py:428
  41.6 0.9 %copy-done = bf16[768,512]{1,0:T(8,128)(2,1)} copy-done((bf16[768,512]{1,0:T(8,128)(2,1)}, bf16[768,512]{1,0:T(8,128)(2,1)S(1)}, u32[]{:S(2)}) %copy-start) | copy-done | bytes 786456
  42.4 1.5 %collective-permute-start.15 = (bf16[2,2,2,16,512]{4,3,2,1,0:T(8,128)(2,1)S(1)}, bf16[2,2,2,16,512]{4,3,2,1,0:T(8,128)(2,1)S(1)}, u32[]{:S(2)}, u32[]{:S(2)}) collective-permute-start(bf16[2,2,2,16,512]{4,3,2,1,0:T(8,128)(2,1)S(1)} %get-tuple-element.85), channel_id=1, source_target_pairs={{0,4},{1,5},{2,6},{3,7},{4,0},{5,1},{6,2},{7,3},{8,12},{9,13},{10,... | collective-permute-start | bytes 393224 | tf_op jit(solution)/shard_map/ppermute | solution.py:428
  44.2 1.3 %collective-permute-start.18 = (bf16[2,2,16,512]{3,2,1,0:T(8,128)(2,1)S(1)}, bf16[2,2,16,512]{3,2,1,0:T(8,128)(2,1)S(1)}, u32[]{:S(2)}, u32[]{:S(2)}) collective-permute-start(bf16[2,2,16,512]{3,2,1,0:T(8,128)(2,1)S(1)} %get-tuple-element.96), channel_id=1, source_target_pairs={{24,0},{28,4},{25,1},{29,5},{26,2},{30,6},{27,3},{31,7}} | collective-permute-start | bytes 196616 | tf_op jit(solution)/shard_map/ppermute | solution.py:436
  45.4 1.3 %collective-permute-start.17 = (bf16[2,2,16,512]{3,2,1,0:T(8,128)(2,1)S(1)}, bf16[2,2,16,512]{3,2,1,0:T(8,128)(2,1)S(1)}, u32[]{:S(2)}, u32[]{:S(2)}) collective-permute-start(bf16[2,2,16,512]{3,2,1,0:T(8,128)(2,1)S(1)} %get-tuple-element.97), channel_id=1, source_target_pairs={{16,0},{20,4},{24,8},{28,12},{17,1},{21,5},{25,9},{29,13},{18,2},{... | collective-permute-start | bytes 196616 | tf_op jit(solution)/shard_map/ppermute | solution.py:436
  46.7 1.6 %collective-permute-done.15 = bf16[2,2,2,16,512]{4,3,2,1,0:T(8,128)(2,1)S(1)} collective-permute-done((bf16[2,2,2,16,512]{4,3,2,1,0:T(8,128)(2,1)S(1)}, bf16[2,2,2,16,512]{4,3,2,1,0:T(8,128)(2,1)S(1)}, u32[]{:S(2)}, u32[]{:S(2)}) %collective-permute-start.15) | collective-permute-done | bytes 131104 | tf_op jit(solution)/shard_map/ppermute | solution.py:428
  48.4 1.3 %collective-permute-start.16 = (bf16[2,2,16,512]{3,2,1,0:T(8,128)(2,1)S(1)}, bf16[2,2,16,512]{3,2,1,0:T(8,128)(2,1)S(1)}, u32[]{:S(2)}, u32[]{:S(2)}) collective-permute-start(bf16[2,2,16,512]{3,2,1,0:T(8,128)(2,1)S(1)} %fusion.2), channel_id=1, source_target_pairs={{8,0},{12,4},{16,8},{20,12},{24,16},{28,20},{9,1},{13,5},{17,9},{2... | collective-permute-start | bytes 196616 | tf_op jit(solution)/shard_map/ppermute | solution.py:436
  49.7 0.9 %copy-done.2 = bf16[768,512]{1,0:T(8,128)(2,1)} copy-done((bf16[768,512]{1,0:T(8,128)(2,1)}, bf16[768,512]{1,0:T(8,128)(2,1)S(1)}, u32[]{:S(2)}) %copy-start.2) | copy-done | bytes 786456
  50.6 1.1 %copy-done.1 = bf16[768,512]{1,0:T(8,128)(2,1)S(1)} copy-done((bf16[768,512]{1,0:T(8,128)(2,1)S(1)}, bf16[768,512]{1,0:T(8,128)(2,1)}, u32[]{:S(2)}) %copy-start.1) | copy-done | bytes 786456
  51.7 1.1 %copy-done.3 = bf16[768,512]{1,0:T(8,128)(2,1)S(1)} copy-done((bf16[768,512]{1,0:T(8,128)(2,1)S(1)}, bf16[768,512]{1,0:T(8,128)(2,1)}, u32[]{:S(2)}) %copy-start.3) | copy-done | bytes 786456
  52.8 1.5 %shard_map.88 = (bf16[512,1024]{1,0:T(8,128)(2,1)}, bf16[512,1024]{1,0:T(8,128)(2,1)}, bf16[128,1024]{1,0:T(8,128)(2,1)}, bf16[128,1024]{1,0:T(8,128)(2,1)}) custom-call(bf16[512,512]{1,0:T(8,128)(2,1)S(1)} %get-tuple-element.68.att_ref, bf16[512,512]{1,0:T(8,128)(2,1)S(1)} %collective-permute-done.12.att_far, bf16[768,512]{1,0:T(8,128)(2,1)S(1)} %copy-done.1, ...), custom_call_target="tpu_custom_call" | custom-call | tf_op jit(solution)/shard_map/pallas_call | solution.py:108
  54.4 0.6 %collective-permute-done.17.refs_1_ = bf16[2,2,16,512]{3,2,1,0:T(8,128)(2,1)S(1)} collective-permute-done((bf16[2,2,16,512]{3,2,1,0:T(8,128)(2,1)S(1)}, bf16[2,2,16,512]{3,2,1,0:T(8,128)(2,1)S(1)}, u32[]{:S(2)}, u32[]{:S(2)}) %collective-permute-start.17) | collective-permute-done | bytes 65568 | tf_op jit(solution)/shard_map/ppermute | solution.py:436
  55.0 0.6 %collective-permute-done.16.refs_0_ = bf16[2,2,16,512]{3,2,1,0:T(8,128)(2,1)S(1)} collective-permute-done((bf16[2,2,16,512]{3,2,1,0:T(8,128)(2,1)S(1)}, bf16[2,2,16,512]{3,2,1,0:T(8,128)(2,1)S(1)}, u32[]{:S(2)}, u32[]{:S(2)}) %collective-permute-start.16) | collective-permute-done | bytes 65568 | tf_op jit(solution)/shard_map/ppermute | solution.py:436
  55.7 1.2 %collective-permute-done.19.far_ref = bf16[2,16,512]{2,1,0:T(8,128)(2,1)S(1)} collective-permute-done((bf16[2,16,512]{2,1,0:T(8,128)(2,1)S(1)}, bf16[2,16,512]{2,1,0:T(8,128)(2,1)S(1)}, u32[]{:S(2)}, u32[]{:S(2)}) %collective-permute-start.19) | collective-permute-done | bytes 32800 | tf_op jit(solution)/shard_map/ppermute | solution.py:428
  56.9 0.8 %shard_map.89 = (bf16[128,1024]{1,0:T(8,128)(2,1)}, bf16[128,1024]{1,0:T(8,128)(2,1)}) custom-call(f32[8,128]{1,0:T(8,128)S(1)} %get-tuple-element.69.block_ref, f32[2,2,16,512]{3,2,1,0:T(8,128)S(1)} %get-tuple-element.83.chosen_ref, bf16[2,16,512]{2,1,0:T(8,128)(2,1)S(1)} %collective-permute-done.19.far_ref, ...), custom_call_target="tpu_custom_call", output_to_operand_aliasing={{0}: (7, {}), {1}: (8, {})} | custom-call | tf_op jit(solution)/shard_map/pallas_call | solution.py:143
  (28 shorter events, 2.6 us)
Async XLA Ops:
  1.9 3.5 %collective-permute-start.4 = (bf16[2,8,16,512]{3,2,1,0:T(8,128)(2,1)S(1)}, bf16[2,8,16,512]{3,2,1,0:T(8,128)(2,1)S(1)}, u32[]{:S(2)}, u32[]{:S(2)}) collective-permute-start(bf16[2,8,16,512]{3,2,1,0:T(8,128)(2,1)S(1)} %get-tuple-element.53), channel_id=1, source_target_pairs={{0,1},{1,0},{2,3},{3,2},{4,5},{5,4},{6,7},{7,6},{8,9},{9,8},{10,11... | collective-permute-start | bytes 786440 | tf_op jit(solution)/shard_map/ppermute | solution.py:428
  2.4 4.1 %collective-permute-start = (bf16[2,16,512]{2,1,0:T(8,128)(2,1)S(1)}, bf16[2,16,512]{2,1,0:T(8,128)(2,1)S(1)}, u32[]{:S(2)}, u32[]{:S(2)}) collective-permute-start(bf16[2,16,512]{2,1,0:T(8,128)(2,1)S(1)} %get-tuple-element.51), channel_id=1, source_target_pairs={{0,1},{1,0},{2,3},{3,2},{4,5},{5,4},{6,7},{7,6},{8,9},{9,8},{10,11... | collective-permute-start | bytes 98312 | tf_op jit(solution)/shard_map/ppermute | solution.py:428
  2.5 15.2 %collective-permute-start.5 = (bf16[2,8,16,512]{3,2,1,0:T(8,128)(2,1)S(1)}, bf16[2,8,16,512]{3,2,1,0:T(8,128)(2,1)S(1)}, u32[]{:S(2)}, u32[]{:S(2)}) collective-permute-start(bf16[2,8,16,512]{3,2,1,0:T(8,128)(2,1)S(1)} %get-tuple-element.54), channel_id=1, source_target_pairs={{0,2},{1,3},{2,0},{3,1},{4,6},{5,7},{6,4},{7,5},{8,10},{9,11},{10,... | collective-permute-start | bytes 786440 | tf_op jit(solution)/shard_map/ppermute | solution.py:428
  5.4 12.3 %collective-permute-start.6 = (bf16[2,8,16,512]{3,2,1,0:T(8,128)(2,1)S(1)}, bf16[2,8,16,512]{3,2,1,0:T(8,128)(2,1)S(1)}, u32[]{:S(2)}, u32[]{:S(2)}) collective-permute-start(bf16[2,8,16,512]{3,2,1,0:T(8,128)(2,1)S(1)} %collective-permute-done.4), channel_id=1, source_target_pairs={{0,2},{1,3},{2,0},{3,1},{4,6},{5,7},{6,4},{7,5},{8,10},{9,11},{10,... | collective-permute-start | bytes 786440 | tf_op jit(solution)/shard_map/ppermute | solution.py:428
  6.4 9.3 %collective-permute-start.3 = (bf16[2,2,16,512]{3,2,1,0:T(8,128)(2,1)S(1)}, bf16[2,2,16,512]{3,2,1,0:T(8,128)(2,1)S(1)}, u32[]{:S(2)}, u32[]{:S(2)}) collective-permute-start(bf16[2,2,16,512]{3,2,1,0:T(8,128)(2,1)S(1)} %pad_maximum_fusion.1.refs_0_.refs_4_), channel_id=1, source_target_pairs={{0,24},{4,28},{1,25},{5,29},{2,26},{6,30},{3,27},{7,31}} | collective-permute-start | bytes 196616 | tf_op jit(solution)/shard_map/ppermute | solution.py:431
  12.0 3.8 %collective-permute-start.2 = (bf16[2,2,16,512]{3,2,1,0:T(8,128)(2,1)S(1)}, bf16[2,2,16,512]{3,2,1,0:T(8,128)(2,1)S(1)}, u32[]{:S(2)}, u32[]{:S(2)}) collective-permute-start(bf16[2,2,16,512]{3,2,1,0:T(8,128)(2,1)S(1)} %pad_maximum_fusion.1.refs_0_.refs_4_), channel_id=1, source_target_pairs={{0,16},{4,20},{8,24},{12,28},{1,17},{5,21},{9,25},{13,29},{2,18},{... | collective-permute-start | bytes 196616 | tf_op jit(solution)/shard_map/ppermute | solution.py:431
  13.3 4.4 %collective-permute-start.1 = (bf16[2,2,16,512]{3,2,1,0:T(8,128)(2,1)S(1)}, bf16[2,2,16,512]{3,2,1,0:T(8,128)(2,1)S(1)}, u32[]{:S(2)}, u32[]{:S(2)}) collective-permute-start(bf16[2,2,16,512]{3,2,1,0:T(8,128)(2,1)S(1)} %pad_maximum_fusion.1.refs_0_.refs_4_), channel_id=1, source_target_pairs={{0,8},{4,12},{8,16},{12,20},{16,24},{20,28},{1,9},{5,13},{9,17},{1... | collective-permute-start | bytes 196616 | tf_op jit(solution)/shard_map/ppermute | solution.py:431
  17.7 9.3 %collective-permute-start.10 = (bf16[3,2,2,16,512]{4,3,2,1,0:T(8,128)(2,1)S(1)}, bf16[3,2,2,16,512]{4,3,2,1,0:T(8,128)(2,1)S(1)}, u32[]{:S(2)}, u32[]{:S(2)}) collective-permute-start(bf16[3,2,2,16,512]{4,3,2,1,0:T(8,128)(2,1)S(1)} %pad_maximum_fusion.refs_1_), channel_id=1, source_target_pairs={{0,6},{1,7},{2,4},{3,5},{4,2},{5,3},{6,0},{7,1},{8,14},{9,15},{10,... | collective-permute-start | bytes 589832 | tf_op jit(solution)/shard_map/ppermute | solution.py:428
  20.2 9.5 %collective-permute-start.9 = (bf16[3,2,2,16,512]{4,3,2,1,0:T(8,128)(2,1)S(1)}, bf16[3,2,2,16,512]{4,3,2,1,0:T(8,128)(2,1)S(1)}, u32[]{:S(2)}, u32[]{:S(2)}) collective-permute-start(bf16[3,2,2,16,512]{4,3,2,1,0:T(8,128)(2,1)S(1)} %pad_maximum_fusion.refs_1_), channel_id=1, source_target_pairs={{0,2},{1,3},{2,0},{3,1},{4,6},{5,7},{6,4},{7,5},{8,10},{9,11},{10,... | collective-permute-start | bytes 589832 | tf_op jit(solution)/shard_map/ppermute | solution.py:428
  20.7 9.7 %collective-permute-start.7 = (bf16[3,2,2,16,512]{4,3,2,1,0:T(8,128)(2,1)S(1)}, bf16[3,2,2,16,512]{4,3,2,1,0:T(8,128)(2,1)S(1)}, u32[]{:S(2)}, u32[]{:S(2)}) collective-permute-start(bf16[3,2,2,16,512]{4,3,2,1,0:T(8,128)(2,1)S(1)} %pad_maximum_fusion.refs_1_), channel_id=1, source_target_pairs={{0,4},{1,5},{2,6},{3,7},{4,0},{5,1},{6,2},{7,3},{8,12},{9,13},{10,... | collective-permute-start | bytes 589832 | tf_op jit(solution)/shard_map/ppermute | solution.py:428
  21.2 9.9 %collective-permute-start.11 = (bf16[2,2,16,512]{3,2,1,0:T(8,128)(2,1)S(1)}, bf16[2,2,16,512]{3,2,1,0:T(8,128)(2,1)S(1)}, u32[]{:S(2)}, u32[]{:S(2)}) collective-permute-start(bf16[2,2,16,512]{3,2,1,0:T(8,128)(2,1)S(1)} %pad_maximum_fusion.1.refs_0_.refs_4_), channel_id=1, source_target_pairs={{0,6},{1,7},{2,4},{3,5},{4,2},{5,3},{6,0},{7,1},{8,14},{9,15},{10,... | collective-permute-start | bytes 196616 | tf_op jit(solution)/shard_map/ppermute | solution.py:428
  23.7 8.1 %collective-permute-start.8 = (bf16[2,2,16,512]{3,2,1,0:T(8,128)(2,1)S(1)}, bf16[2,2,16,512]{3,2,1,0:T(8,128)(2,1)S(1)}, u32[]{:S(2)}, u32[]{:S(2)}) collective-permute-start(bf16[2,2,16,512]{3,2,1,0:T(8,128)(2,1)S(1)} %pad_maximum_fusion.1.refs_0_.refs_4_), channel_id=1, source_target_pairs={{0,4},{1,5},{2,6},{3,7},{4,0},{5,1},{6,2},{7,3},{8,12},{9,13},{10,... | collective-permute-start | bytes 196616 | tf_op jit(solution)/shard_map/ppermute | solution.py:428
  36.4 5.0 %collective-permute-start.13 = (bf16[2,2,2,16,512]{4,3,2,1,0:T(8,128)(2,1)S(1)}, bf16[2,2,2,16,512]{4,3,2,1,0:T(8,128)(2,1)S(1)}, u32[]{:S(2)}, u32[]{:S(2)}) collective-permute-start(bf16[2,2,2,16,512]{4,3,2,1,0:T(8,128)(2,1)S(1)} %get-tuple-element.77), channel_id=1, source_target_pairs={{0,4},{1,5},{2,6},{3,7},{4,0},{5,1},{6,2},{7,3},{8,12},{9,13},{10,... | collective-permute-start | bytes 393224 | tf_op jit(solution)/shard_map/ppermute | solution.py:428
  41.5 8.2 %collective-permute-start.14 = (bf16[768,512]{1,0:T(8,128)(2,1)S(1)}, bf16[768,512]{1,0:T(8,128)(2,1)S(1)}, u32[]{:S(2)}, u32[]{:S(2)}) collective-permute-start(bf16[768,512]{1,0:T(8,128)(2,1)S(1)} %get-tuple-element.79.sent_ref), channel_id=1, source_target_pairs={{0,1},{1,0},{2,3},{3,2},{4,5},{5,4},{6,7},{7,6},{8,9},{9,8},{10,11... | collective-permute-start | bytes 2359304 | tf_op jit(solution)/shard_map/ppermute | solution.py:428
  41.6 0.9 %copy-start = (bf16[768,512]{1,0:T(8,128)(2,1)}, bf16[768,512]{1,0:T(8,128)(2,1)S(1)}, u32[]{:S(2)}) copy-start(bf16[768,512]{1,0:T(8,128)(2,1)S(1)} %get-tuple-element.79.sent_ref) | copy-start | bytes 2359300
  42.4 5.9 %collective-permute-start.15 = (bf16[2,2,2,16,512]{4,3,2,1,0:T(8,128)(2,1)S(1)}, bf16[2,2,2,16,512]{4,3,2,1,0:T(8,128)(2,1)S(1)}, u32[]{:S(2)}, u32[]{:S(2)}) collective-permute-start(bf16[2,2,2,16,512]{4,3,2,1,0:T(8,128)(2,1)S(1)} %get-tuple-element.85), channel_id=1, source_target_pairs={{0,4},{1,5},{2,6},{3,7},{4,0},{5,1},{6,2},{7,3},{8,12},{9,13},{10,... | collective-permute-start | bytes 393224 | tf_op jit(solution)/shard_map/ppermute | solution.py:428
  43.9 5.7 %collective-permute-start.12 = (bf16[512,512]{1,0:T(8,128)(2,1)S(1)}, bf16[512,512]{1,0:T(8,128)(2,1)S(1)}, u32[]{:S(2)}, u32[]{:S(2)}) collective-permute-start(bf16[512,512]{1,0:T(8,128)(2,1)S(1)} %get-tuple-element.68.att_ref), channel_id=1, source_target_pairs={{0,1},{1,0},{2,3},{3,2},{4,5},{5,4},{6,7},{7,6},{8,9},{9,8},{10,11... | collective-permute-start | bytes 1572872 | tf_op jit(solution)/shard_map/ppermute | solution.py:428
  44.2 10.2 %collective-permute-start.18 = (bf16[2,2,16,512]{3,2,1,0:T(8,128)(2,1)S(1)}, bf16[2,2,16,512]{3,2,1,0:T(8,128)(2,1)S(1)}, u32[]{:S(2)}, u32[]{:S(2)}) collective-permute-start(bf16[2,2,16,512]{3,2,1,0:T(8,128)(2,1)S(1)} %get-tuple-element.96), channel_id=1, source_target_pairs={{24,0},{28,4},{25,1},{29,5},{26,2},{30,6},{27,3},{31,7}} | collective-permute-start | bytes 196616 | tf_op jit(solution)/shard_map/ppermute | solution.py:436
  45.4 9.6 %collective-permute-start.17 = (bf16[2,2,16,512]{3,2,1,0:T(8,128)(2,1)S(1)}, bf16[2,2,16,512]{3,2,1,0:T(8,128)(2,1)S(1)}, u32[]{:S(2)}, u32[]{:S(2)}) collective-permute-start(bf16[2,2,16,512]{3,2,1,0:T(8,128)(2,1)S(1)} %get-tuple-element.97), channel_id=1, source_target_pairs={{16,0},{20,4},{24,8},{28,12},{17,1},{21,5},{25,9},{29,13},{18,2},{... | collective-permute-start | bytes 196616 | tf_op jit(solution)/shard_map/ppermute | solution.py:436
  48.4 7.3 %collective-permute-start.16 = (bf16[2,2,16,512]{3,2,1,0:T(8,128)(2,1)S(1)}, bf16[2,2,16,512]{3,2,1,0:T(8,128)(2,1)S(1)}, u32[]{:S(2)}, u32[]{:S(2)}) collective-permute-start(bf16[2,2,16,512]{3,2,1,0:T(8,128)(2,1)S(1)} %fusion.2), channel_id=1, source_target_pairs={{8,0},{12,4},{16,8},{20,12},{24,16},{28,20},{9,1},{13,5},{17,9},{2... | collective-permute-start | bytes 196616 | tf_op jit(solution)/shard_map/ppermute | solution.py:436
  49.7 0.9 %copy-start.2 = (bf16[768,512]{1,0:T(8,128)(2,1)}, bf16[768,512]{1,0:T(8,128)(2,1)S(1)}, u32[]{:S(2)}) copy-start(bf16[768,512]{1,0:T(8,128)(2,1)S(1)} %collective-permute-done.14.sent_far) | copy-start | bytes 2359300
  50.6 1.1 %copy-start.1 = (bf16[768,512]{1,0:T(8,128)(2,1)S(1)}, bf16[768,512]{1,0:T(8,128)(2,1)}, u32[]{:S(2)}) copy-start(bf16[768,512]{1,0:T(8,128)(2,1)} %copy-done) | copy-start | bytes 2359300
  51.7 1.1 %copy-start.3 = (bf16[768,512]{1,0:T(8,128)(2,1)S(1)}, bf16[768,512]{1,0:T(8,128)(2,1)}, u32[]{:S(2)}) copy-start(bf16[768,512]{1,0:T(8,128)(2,1)} %copy-done.2) | copy-start | bytes 2359300
  55.7 1.3 %collective-permute-start.19 = (bf16[2,16,512]{2,1,0:T(8,128)(2,1)S(1)}, bf16[2,16,512]{2,1,0:T(8,128)(2,1)S(1)}, u32[]{:S(2)}, u32[]{:S(2)}) collective-permute-start(bf16[2,16,512]{2,1,0:T(8,128)(2,1)S(1)} %fusion.3), channel_id=1, source_target_pairs={{0,1},{1,0},{2,3},{3,2},{4,5},{5,4},{6,7},{7,6},{8,9},{9,8},{10,11... | collective-permute-start | bytes 98312 | tf_op jit(solution)/shard_map/ppermute | solution.py:428

commit v2 on v1

--- a/solution.py
+++ b/solution.py
@@ -460,7 +460,7 @@
     def far_out(count):
         return pltpu.VMEM((count,) + own_pair.shape, jnp.bfloat16)
 
-    low = (levels + 1) // 2
+    low = 1
     near_pairs = HEADS // CORES * tok_rows * members * near
     far_width = members * seq_count * part_tok
     far_pairs = HEADS // CORES * tok_rows * far_width

time: 58.1 us -> 58.5 us (level)
  waiting for transfers between devices: 11.7 us -> 10.7 us
  other arithmetic: 0.11 us -> 0.74 us
  Pallas kernels: 13.3 us -> 13.9 us
    ppermute x14, waiting for transfers between devices: 8.57 us -> 7.68 us  [hop(): return lax.ppermute(part, ('seq', 'kv'), pairs)]
    convert_element_type x2 -> x1, other arithmetic: 0.05 us -> 0.68 us  [add(): (own.astype(jnp.float32) + cross.astype(jnp.float32)).astype(jnp.bfloat16)]
    pallas_call x3, Pallas kernels: 9.81 us -> 10.4 us  [call(): pl.pallas_call(kernel, in_specs=in_specs or [WHOLE] * len(operands), out_...]
  transfers between devices with their start and end apart: 20 -> 20, of which waited for: 10 -> 8; matrix products, arithmetic and copies ran while one was open for 0% -> 0% of each run, Pallas kernels for 12% -> 12%
where the time goes in v2:
time: 58.5 us; the launch traced here: 58.2 us
  starting transfers between devices  27.9 us (48%)
  Pallas kernels  13.9 us (24%)
  waiting for transfers between devices  10.7 us (18%)
  local copies, waits for them, and re-layouts  4.02 us (7%)
  between operations  0.83 us (1%)
  other arithmetic  0.74 us (1%)
    ppermute x14, starting transfers between devices, hop(): return lax.ppermute(part, ('seq', 'kv'), pairs)  14.8 us
    pallas_call x3, Pallas kernels, call(): pl.pallas_call(kernel, in_specs=in_specs or [WHOLE] * len(operands), out_...  10.4 us
    ppermute x3, starting transfers between devices, climb(): lax.ppermute(part, 'seq', [(s, s + COLUMNS * d) for s in range(seq_count...  9.27 us
    ppermute x14, waiting for transfers between devices, hop(): return lax.ppermute(part, ('seq', 'kv'), pairs)  7.68 us
    unnamed x8, local copies, waits for them, and re-layouts  4.02 us
    ppermute x3, starting transfers between devices, sink(): lax.ppermute(part, 'seq', [(s, s - COLUMNS * d) for s in range(COLUMNS *...  3.85 us
    ppermute x3, waiting for transfers between devices, climb(): lax.ppermute(part, 'seq', [(s, s + COLUMNS * d) for s in range(seq_count...  1.87 us
    pallas_call x1, Pallas kernels, join(): pl.pallas_call(join_kernel, in_specs=[WHOLE] * len(operands), out_specs=[...  1.54 us
  transfers between devices with their start and end apart: 20, of which 8 were waited for; matrix products, arithmetic and copies ran while one was open for 0% of the time, Pallas kernels for 12%

profile of v2, /device:TPU:0, one launch (start us, length us, event | category | flops | bytes accessed | tf_op | source)
XLA Modules:
  0.0 58.2 jit_solution(13391164729804105724)
XLA Ops:
  0.6 1.2 %shard_map.84 = (bf16[2,8,16,512]{3,2,1,0:T(8,128)(2,1)S(1)}, bf16[2,8,16,512]{3,2,1,0:T(8,128)(2,1)S(1)}, bf16[2,16,512]{2,1,0:T(8,128)(2,1)S(1)}, bf16[2,16,512]{2,1,0:T(8,128)(2,1)S(1)}, f32[8,128]{1,0:T(8,128)S(1)}) custom-call(s32[15,64]{1,0:T(8,128)} %bitcast.38, bf16[8,16,1024]{2,1,0:T(8,128)(2,1)} %keys_hbm.1, bf16[8,16,1024]{2,1,0:T(8,128)(2,1)} %values_hbm.1), custom_call_target="tpu_custom_call" | custom-call | tf_op jit(solution)/shard_map/pallas_call | solution.py:74
  2.5 2.9 %collective-permute-start.5 = (bf16[2,8,16,512]{3,2,1,0:T(8,128)(2,1)S(1)}, bf16[2,8,16,512]{3,2,1,0:T(8,128)(2,1)S(1)}, u32[]{:S(2)}, u32[]{:S(2)}) collective-permute-start(bf16[2,8,16,512]{3,2,1,0:T(8,128)(2,1)S(1)} %get-tuple-element.53), channel_id=1, source_target_pairs={{0,2},{1,3},{2,0},{3,1},{4,6},{5,7},{6,4},{7,5},{8,10},{9,11},{10,... | collective-permute-start | bytes 786440 | tf_op jit(solution)/shard_map/ppermute | solution.py:428
  5.4 1.0 %collective-permute-start.6 = (bf16[2,8,16,512]{3,2,1,0:T(8,128)(2,1)S(1)}, bf16[2,8,16,512]{3,2,1,0:T(8,128)(2,1)S(1)}, u32[]{:S(2)}, u32[]{:S(2)}) collective-permute-start(bf16[2,8,16,512]{3,2,1,0:T(8,128)(2,1)S(1)} %collective-permute-done.4), channel_id=1, source_target_pairs={{0,2},{1,3},{2,0},{3,1},{4,6},{5,7},{6,4},{7,5},{8,10},{9,11},{10,... | collective-permute-start | bytes 786440 | tf_op jit(solution)/shard_map/ppermute | solution.py:428
  6.4 5.5 %collective-permute-start.3 = (bf16[2,2,16,512]{3,2,1,0:T(8,128)(2,1)S(1)}, bf16[2,2,16,512]{3,2,1,0:T(8,128)(2,1)S(1)}, u32[]{:S(2)}, u32[]{:S(2)}) collective-permute-start(bf16[2,2,16,512]{3,2,1,0:T(8,128)(2,1)S(1)} %pad_maximum_fusion.1.refs_0_.refs_4_), channel_id=1, source_target_pairs={{0,24},{4,28},{1,25},{5,29},{2,26},{6,30},{3,27},{7,31}} | collective-permute-start | bytes 196616 | tf_op jit(solution)/shard_map/ppermute | solution.py:431
  12.0 1.3 %collective-permute-start.2 = (bf16[2,2,16,512]{3,2,1,0:T(8,128)(2,1)S(1)}, bf16[2,2,16,512]{3,2,1,0:T(8,128)(2,1)S(1)}, u32[]{:S(2)}, u32[]{:S(2)}) collective-permute-start(bf16[2,2,16,512]{3,2,1,0:T(8,128)(2,1)S(1)} %pad_maximum_fusion.1.refs_0_.refs_4_), channel_id=1, source_target_pairs={{0,16},{4,20},{8,24},{12,28},{1,17},{5,21},{9,25},{13,29},{2,18},{... | collective-permute-start | bytes 196616 | tf_op jit(solution)/shard_map/ppermute | solution.py:431
  13.3 2.5 %collective-permute-start.1 = (bf16[2,2,16,512]{3,2,1,0:T(8,128)(2,1)S(1)}, bf16[2,2,16,512]{3,2,1,0:T(8,128)(2,1)S(1)}, u32[]{:S(2)}, u32[]{:S(2)}) collective-permute-start(bf16[2,2,16,512]{3,2,1,0:T(8,128)(2,1)S(1)} %pad_maximum_fusion.1.refs_0_.refs_4_), channel_id=1, source_target_pairs={{0,8},{4,12},{8,16},{12,20},{16,24},{20,28},{1,9},{5,13},{9,17},{1... | collective-permute-start | bytes 196616 | tf_op jit(solution)/shard_map/ppermute | solution.py:431
  15.8 1.9 %collective-permute-done.1 = bf16[2,2,16,512]{3,2,1,0:T(8,128)(2,1)S(1)} collective-permute-done((bf16[2,2,16,512]{3,2,1,0:T(8,128)(2,1)S(1)}, bf16[2,2,16,512]{3,2,1,0:T(8,128)(2,1)S(1)}, u32[]{:S(2)}, u32[]{:S(2)}) %collective-permute-start.1) | collective-permute-done | bytes 65568 | tf_op jit(solution)/shard_map/ppermute | solution.py:431
  17.7 2.6 %collective-permute-start.10 = (bf16[3,2,2,16,512]{4,3,2,1,0:T(8,128)(2,1)S(1)}, bf16[3,2,2,16,512]{4,3,2,1,0:T(8,128)(2,1)S(1)}, u32[]{:S(2)}, u32[]{:S(2)}) collective-permute-start(bf16[3,2,2,16,512]{4,3,2,1,0:T(8,128)(2,1)S(1)} %pad_maximum_fusion.refs_1_), channel_id=1, source_target_pairs={{0,6},{1,7},{2,4},{3,5},{4,2},{5,3},{6,0},{7,1},{8,14},{9,15},{10,... | collective-permute-start | bytes 589832 | tf_op jit(solution)/shard_map/ppermute | solution.py:428
  21.2 2.5 %collective-permute-start.11 = (bf16[2,2,16,512]{3,2,1,0:T(8,128)(2,1)S(1)}, bf16[2,2,16,512]{3,2,1,0:T(8,128)(2,1)S(1)}, u32[]{:S(2)}, u32[]{:S(2)}) collective-permute-start(bf16[2,2,16,512]{3,2,1,0:T(8,128)(2,1)S(1)} %pad_maximum_fusion.1.refs_0_.refs_4_), channel_id=1, source_target_pairs={{0,6},{1,7},{2,4},{3,5},{4,2},{5,3},{6,0},{7,1},{8,14},{9,15},{10,... | collective-permute-start | bytes 196616 | tf_op jit(solution)/shard_map/ppermute | solution.py:428
  23.7 0.5 collective-permute-start.8
  24.3 2.7 %shard_map.85 = (f32[512,512]{1,0:T(8,128)S(1)}, f32[512,512]{1,0:T(8,128)S(1)}, f32[512,512]{1,0:T(8,128)S(1)}, bf16[512,512]{1,0:T(8,128)(2,1)S(1)}, bf16[512,512]{1,0:T(8,128)(2,1)S(1)}) custom-call(bf16[512,1024]{1,0:T(8,128)(2,1)} %q_hbm.1, bf16[512,1024]{1,0:T(8,128)(2,1)} %g_hbm.1, bf16[2,128,512]{2,1,0:T(8,128)(2,1)S(1)} %bitcast.24, ...), custom_call_target="tpu_custom_call" | custom-call | flops 1073741824 | bytes 3145728 | tf_op jit(solution)/shard_map/pallas_call | solution.py:397
  27.0 2.7 %collective-permute-done.9.refs_5_ = bf16[3,2,2,16,512]{4,3,2,1,0:T(8,128)(2,1)S(1)} collective-permute-done((bf16[3,2,2,16,512]{4,3,2,1,0:T(8,128)(2,1)S(1)}, bf16[3,2,2,16,512]{4,3,2,1,0:T(8,128)(2,1)S(1)}, u32[]{:S(2)}, u32[]{:S(2)}) %collective-permute-start.9) | collective-permute-done | bytes 196640 | tf_op jit(solution)/shard_map/ppermute | solution.py:428
  29.7 0.7 %collective-permute-done.7.refs_3_ = bf16[3,2,2,16,512]{4,3,2,1,0:T(8,128)(2,1)S(1)} collective-permute-done((bf16[3,2,2,16,512]{4,3,2,1,0:T(8,128)(2,1)S(1)}, bf16[3,2,2,16,512]{4,3,2,1,0:T(8,128)(2,1)S(1)}, u32[]{:S(2)}, u32[]{:S(2)}) %collective-permute-start.7) | collective-permute-done | bytes 196640 | tf_op jit(solution)/shard_map/ppermute | solution.py:428
  30.5 0.7 %collective-permute-done.11.refs_6_ = bf16[2,2,16,512]{3,2,1,0:T(8,128)(2,1)S(1)} collective-permute-done((bf16[2,2,16,512]{3,2,1,0:T(8,128)(2,1)S(1)}, bf16[2,2,16,512]{3,2,1,0:T(8,128)(2,1)S(1)}, u32[]{:S(2)}, u32[]{:S(2)}) %collective-permute-start.11) | collective-permute-done | bytes 65568 | tf_op jit(solution)/shard_map/ppermute | solution.py:428
  31.2 0.7 %collective-permute-done.8.refs_2_ = bf16[2,2,16,512]{3,2,1,0:T(8,128)(2,1)S(1)} collective-permute-done((bf16[2,2,16,512]{3,2,1,0:T(8,128)(2,1)S(1)}, bf16[2,2,16,512]{3,2,1,0:T(8,128)(2,1)S(1)}, u32[]{:S(2)}, u32[]{:S(2)}) %collective-permute-start.8) | collective-permute-done | bytes 65568 | tf_op jit(solution)/shard_map/ppermute | solution.py:428
  31.9 5.1 %shard_map.86 = (bf16[512,512]{1,0:T(8,128)(2,1)S(1)}, f32[512,512]{1,0:T(8,128)S(1)}, f32[512,512]{1,0:T(8,128)S(1)}, f32[512,512]{1,0:T(8,128)S(1)}, bf16[1,2,...) custom-call(bf16[512,512]{1,0:T(8,128)(2,1)S(1)} %get-tuple-element., ...), custom_call_target="tpu_custom_call" | custom-call | flops 2684354560 | bytes 4194304 | tf_op jit(solution)/shard_map/pallas_call | solution.py:397
  37.0 1.5 %collective-permute-start.13 = (bf16[3,2,2,16,512]{4,3,2,1,0:T(8,128)(2,1)S(1)}, bf16[3,2,2,16,512]{4,3,2,1,0:T(8,128)(2,1)S(1)}, u32[]{:S(2)}, u32[]{:S(2)}) collective-permute-start(bf16[3,2,2,16,512]{4,3,2,1,0:T(8,128)(2,1)S(1)} %get-tuple-element.76), channel_id=1, source_target_pairs={{0,4},{1,5},{2,6},{3,7},{4,0},{5,1},{6,2},{7,3},{8,12},{9,13},{10,... | collective-permute-start | bytes 589832 | tf_op jit(solution)/shard_map/ppermute | solution.py:428
  38.5 2.5 %shard_map.87 = (f32[2,2,16,512]{3,2,1,0:T(8,128)S(1)}, bf16[256,512]{1,0:T(8,128)(2,1)S(1)}, bf16[768,512]{1,0:T(8,128)(2,1)S(1)}) custom-call(f32[8,128]{1,0:T(8,128)S(1)} %get-tuple-element.68.block_ref, f32[512,512]{1,0:T(8,128)S(1)} %get-tuple-element.69.bias_ref, bf16[512,512]{1,0:T(8,128)(2,1)S(1)} %get-tuple-element.57.q_ref, ...), custom_call_target="tpu_custom_call" | custom-call | flops 2147483648 | bytes 6295552 | tf_op jit(solution)/shard_map/pallas_call | solution.py:397
  41.1 1.6 %collective-permute-done.13 = bf16[3,2,2,16,512]{4,3,2,1,0:T(8,128)(2,1)S(1)} collective-permute-done((bf16[3,2,2,16,512]{4,3,2,1,0:T(8,128)(2,1)S(1)}, bf16[3,2,2,16,512]{4,3,2,1,0:T(8,128)(2,1)S(1)}, u32[]{:S(2)}, u32[]{:S(2)}) %collective-permute-start.13) | collective-permute-done | bytes 196640 | tf_op jit(solution)/shard_map/ppermute | solution.py:428
  42.7 0.7 %fusion.2 = (bf16[2,2,16,512]{3,2,1,0:T(8,128)(2,1)}, bf16[2,2,16,512]{3,2,1,0:T(8,128)(2,1)S(1)}, bf16[2,2,16,512]{3,2,1,0:T(8,128)(2,1)S(1)}) fusion(bf16[3,2,2,16,512]{4,3,2,1,0:T(8,128)(2,1)S(1)} %collective-permute-done.13, bf16[3,2,2,16,512]{4,3,2,1,0:T(8,128)(2,1)S(1)} %get-tuple-element.75), kind=kLoop, calls=%fused_computation.6 | loop fusion | flops 393216 | bytes 589824 | tf_op jit(solution)/shard_map/convert_element_type | solution.py:498
  43.4 0.9 %copy-done = bf16[768,512]{1,0:T(8,128)(2,1)} copy-done((bf16[768,512]{1,0:T(8,128)(2,1)}, bf16[768,512]{1,0:T(8,128)(2,1)S(1)}, u32[]{:S(2)}) %copy-start) | copy-done | bytes 786456
  44.7 1.3 %collective-permute-start.17 = (bf16[2,2,16,512]{3,2,1,0:T(8,128)(2,1)}, bf16[2,2,16,512]{3,2,1,0:T(8,128)(2,1)S(1)}, u32[]{:S(2)}, u32[]{:S(2)}) collective-permute-start(bf16[2,2,16,512]{3,2,1,0:T(8,128)(2,1)} %get-tuple-element.94), channel_id=1, source_target_pairs={{24,0},{28,4},{25,1},{29,5},{26,2},{30,6},{27,3},{31,7}} | collective-permute-start | bytes 196616 | tf_op jit(solution)/shard_map/ppermute | solution.py:436
  46.0 1.6 %collective-permute-start.18 = (bf16[1,2,2,16,512]{4,3,2,1,0:T(8,128)(2,1)S(1)}, bf16[1,2,2,16,512]{4,3,2,1,0:T(8,128)(2,1)S(1)}, u32[]{:S(2)}, u32[]{:S(2)}) collective-permute-start(bf16[1,2,2,16,512]{4,3,2,1,0:T(8,128)(2,1)S(1)} %get-tuple-element.83), channel_id=1, source_target_pairs={{0,4},{1,5},{2,6},{3,7},{4,0},{5,1},{6,2},{7,3},{8,12},{9,13},{10,... | collective-permute-start | bytes 196616 | tf_op jit(solution)/shard_map/ppermute | solution.py:428
  47.6 1.3 %collective-permute-start.16 = (bf16[2,2,16,512]{3,2,1,0:T(8,128)(2,1)S(1)}, bf16[2,2,16,512]{3,2,1,0:T(8,128)(2,1)S(1)}, u32[]{:S(2)}, u32[]{:S(2)}) collective-permute-start(bf16[2,2,16,512]{3,2,1,0:T(8,128)(2,1)S(1)} %get-tuple-element.95), channel_id=1, source_target_pairs={{16,0},{20,4},{24,8},{28,12},{17,1},{21,5},{25,9},{29,13},{18,2},{... | collective-permute-start | bytes 196616 | tf_op jit(solution)/shard_map/ppermute | solution.py:436
  48.9 1.3 %collective-permute-start.15 = (bf16[2,2,16,512]{3,2,1,0:T(8,128)(2,1)S(1)}, bf16[2,2,16,512]{3,2,1,0:T(8,128)(2,1)S(1)}, u32[]{:S(2)}, u32[]{:S(2)}) collective-permute-start(bf16[2,2,16,512]{3,2,1,0:T(8,128)(2,1)S(1)} %get-tuple-element.96), channel_id=1, source_target_pairs={{8,0},{12,4},{16,8},{20,12},{24,16},{28,20},{9,1},{13,5},{17,9},{2... | collective-permute-start | bytes 196616 | tf_op jit(solution)/shard_map/ppermute | solution.py:436
  50.2 0.9 %copy-done.2 = bf16[768,512]{1,0:T(8,128)(2,1)} copy-done((bf16[768,512]{1,0:T(8,128)(2,1)}, bf16[768,512]{1,0:T(8,128)(2,1)S(1)}, u32[]{:S(2)}) %copy-start.2) | copy-done | bytes 786456
  51.1 1.1 %copy-done.1 = bf16[768,512]{1,0:T(8,128)(2,1)S(1)} copy-done((bf16[768,512]{1,0:T(8,128)(2,1)S(1)}, bf16[768,512]{1,0:T(8,128)(2,1)}, u32[]{:S(2)}) %copy-start.1) | copy-done | bytes 786456
  52.2 1.1 %copy-done.3 = bf16[768,512]{1,0:T(8,128)(2,1)S(1)} copy-done((bf16[768,512]{1,0:T(8,128)(2,1)S(1)}, bf16[768,512]{1,0:T(8,128)(2,1)}, u32[]{:S(2)}) %copy-start.3) | copy-done | bytes 786456
  53.4 1.5 %shard_map.88 = (bf16[512,1024]{1,0:T(8,128)(2,1)}, bf16[512,1024]{1,0:T(8,128)(2,1)}, bf16[128,1024]{1,0:T(8,128)(2,1)}, bf16[128,1024]{1,0:T(8,128)(2,1)}) custom-call(bf16[512,512]{1,0:T(8,128)(2,1)S(1)} %get-tuple-element.67.att_ref, bf16[512,512]{1,0:T(8,128)(2,1)S(1)} %collective-permute-done.12.att_far, bf16[768,512]{1,0:T(8,128)(2,1)S(1)} %copy-done.1, ...), custom_call_target="tpu_custom_call" | custom-call | tf_op jit(solution)/shard_map/pallas_call | solution.py:108
  54.9 1.2 %collective-permute-done.16.refs_1_ = bf16[2,2,16,512]{3,2,1,0:T(8,128)(2,1)S(1)} collective-permute-done((bf16[2,2,16,512]{3,2,1,0:T(8,128)(2,1)S(1)}, bf16[2,2,16,512]{3,2,1,0:T(8,128)(2,1)S(1)}, u32[]{:S(2)}, u32[]{:S(2)}) %collective-permute-start.16) | collective-permute-done | bytes 65568 | tf_op jit(solution)/shard_map/ppermute | solution.py:436
  56.2 1.2 %collective-permute-done.19.far_ref = bf16[2,16,512]{2,1,0:T(8,128)(2,1)S(1)} collective-permute-done((bf16[2,16,512]{2,1,0:T(8,128)(2,1)S(1)}, bf16[2,16,512]{2,1,0:T(8,128)(2,1)S(1)}, u32[]{:S(2)}, u32[]{:S(2)}) %collective-permute-start.19) | collective-permute-done | bytes 32800 | tf_op jit(solution)/shard_map/ppermute | solution.py:428
  57.4 0.8 %shard_map.89 = (bf16[128,1024]{1,0:T(8,128)(2,1)}, bf16[128,1024]{1,0:T(8,128)(2,1)}) custom-call(f32[8,128]{1,0:T(8,128)S(1)} %get-tuple-element.68.block_ref, f32[2,2,16,512]{3,2,1,0:T(8,128)S(1)} %get-tuple-element.82.chosen_ref, bf16[2,16,512]{2,1,0:T(8,128)(2,1)S(1)} %collective-permute-done.19.far_ref, ...), custom_call_target="tpu_custom_call", output_to_operand_aliasing={{0}: (7, {}), {1}: (8, {})} | custom-call | tf_op jit(solution)/shard_map/pallas_call | solution.py:143
  (26 shorter events, 2.3 us)
Async XLA Ops:
  1.9 3.5 %collective-permute-start.4 = (bf16[2,8,16,512]{3,2,1,0:T(8,128)(2,1)S(1)}, bf16[2,8,16,512]{3,2,1,0:T(8,128)(2,1)S(1)}, u32[]{:S(2)}, u32[]{:S(2)}) collective-permute-start(bf16[2,8,16,512]{3,2,1,0:T(8,128)(2,1)S(1)} %get-tuple-element.52), channel_id=1, source_target_pairs={{0,1},{1,0},{2,3},{3,2},{4,5},{5,4},{6,7},{7,6},{8,9},{9,8},{10,11... | collective-permute-start | bytes 786440 | tf_op jit(solution)/shard_map/ppermute | solution.py:428
  2.4 4.1 %collective-permute-start = (bf16[2,16,512]{2,1,0:T(8,128)(2,1)S(1)}, bf16[2,16,512]{2,1,0:T(8,128)(2,1)S(1)}, u32[]{:S(2)}, u32[]{:S(2)}) collective-permute-start(bf16[2,16,512]{2,1,0:T(8,128)(2,1)S(1)} %get-tuple-element.50), channel_id=1, source_target_pairs={{0,1},{1,0},{2,3},{3,2},{4,5},{5,4},{6,7},{7,6},{8,9},{9,8},{10,11... | collective-permute-start | bytes 98312 | tf_op jit(solution)/shard_map/ppermute | solution.py:428
  2.5 15.2 %collective-permute-start.5 = (bf16[2,8,16,512]{3,2,1,0:T(8,128)(2,1)S(1)}, bf16[2,8,16,512]{3,2,1,0:T(8,128)(2,1)S(1)}, u32[]{:S(2)}, u32[]{:S(2)}) collective-permute-start(bf16[2,8,16,512]{3,2,1,0:T(8,128)(2,1)S(1)} %get-tuple-element.53), channel_id=1, source_target_pairs={{0,2},{1,3},{2,0},{3,1},{4,6},{5,7},{6,4},{7,5},{8,10},{9,11},{10,... | collective-permute-start | bytes 786440 | tf_op jit(solution)/shard_map/ppermute | solution.py:428
  5.4 12.3 %collective-permute-start.6 = (bf16[2,8,16,512]{3,2,1,0:T(8,128)(2,1)S(1)}, bf16[2,8,16,512]{3,2,1,0:T(8,128)(2,1)S(1)}, u32[]{:S(2)}, u32[]{:S(2)}) collective-permute-start(bf16[2,8,16,512]{3,2,1,0:T(8,128)(2,1)S(1)} %collective-permute-done.4), channel_id=1, source_target_pairs={{0,2},{1,3},{2,0},{3,1},{4,6},{5,7},{6,4},{7,5},{8,10},{9,11},{10,... | collective-permute-start | bytes 786440 | tf_op jit(solution)/shard_map/ppermute | solution.py:428
  6.4 9.3 %collective-permute-start.3 = (bf16[2,2,16,512]{3,2,1,0:T(8,128)(2,1)S(1)}, bf16[2,2,16,512]{3,2,1,0:T(8,128)(2,1)S(1)}, u32[]{:S(2)}, u32[]{:S(2)}) collective-permute-start(bf16[2,2,16,512]{3,2,1,0:T(8,128)(2,1)S(1)} %pad_maximum_fusion.1.refs_0_.refs_4_), channel_id=1, source_target_pairs={{0,24},{4,28},{1,25},{5,29},{2,26},{6,30},{3,27},{7,31}} | collective-permute-start | bytes 196616 | tf_op jit(solution)/shard_map/ppermute | solution.py:431
  12.0 3.8 %collective-permute-start.2 = (bf16[2,2,16,512]{3,2,1,0:T(8,128)(2,1)S(1)}, bf16[2,2,16,512]{3,2,1,0:T(8,128)(2,1)S(1)}, u32[]{:S(2)}, u32[]{:S(2)}) collective-permute-start(bf16[2,2,16,512]{3,2,1,0:T(8,128)(2,1)S(1)} %pad_maximum_fusion.1.refs_0_.refs_4_), channel_id=1, source_target_pairs={{0,16},{4,20},{8,24},{12,28},{1,17},{5,21},{9,25},{13,29},{2,18},{... | collective-permute-start | bytes 196616 | tf_op jit(solution)/shard_map/ppermute | solution.py:431
  13.3 4.4 %collective-permute-start.1 = (bf16[2,2,16,512]{3,2,1,0:T(8,128)(2,1)S(1)}, bf16[2,2,16,512]{3,2,1,0:T(8,128)(2,1)S(1)}, u32[]{:S(2)}, u32[]{:S(2)}) collective-permute-start(bf16[2,2,16,512]{3,2,1,0:T(8,128)(2,1)S(1)} %pad_maximum_fusion.1.refs_0_.refs_4_), channel_id=1, source_target_pairs={{0,8},{4,12},{8,16},{12,20},{16,24},{20,28},{1,9},{5,13},{9,17},{1... | collective-permute-start | bytes 196616 | tf_op jit(solution)/shard_map/ppermute | solution.py:431
  17.7 9.3 %collective-permute-start.10 = (bf16[3,2,2,16,512]{4,3,2,1,0:T(8,128)(2,1)S(1)}, bf16[3,2,2,16,512]{4,3,2,1,0:T(8,128)(2,1)S(1)}, u32[]{:S(2)}, u32[]{:S(2)}) collective-permute-start(bf16[3,2,2,16,512]{4,3,2,1,0:T(8,128)(2,1)S(1)} %pad_maximum_fusion.refs_1_), channel_id=1, source_target_pairs={{0,6},{1,7},{2,4},{3,5},{4,2},{5,3},{6,0},{7,1},{8,14},{9,15},{10,... | collective-permute-start | bytes 589832 | tf_op jit(solution)/shard_map/ppermute | solution.py:428
  20.2 9.5 %collective-permute-start.9 = (bf16[3,2,2,16,512]{4,3,2,1,0:T(8,128)(2,1)S(1)}, bf16[3,2,2,16,512]{4,3,2,1,0:T(8,128)(2,1)S(1)}, u32[]{:S(2)}, u32[]{:S(2)}) collective-permute-start(bf16[3,2,2,16,512]{4,3,2,1,0:T(8,128)(2,1)S(1)} %pad_maximum_fusion.refs_1_), channel_id=1, source_target_pairs={{0,2},{1,3},{2,0},{3,1},{4,6},{5,7},{6,4},{7,5},{8,10},{9,11},{10,... | collective-permute-start | bytes 589832 | tf_op jit(solution)/shard_map/ppermute | solution.py:428
  20.7 9.7 %collective-permute-start.7 = (bf16[3,2,2,16,512]{4,3,2,1,0:T(8,128)(2,1)S(1)}, bf16[3,2,2,16,512]{4,3,2,1,0:T(8,128)(2,1)S(1)}, u32[]{:S(2)}, u32[]{:S(2)}) collective-permute-start(bf16[3,2,2,16,512]{4,3,2,1,0:T(8,128)(2,1)S(1)} %pad_maximum_fusion.refs_1_), channel_id=1, source_target_pairs={{0,4},{1,5},{2,6},{3,7},{4,0},{5,1},{6,2},{7,3},{8,12},{9,13},{10,... | collective-permute-start | bytes 589832 | tf_op jit(solution)/shard_map/ppermute | solution.py:428
  21.2 9.9 %collective-permute-start.11 = (bf16[2,2,16,512]{3,2,1,0:T(8,128)(2,1)S(1)}, bf16[2,2,16,512]{3,2,1,0:T(8,128)(2,1)S(1)}, u32[]{:S(2)}, u32[]{:S(2)}) collective-permute-start(bf16[2,2,16,512]{3,2,1,0:T(8,128)(2,1)S(1)} %pad_maximum_fusion.1.refs_0_.refs_4_), channel_id=1, source_target_pairs={{0,6},{1,7},{2,4},{3,5},{4,2},{5,3},{6,0},{7,1},{8,14},{9,15},{10,... | collective-permute-start | bytes 196616 | tf_op jit(solution)/shard_map/ppermute | solution.py:428
  23.7 8.1 %collective-permute-start.8 = (bf16[2,2,16,512]{3,2,1,0:T(8,128)(2,1)S(1)}, bf16[2,2,16,512]{3,2,1,0:T(8,128)(2,1)S(1)}, u32[]{:S(2)}, u32[]{:S(2)}) collective-permute-start(bf16[2,2,16,512]{3,2,1,0:T(8,128)(2,1)S(1)} %pad_maximum_fusion.1.refs_0_.refs_4_), channel_id=1, source_target_pairs={{0,4},{1,5},{2,6},{3,7},{4,0},{5,1},{6,2},{7,3},{8,12},{9,13},{10,... | collective-permute-start | bytes 196616 | tf_op jit(solution)/shard_map/ppermute | solution.py:428
  37.0 5.7 %collective-permute-start.13 = (bf16[3,2,2,16,512]{4,3,2,1,0:T(8,128)(2,1)S(1)}, bf16[3,2,2,16,512]{4,3,2,1,0:T(8,128)(2,1)S(1)}, u32[]{:S(2)}, u32[]{:S(2)}) collective-permute-start(bf16[3,2,2,16,512]{4,3,2,1,0:T(8,128)(2,1)S(1)} %get-tuple-element.76), channel_id=1, source_target_pairs={{0,4},{1,5},{2,6},{3,7},{4,0},{5,1},{6,2},{7,3},{8,12},{9,13},{10,... | collective-permute-start | bytes 589832 | tf_op jit(solution)/shard_map/ppermute | solution.py:428
  43.4 6.8 %collective-permute-start.14 = (bf16[768,512]{1,0:T(8,128)(2,1)S(1)}, bf16[768,512]{1,0:T(8,128)(2,1)S(1)}, u32[]{:S(2)}, u32[]{:S(2)}) collective-permute-start(bf16[768,512]{1,0:T(8,128)(2,1)S(1)} %get-tuple-element.78.sent_ref), channel_id=1, source_target_pairs={{0,1},{1,0},{2,3},{3,2},{4,5},{5,4},{6,7},{7,6},{8,9},{9,8},{10,11... | collective-permute-start | bytes 2359304 | tf_op jit(solution)/shard_map/ppermute | solution.py:428
  43.4 0.9 %copy-start = (bf16[768,512]{1,0:T(8,128)(2,1)}, bf16[768,512]{1,0:T(8,128)(2,1)S(1)}, u32[]{:S(2)}) copy-start(bf16[768,512]{1,0:T(8,128)(2,1)S(1)} %get-tuple-element.78.sent_ref) | copy-start | bytes 2359300
  44.2 4.6 %collective-permute-start.12 = (bf16[512,512]{1,0:T(8,128)(2,1)S(1)}, bf16[512,512]{1,0:T(8,128)(2,1)S(1)}, u32[]{:S(2)}, u32[]{:S(2)}) collective-permute-start(bf16[512,512]{1,0:T(8,128)(2,1)S(1)} %get-tuple-element.67.att_ref), channel_id=1, source_target_pairs={{0,1},{1,0},{2,3},{3,2},{4,5},{5,4},{6,7},{7,6},{8,9},{9,8},{10,11... | collective-permute-start | bytes 1572872 | tf_op jit(solution)/shard_map/ppermute | solution.py:428
  44.7 10.2 %collective-permute-start.17 = (bf16[2,2,16,512]{3,2,1,0:T(8,128)(2,1)}, bf16[2,2,16,512]{3,2,1,0:T(8,128)(2,1)S(1)}, u32[]{:S(2)}, u32[]{:S(2)}) collective-permute-start(bf16[2,2,16,512]{3,2,1,0:T(8,128)(2,1)} %get-tuple-element.94), channel_id=1, source_target_pairs={{24,0},{28,4},{25,1},{29,5},{26,2},{30,6},{27,3},{31,7}} | collective-permute-start | bytes 196616 | tf_op jit(solution)/shard_map/ppermute | solution.py:436
  46.0 8.9 %collective-permute-start.18 = (bf16[1,2,2,16,512]{4,3,2,1,0:T(8,128)(2,1)S(1)}, bf16[1,2,2,16,512]{4,3,2,1,0:T(8,128)(2,1)S(1)}, u32[]{:S(2)}, u32[]{:S(2)}) collective-permute-start(bf16[1,2,2,16,512]{4,3,2,1,0:T(8,128)(2,1)S(1)} %get-tuple-element.83), channel_id=1, source_target_pairs={{0,4},{1,5},{2,6},{3,7},{4,0},{5,1},{6,2},{7,3},{8,12},{9,13},{10,... | collective-permute-start | bytes 196616 | tf_op jit(solution)/shard_map/ppermute | solution.py:428
  47.6 8.5 %collective-permute-start.16 = (bf16[2,2,16,512]{3,2,1,0:T(8,128)(2,1)S(1)}, bf16[2,2,16,512]{3,2,1,0:T(8,128)(2,1)S(1)}, u32[]{:S(2)}, u32[]{:S(2)}) collective-permute-start(bf16[2,2,16,512]{3,2,1,0:T(8,128)(2,1)S(1)} %get-tuple-element.95), channel_id=1, source_target_pairs={{16,0},{20,4},{24,8},{28,12},{17,1},{21,5},{25,9},{29,13},{18,2},{... | collective-permute-start | bytes 196616 | tf_op jit(solution)/shard_map/ppermute | solution.py:436
  48.9 7.2 %collective-permute-start.15 = (bf16[2,2,16,512]{3,2,1,0:T(8,128)(2,1)S(1)}, bf16[2,2,16,512]{3,2,1,0:T(8,128)(2,1)S(1)}, u32[]{:S(2)}, u32[]{:S(2)}) collective-permute-start(bf16[2,2,16,512]{3,2,1,0:T(8,128)(2,1)S(1)} %get-tuple-element.96), channel_id=1, source_target_pairs={{8,0},{12,4},{16,8},{20,12},{24,16},{28,20},{9,1},{13,5},{17,9},{2... | collective-permute-start | bytes 196616 | tf_op jit(solution)/shard_map/ppermute | solution.py:436
  50.2 0.9 %copy-start.2 = (bf16[768,512]{1,0:T(8,128)(2,1)}, bf16[768,512]{1,0:T(8,128)(2,1)S(1)}, u32[]{:S(2)}) copy-start(bf16[768,512]{1,0:T(8,128)(2,1)S(1)} %collective-permute-done.14.sent_far) | copy-start | bytes 2359300
  51.1 1.1 %copy-start.1 = (bf16[768,512]{1,0:T(8,128)(2,1)S(1)}, bf16[768,512]{1,0:T(8,128)(2,1)}, u32[]{:S(2)}) copy-start(bf16[768,512]{1,0:T(8,128)(2,1)} %copy-done) | copy-start | bytes 2359300
  52.2 1.1 %copy-start.3 = (bf16[768,512]{1,0:T(8,128)(2,1)S(1)}, bf16[768,512]{1,0:T(8,128)(2,1)}, u32[]{:S(2)}) copy-start(bf16[768,512]{1,0:T(8,128)(2,1)} %copy-done.2) | copy-start | bytes 2359300
  56.1 1.3 %collective-permute-start.19 = (bf16[2,16,512]{2,1,0:T(8,128)(2,1)S(1)}, bf16[2,16,512]{2,1,0:T(8,128)(2,1)S(1)}, u32[]{:S(2)}, u32[]{:S(2)}) collective-permute-start(bf16[2,16,512]{2,1,0:T(8,128)(2,1)S(1)} %fusion.3), channel_id=1, source_target_pairs={{0,1},{1,0},{2,3},{3,2},{4,5},{5,4},{6,7},{7,6},{8,9},{9,8},{10,11... | collective-permute-start | bytes 98312 | tf_op jit(solution)/shard_map/ppermute | solution.py:428

commit v3 on v1

--- a/solution.py
+++ b/solution.py
@@ -511,11 +511,12 @@
         head_dim,
         scratch=[pltpu.VMEM((CORES, 2, near, half), jnp.float32)],
     )
-    high, _ = lax.optimization_barrier((high, sent))
+    high, _ = lax.optimization_barrier((high, chosen))
     sums = [add(own_high[d - low], high[d - low]) for d in range(low, levels)]
-    cross_low, sent_mine, _ = lax.optimization_barrier((cross_low, sent, sums))
+    cross_low, _ = lax.optimization_barrier((cross_low, sums))
     crossed = hop(cross_low, 1, 0)
-    sent_far = hop(sent_mine, 0, 1)
+    sent = sent + high[0, 0, 0, 0][None] * 0
+    sent_far = hop(sent, 0, 1)
     att_far = hop(attended, 0, 1)
     sums = [add(own_low[d], crossed[d]) for d in range(1, low)] + sums
     returned = [sink(part, d) for d, part in enumerate(sums, 1)] + [crossed[0]]

time: 58.1 us -> 58.2 us (level)
  no operation moved by 1% of the time
where the time goes in v3:
time: 58.2 us; the launch traced here: 57.8 us
  starting transfers between devices  27.8 us (48%)
  Pallas kernels  13.4 us (23%)
  waiting for transfers between devices  11.6 us (20%)
  local copies, waits for them, and re-layouts  4.02 us (7%)
  between operations  0.86 us (1%)
    ppermute x14, starting transfers between devices, hop(): return lax.ppermute(part, ('seq', 'kv'), pairs)  14.6 us
    pallas_call x3, Pallas kernels, call(): pl.pallas_call(kernel, in_specs=in_specs or [WHOLE] * len(operands), out_...  9.91 us
    ppermute x3, starting transfers between devices, climb(): lax.ppermute(part, 'seq', [(s, s + COLUMNS * d) for s in range(seq_count...  9.27 us
    ppermute x14, waiting for transfers between devices, hop(): return lax.ppermute(part, ('seq', 'kv'), pairs)  8.48 us
    unnamed x8, local copies, waits for them, and re-layouts  4.01 us
    ppermute x3, starting transfers between devices, sink(): lax.ppermute(part, 'seq', [(s, s - COLUMNS * d) for s in range(COLUMNS *...  3.86 us
    ppermute x3, waiting for transfers between devices, climb(): lax.ppermute(part, 'seq', [(s, s + COLUMNS * d) for s in range(seq_count...  1.87 us
    pallas_call x1, Pallas kernels, join(): pl.pallas_call(join_kernel, in_specs=[WHOLE] * len(operands), out_specs=[...  1.54 us
  transfers between devices with their start and end apart: 20, of which 10 were waited for; matrix products, arithmetic and copies ran while one was open for 0% of the time, Pallas kernels for 12%

profile of v3, /device:TPU:0, one launch (start us, length us, event | category | flops | bytes accessed | tf_op | source)
XLA Modules:
  0.0 57.8 jit_solution(8989638770810801399)
XLA Ops:
  0.6 1.2 %shard_map.84 = (bf16[2,8,16,512]{3,2,1,0:T(8,128)(2,1)S(1)}, bf16[2,8,16,512]{3,2,1,0:T(8,128)(2,1)S(1)}, bf16[2,16,512]{2,1,0:T(8,128)(2,1)S(1)}, bf16[2,16,512]{2,1,0:T(8,128)(2,1)S(1)}, f32[8,128]{1,0:T(8,128)S(1)}) custom-call(s32[15,64]{1,0:T(8,128)} %bitcast.37, bf16[8,16,1024]{2,1,0:T(8,128)(2,1)} %keys_hbm.1, bf16[8,16,1024]{2,1,0:T(8,128)(2,1)} %values_hbm.1), custom_call_target="tpu_custom_call" | custom-call | tf_op jit(solution)/shard_map/pallas_call | solution.py:74
  2.5 2.9 %collective-permute-start.5 = (bf16[2,8,16,512]{3,2,1,0:T(8,128)(2,1)S(1)}, bf16[2,8,16,512]{3,2,1,0:T(8,128)(2,1)S(1)}, u32[]{:S(2)}, u32[]{:S(2)}) collective-permute-start(bf16[2,8,16,512]{3,2,1,0:T(8,128)(2,1)S(1)} %get-tuple-element.53), channel_id=1, source_target_pairs={{0,2},{1,3},{2,0},{3,1},{4,6},{5,7},{6,4},{7,5},{8,10},{9,11},{10,... | collective-permute-start | bytes 786440 | tf_op jit(solution)/shard_map/ppermute | solution.py:428
  5.4 1.0 %collective-permute-start.6 = (bf16[2,8,16,512]{3,2,1,0:T(8,128)(2,1)S(1)}, bf16[2,8,16,512]{3,2,1,0:T(8,128)(2,1)S(1)}, u32[]{:S(2)}, u32[]{:S(2)}) collective-permute-start(bf16[2,8,16,512]{3,2,1,0:T(8,128)(2,1)S(1)} %collective-permute-done.4), channel_id=1, source_target_pairs={{0,2},{1,3},{2,0},{3,1},{4,6},{5,7},{6,4},{7,5},{8,10},{9,11},{10,... | collective-permute-start | bytes 786440 | tf_op jit(solution)/shard_map/ppermute | solution.py:428
  6.4 5.5 %collective-permute-start.3 = (bf16[2,2,16,512]{3,2,1,0:T(8,128)(2,1)S(1)}, bf16[2,2,16,512]{3,2,1,0:T(8,128)(2,1)S(1)}, u32[]{:S(2)}, u32[]{:S(2)}) collective-permute-start(bf16[2,2,16,512]{3,2,1,0:T(8,128)(2,1)S(1)} %pad_maximum_fusion.1.refs_0_.refs_4_), channel_id=1, source_target_pairs={{0,24},{4,28},{1,25},{5,29},{2,26},{6,30},{3,27},{7,31}} | collective-permute-start | bytes 196616 | tf_op jit(solution)/shard_map/ppermute | solution.py:431
  12.0 1.3 %collective-permute-start.2 = (bf16[2,2,16,512]{3,2,1,0:T(8,128)(2,1)S(1)}, bf16[2,2,16,512]{3,2,1,0:T(8,128)(2,1)S(1)}, u32[]{:S(2)}, u32[]{:S(2)}) collective-permute-start(bf16[2,2,16,512]{3,2,1,0:T(8,128)(2,1)S(1)} %pad_maximum_fusion.1.refs_0_.refs_4_), channel_id=1, source_target_pairs={{0,16},{4,20},{8,24},{12,28},{1,17},{5,21},{9,25},{13,29},{2,18},{... | collective-permute-start | bytes 196616 | tf_op jit(solution)/shard_map/ppermute | solution.py:431
  13.3 2.5 %collective-permute-start.1 = (bf16[2,2,16,512]{3,2,1,0:T(8,128)(2,1)S(1)}, bf16[2,2,16,512]{3,2,1,0:T(8,128)(2,1)S(1)}, u32[]{:S(2)}, u32[]{:S(2)}) collective-permute-start(bf16[2,2,16,512]{3,2,1,0:T(8,128)(2,1)S(1)} %pad_maximum_fusion.1.refs_0_.refs_4_), channel_id=1, source_target_pairs={{0,8},{4,12},{8,16},{12,20},{16,24},{20,28},{1,9},{5,13},{9,17},{1... | collective-permute-start | bytes 196616 | tf_op jit(solution)/shard_map/ppermute | solution.py:431
  15.8 1.9 %collective-permute-done.1 = bf16[2,2,16,512]{3,2,1,0:T(8,128)(2,1)S(1)} collective-permute-done((bf16[2,2,16,512]{3,2,1,0:T(8,128)(2,1)S(1)}, bf16[2,2,16,512]{3,2,1,0:T(8,128)(2,1)S(1)}, u32[]{:S(2)}, u32[]{:S(2)}) %collective-permute-start.1) | collective-permute-done | bytes 65568 | tf_op jit(solution)/shard_map/ppermute | solution.py:431
  17.7 2.6 %collective-permute-start.10 = (bf16[3,2,2,16,512]{4,3,2,1,0:T(8,128)(2,1)S(1)}, bf16[3,2,2,16,512]{4,3,2,1,0:T(8,128)(2,1)S(1)}, u32[]{:S(2)}, u32[]{:S(2)}) collective-permute-start(bf16[3,2,2,16,512]{4,3,2,1,0:T(8,128)(2,1)S(1)} %pad_maximum_fusion.refs_1_), channel_id=1, source_target_pairs={{0,6},{1,7},{2,4},{3,5},{4,2},{5,3},{6,0},{7,1},{8,14},{9,15},{10,... | collective-permute-start | bytes 589832 | tf_op jit(solution)/shard_map/ppermute | solution.py:428
  21.2 2.5 %collective-permute-start.11 = (bf16[2,2,16,512]{3,2,1,0:T(8,128)(2,1)S(1)}, bf16[2,2,16,512]{3,2,1,0:T(8,128)(2,1)S(1)}, u32[]{:S(2)}, u32[]{:S(2)}) collective-permute-start(bf16[2,2,16,512]{3,2,1,0:T(8,128)(2,1)S(1)} %pad_maximum_fusion.1.refs_0_.refs_4_), channel_id=1, source_target_pairs={{0,6},{1,7},{2,4},{3,5},{4,2},{5,3},{6,0},{7,1},{8,14},{9,15},{10,... | collective-permute-start | bytes 196616 | tf_op jit(solution)/shard_map/ppermute | solution.py:428
  24.3 2.8 %shard_map.85 = (f32[512,512]{1,0:T(8,128)S(1)}, f32[512,512]{1,0:T(8,128)S(1)}, f32[512,512]{1,0:T(8,128)S(1)}, bf16[512,512]{1,0:T(8,128)(2,1)S(1)}, bf16[512,512]{1,0:T(8,128)(2,1)S(1)}) custom-call(bf16[512,1024]{1,0:T(8,128)(2,1)} %q_hbm.1, bf16[512,1024]{1,0:T(8,128)(2,1)} %g_hbm.1, bf16[2,128,512]{2,1,0:T(8,128)(2,1)S(1)} %bitcast.23, ...), custom_call_target="tpu_custom_call" | custom-call | flops 1073741824 | bytes 3145728 | tf_op jit(solution)/shard_map/pallas_call | solution.py:397
  27.1 2.7 %collective-permute-done.9.refs_5_ = bf16[3,2,2,16,512]{4,3,2,1,0:T(8,128)(2,1)S(1)} collective-permute-done((bf16[3,2,2,16,512]{4,3,2,1,0:T(8,128)(2,1)S(1)}, bf16[3,2,2,16,512]{4,3,2,1,0:T(8,128)(2,1)S(1)}, u32[]{:S(2)}, u32[]{:S(2)}) %collective-permute-start.9) | collective-permute-done | bytes 196640 | tf_op jit(solution)/shard_map/ppermute | solution.py:428
  29.7 0.7 %collective-permute-done.7.refs_3_ = bf16[3,2,2,16,512]{4,3,2,1,0:T(8,128)(2,1)S(1)} collective-permute-done((bf16[3,2,2,16,512]{4,3,2,1,0:T(8,128)(2,1)S(1)}, bf16[3,2,2,16,512]{4,3,2,1,0:T(8,128)(2,1)S(1)}, u32[]{:S(2)}, u32[]{:S(2)}) %collective-permute-start.7) | collective-permute-done | bytes 196640 | tf_op jit(solution)/shard_map/ppermute | solution.py:428
  30.5 0.7 %collective-permute-done.11.refs_6_ = bf16[2,2,16,512]{3,2,1,0:T(8,128)(2,1)S(1)} collective-permute-done((bf16[2,2,16,512]{3,2,1,0:T(8,128)(2,1)S(1)}, bf16[2,2,16,512]{3,2,1,0:T(8,128)(2,1)S(1)}, u32[]{:S(2)}, u32[]{:S(2)}) %collective-permute-start.11) | collective-permute-done | bytes 65568 | tf_op jit(solution)/shard_map/ppermute | solution.py:428
  31.2 0.7 %collective-permute-done.8.refs_2_ = bf16[2,2,16,512]{3,2,1,0:T(8,128)(2,1)S(1)} collective-permute-done((bf16[2,2,16,512]{3,2,1,0:T(8,128)(2,1)S(1)}, bf16[2,2,16,512]{3,2,1,0:T(8,128)(2,1)S(1)}, u32[]{:S(2)}, u32[]{:S(2)}) %collective-permute-start.8) | collective-permute-done | bytes 65568 | tf_op jit(solution)/shard_map/ppermute | solution.py:428
  31.9 4.5 %shard_map.86 = (bf16[512,512]{1,0:T(8,128)(2,1)S(1)}, f32[512,512]{1,0:T(8,128)S(1)}, f32[512,512]{1,0:T(8,128)S(1)}, f32[512,512]{1,0:T(8,128)S(1)}, bf16[2,2,...) custom-call(bf16[512,512]{1,0:T(8,128)(2,1)S(1)} %get-tuple-element., ...), custom_call_target="tpu_custom_call" | custom-call | flops 2684354560 | bytes 4194304 | tf_op jit(solution)/shard_map/pallas_call | solution.py:397
  36.4 1.6 %collective-permute-start.13 = (bf16[2,2,2,16,512]{4,3,2,1,0:T(8,128)(2,1)S(1)}, bf16[2,2,2,16,512]{4,3,2,1,0:T(8,128)(2,1)S(1)}, u32[]{:S(2)}, u32[]{:S(2)}) collective-permute-start(bf16[2,2,2,16,512]{4,3,2,1,0:T(8,128)(2,1)S(1)} %get-tuple-element.74), channel_id=1, source_target_pairs={{0,4},{1,5},{2,6},{3,7},{4,0},{5,1},{6,2},{7,3},{8,12},{9,13},{10,... | collective-permute-start | bytes 393224 | tf_op jit(solution)/shard_map/ppermute | solution.py:428
  38.0 2.6 %shard_map.87 = (f32[2,2,16,512]{3,2,1,0:T(8,128)S(1)}, bf16[256,512]{1,0:T(8,128)(2,1)S(1)}, bf16[768,512]{1,0:T(8,128)(2,1)S(1)}) custom-call(f32[8,128]{1,0:T(8,128)S(1)} %get-tuple-element.68.block_ref, f32[512,512]{1,0:T(8,128)S(1)} %get-tuple-element.69.bias_ref, bf16[512,512]{1,0:T(8,128)(2,1)S(1)} %get-tuple-element.57.q_ref, ...), custom_call_target="tpu_custom_call" | custom-call | flops 2147483648 | bytes 6295552 | tf_op jit(solution)/shard_map/pallas_call | solution.py:397
  40.5 0.9 %collective-permute-done.13 = bf16[2,2,2,16,512]{4,3,2,1,0:T(8,128)(2,1)S(1)} collective-permute-done((bf16[2,2,2,16,512]{4,3,2,1,0:T(8,128)(2,1)S(1)}, bf16[2,2,2,16,512]{4,3,2,1,0:T(8,128)(2,1)S(1)}, u32[]{:S(2)}, u32[]{:S(2)}) %collective-permute-start.13) | collective-permute-done | bytes 131104 | tf_op jit(solution)/shard_map/ppermute | solution.py:428
  41.6 0.9 %copy-done = bf16[768,512]{1,0:T(8,128)(2,1)} copy-done((bf16[768,512]{1,0:T(8,128)(2,1)}, bf16[768,512]{1,0:T(8,128)(2,1)S(1)}, u32[]{:S(2)}) %copy-start) | copy-done | bytes 786456
  42.5 1.6 %collective-permute-start.15 = (bf16[2,2,2,16,512]{4,3,2,1,0:T(8,128)(2,1)S(1)}, bf16[2,2,2,16,512]{4,3,2,1,0:T(8,128)(2,1)S(1)}, u32[]{:S(2)}, u32[]{:S(2)}) collective-permute-start(bf16[2,2,2,16,512]{4,3,2,1,0:T(8,128)(2,1)S(1)} %get-tuple-element.83), channel_id=1, source_target_pairs={{0,4},{1,5},{2,6},{3,7},{4,0},{5,1},{6,2},{7,3},{8,12},{9,13},{10,... | collective-permute-start | bytes 393224 | tf_op jit(solution)/shard_map/ppermute | solution.py:428
  44.3 1.3 %collective-permute-start.18 = (bf16[2,2,16,512]{3,2,1,0:T(8,128)(2,1)S(1)}, bf16[2,2,16,512]{3,2,1,0:T(8,128)(2,1)S(1)}, u32[]{:S(2)}, u32[]{:S(2)}) collective-permute-start(bf16[2,2,16,512]{3,2,1,0:T(8,128)(2,1)S(1)} %get-tuple-element.94), channel_id=1, source_target_pairs={{24,0},{28,4},{25,1},{29,5},{26,2},{30,6},{27,3},{31,7}} | collective-permute-start | bytes 196616 | tf_op jit(solution)/shard_map/ppermute | solution.py:436
  45.6 1.3 %collective-permute-start.17 = (bf16[2,2,16,512]{3,2,1,0:T(8,128)(2,1)S(1)}, bf16[2,2,16,512]{3,2,1,0:T(8,128)(2,1)S(1)}, u32[]{:S(2)}, u32[]{:S(2)}) collective-permute-start(bf16[2,2,16,512]{3,2,1,0:T(8,128)(2,1)S(1)} %get-tuple-element.95), channel_id=1, source_target_pairs={{16,0},{20,4},{24,8},{28,12},{17,1},{21,5},{25,9},{29,13},{18,2},{... | collective-permute-start | bytes 196616 | tf_op jit(solution)/shard_map/ppermute | solution.py:436
  46.9 1.6 %collective-permute-done.15 = bf16[2,2,2,16,512]{4,3,2,1,0:T(8,128)(2,1)S(1)} collective-permute-done((bf16[2,2,2,16,512]{4,3,2,1,0:T(8,128)(2,1)S(1)}, bf16[2,2,2,16,512]{4,3,2,1,0:T(8,128)(2,1)S(1)}, u32[]{:S(2)}, u32[]{:S(2)}) %collective-permute-start.15) | collective-permute-done | bytes 131104 | tf_op jit(solution)/shard_map/ppermute | solution.py:428
  48.5 1.3 %collective-permute-start.16 = (bf16[2,2,16,512]{3,2,1,0:T(8,128)(2,1)S(1)}, bf16[2,2,16,512]{3,2,1,0:T(8,128)(2,1)S(1)}, u32[]{:S(2)}, u32[]{:S(2)}) collective-permute-start(bf16[2,2,16,512]{3,2,1,0:T(8,128)(2,1)S(1)} %fusion.2), channel_id=1, source_target_pairs={{8,0},{12,4},{16,8},{20,12},{24,16},{28,20},{9,1},{13,5},{17,9},{2... | collective-permute-start | bytes 196616 | tf_op jit(solution)/shard_map/ppermute | solution.py:436
  49.9 0.9 %copy-done.2 = bf16[768,512]{1,0:T(8,128)(2,1)} copy-done((bf16[768,512]{1,0:T(8,128)(2,1)}, bf16[768,512]{1,0:T(8,128)(2,1)S(1)}, u32[]{:S(2)}) %copy-start.2) | copy-done | bytes 786456
  50.7 1.1 %copy-done.1 = bf16[768,512]{1,0:T(8,128)(2,1)S(1)} copy-done((bf16[768,512]{1,0:T(8,128)(2,1)S(1)}, bf16[768,512]{1,0:T(8,128)(2,1)}, u32[]{:S(2)}) %copy-start.1) | copy-done | bytes 786456
  51.9 1.1 %copy-done.3 = bf16[768,512]{1,0:T(8,128)(2,1)S(1)} copy-done((bf16[768,512]{1,0:T(8,128)(2,1)S(1)}, bf16[768,512]{1,0:T(8,128)(2,1)}, u32[]{:S(2)}) %copy-start.3) | copy-done | bytes 786456
  53.0 1.5 %shard_map.88 = (bf16[512,1024]{1,0:T(8,128)(2,1)}, bf16[512,1024]{1,0:T(8,128)(2,1)}, bf16[128,1024]{1,0:T(8,128)(2,1)}, bf16[128,1024]{1,0:T(8,128)(2,1)}) custom-call(bf16[512,512]{1,0:T(8,128)(2,1)S(1)} %get-tuple-element.67.att_ref, bf16[512,512]{1,0:T(8,128)(2,1)S(1)} %collective-permute-done.12.att_far, bf16[768,512]{1,0:T(8,128)(2,1)S(1)} %copy-done.1, ...), custom_call_target="tpu_custom_call" | custom-call | tf_op jit(solution)/shard_map/pallas_call | solution.py:108
  54.5 0.6 %collective-permute-done.17.refs_1_ = bf16[2,2,16,512]{3,2,1,0:T(8,128)(2,1)S(1)} collective-permute-done((bf16[2,2,16,512]{3,2,1,0:T(8,128)(2,1)S(1)}, bf16[2,2,16,512]{3,2,1,0:T(8,128)(2,1)S(1)}, u32[]{:S(2)}, u32[]{:S(2)}) %collective-permute-start.17) | collective-permute-done | bytes 65568 | tf_op jit(solution)/shard_map/ppermute | solution.py:436
  55.2 0.6 %collective-permute-done.16.refs_0_ = bf16[2,2,16,512]{3,2,1,0:T(8,128)(2,1)S(1)} collective-permute-done((bf16[2,2,16,512]{3,2,1,0:T(8,128)(2,1)S(1)}, bf16[2,2,16,512]{3,2,1,0:T(8,128)(2,1)S(1)}, u32[]{:S(2)}, u32[]{:S(2)}) %collective-permute-start.16) | collective-permute-done | bytes 65568 | tf_op jit(solution)/shard_map/ppermute | solution.py:436
  55.9 1.2 %collective-permute-done.19.far_ref = bf16[2,16,512]{2,1,0:T(8,128)(2,1)S(1)} collective-permute-done((bf16[2,16,512]{2,1,0:T(8,128)(2,1)S(1)}, bf16[2,16,512]{2,1,0:T(8,128)(2,1)S(1)}, u32[]{:S(2)}, u32[]{:S(2)}) %collective-permute-start.19) | collective-permute-done | bytes 32800 | tf_op jit(solution)/shard_map/ppermute | solution.py:428
  57.1 0.8 %shard_map.89 = (bf16[128,1024]{1,0:T(8,128)(2,1)}, bf16[128,1024]{1,0:T(8,128)(2,1)}) custom-call(f32[8,128]{1,0:T(8,128)S(1)} %get-tuple-element.68.block_ref, f32[2,2,16,512]{3,2,1,0:T(8,128)S(1)} %get-tuple-element.75.chosen_ref, bf16[2,16,512]{2,1,0:T(8,128)(2,1)S(1)} %collective-permute-done.19.far_ref, ...), custom_call_target="tpu_custom_call", output_to_operand_aliasing={{0}: (7, {}), {1}: (8, {})} | custom-call | tf_op jit(solution)/shard_map/pallas_call | solution.py:143
  (30 shorter events, 2.7 us)
Async XLA Ops:
  1.9 3.5 %collective-permute-start.4 = (bf16[2,8,16,512]{3,2,1,0:T(8,128)(2,1)S(1)}, bf16[2,8,16,512]{3,2,1,0:T(8,128)(2,1)S(1)}, u32[]{:S(2)}, u32[]{:S(2)}) collective-permute-start(bf16[2,8,16,512]{3,2,1,0:T(8,128)(2,1)S(1)} %get-tuple-element.52), channel_id=1, source_target_pairs={{0,1},{1,0},{2,3},{3,2},{4,5},{5,4},{6,7},{7,6},{8,9},{9,8},{10,11... | collective-permute-start | bytes 786440 | tf_op jit(solution)/shard_map/ppermute | solution.py:428
  2.4 4.1 %collective-permute-start = (bf16[2,16,512]{2,1,0:T(8,128)(2,1)S(1)}, bf16[2,16,512]{2,1,0:T(8,128)(2,1)S(1)}, u32[]{:S(2)}, u32[]{:S(2)}) collective-permute-start(bf16[2,16,512]{2,1,0:T(8,128)(2,1)S(1)} %get-tuple-element.50), channel_id=1, source_target_pairs={{0,1},{1,0},{2,3},{3,2},{4,5},{5,4},{6,7},{7,6},{8,9},{9,8},{10,11... | collective-permute-start | bytes 98312 | tf_op jit(solution)/shard_map/ppermute | solution.py:428
  2.5 15.2 %collective-permute-start.5 = (bf16[2,8,16,512]{3,2,1,0:T(8,128)(2,1)S(1)}, bf16[2,8,16,512]{3,2,1,0:T(8,128)(2,1)S(1)}, u32[]{:S(2)}, u32[]{:S(2)}) collective-permute-start(bf16[2,8,16,512]{3,2,1,0:T(8,128)(2,1)S(1)} %get-tuple-element.53), channel_id=1, source_target_pairs={{0,2},{1,3},{2,0},{3,1},{4,6},{5,7},{6,4},{7,5},{8,10},{9,11},{10,... | collective-permute-start | bytes 786440 | tf_op jit(solution)/shard_map/ppermute | solution.py:428
  5.4 12.3 %collective-permute-start.6 = (bf16[2,8,16,512]{3,2,1,0:T(8,128)(2,1)S(1)}, bf16[2,8,16,512]{3,2,1,0:T(8,128)(2,1)S(1)}, u32[]{:S(2)}, u32[]{:S(2)}) collective-permute-start(bf16[2,8,16,512]{3,2,1,0:T(8,128)(2,1)S(1)} %collective-permute-done.4), channel_id=1, source_target_pairs={{0,2},{1,3},{2,0},{3,1},{4,6},{5,7},{6,4},{7,5},{8,10},{9,11},{10,... | collective-permute-start | bytes 786440 | tf_op jit(solution)/shard_map/ppermute | solution.py:428
  6.4 9.3 %collective-permute-start.3 = (bf16[2,2,16,512]{3,2,1,0:T(8,128)(2,1)S(1)}, bf16[2,2,16,512]{3,2,1,0:T(8,128)(2,1)S(1)}, u32[]{:S(2)}, u32[]{:S(2)}) collective-permute-start(bf16[2,2,16,512]{3,2,1,0:T(8,128)(2,1)S(1)} %pad_maximum_fusion.1.refs_0_.refs_4_), channel_id=1, source_target_pairs={{0,24},{4,28},{1,25},{5,29},{2,26},{6,30},{3,27},{7,31}} | collective-permute-start | bytes 196616 | tf_op jit(solution)/shard_map/ppermute | solution.py:431
  12.0 3.8 %collective-permute-start.2 = (bf16[2,2,16,512]{3,2,1,0:T(8,128)(2,1)S(1)}, bf16[2,2,16,512]{3,2,1,0:T(8,128)(2,1)S(1)}, u32[]{:S(2)}, u32[]{:S(2)}) collective-permute-start(bf16[2,2,16,512]{3,2,1,0:T(8,128)(2,1)S(1)} %pad_maximum_fusion.1.refs_0_.refs_4_), channel_id=1, source_target_pairs={{0,16},{4,20},{8,24},{12,28},{1,17},{5,21},{9,25},{13,29},{2,18},{... | collective-permute-start | bytes 196616 | tf_op jit(solution)/shard_map/ppermute | solution.py:431
  13.3 4.4 %collective-permute-start.1 = (bf16[2,2,16,512]{3,2,1,0:T(8,128)(2,1)S(1)}, bf16[2,2,16,512]{3,2,1,0:T(8,128)(2,1)S(1)}, u32[]{:S(2)}, u32[]{:S(2)}) collective-permute-start(bf16[2,2,16,512]{3,2,1,0:T(8,128)(2,1)S(1)} %pad_maximum_fusion.1.refs_0_.refs_4_), channel_id=1, source_target_pairs={{0,8},{4,12},{8,16},{12,20},{16,24},{20,28},{1,9},{5,13},{9,17},{1... | collective-permute-start | bytes 196616 | tf_op jit(solution)/shard_map/ppermute | solution.py:431
  17.7 9.4 %collective-permute-start.10 = (bf16[3,2,2,16,512]{4,3,2,1,0:T(8,128)(2,1)S(1)}, bf16[3,2,2,16,512]{4,3,2,1,0:T(8,128)(2,1)S(1)}, u32[]{:S(2)}, u32[]{:S(2)}) collective-permute-start(bf16[3,2,2,16,512]{4,3,2,1,0:T(8,128)(2,1)S(1)} %pad_maximum_fusion.refs_1_), channel_id=1, source_target_pairs={{0,6},{1,7},{2,4},{3,5},{4,2},{5,3},{6,0},{7,1},{8,14},{9,15},{10,... | collective-permute-start | bytes 589832 | tf_op jit(solution)/shard_map/ppermute | solution.py:428
  20.2 9.5 %collective-permute-start.9 = (bf16[3,2,2,16,512]{4,3,2,1,0:T(8,128)(2,1)S(1)}, bf16[3,2,2,16,512]{4,3,2,1,0:T(8,128)(2,1)S(1)}, u32[]{:S(2)}, u32[]{:S(2)}) collective-permute-start(bf16[3,2,2,16,512]{4,3,2,1,0:T(8,128)(2,1)S(1)} %pad_maximum_fusion.refs_1_), channel_id=1, source_target_pairs={{0,2},{1,3},{2,0},{3,1},{4,6},{5,7},{6,4},{7,5},{8,10},{9,11},{10,... | collective-permute-start | bytes 589832 | tf_op jit(solution)/shard_map/ppermute | solution.py:428
  20.7 9.7 %collective-permute-start.7 = (bf16[3,2,2,16,512]{4,3,2,1,0:T(8,128)(2,1)S(1)}, bf16[3,2,2,16,512]{4,3,2,1,0:T(8,128)(2,1)S(1)}, u32[]{:S(2)}, u32[]{:S(2)}) collective-permute-start(bf16[3,2,2,16,512]{4,3,2,1,0:T(8,128)(2,1)S(1)} %pad_maximum_fusion.refs_1_), channel_id=1, source_target_pairs={{0,4},{1,5},{2,6},{3,7},{4,0},{5,1},{6,2},{7,3},{8,12},{9,13},{10,... | collective-permute-start | bytes 589832 | tf_op jit(solution)/shard_map/ppermute | solution.py:428
  21.2 9.9 %collective-permute-start.11 = (bf16[2,2,16,512]{3,2,1,0:T(8,128)(2,1)S(1)}, bf16[2,2,16,512]{3,2,1,0:T(8,128)(2,1)S(1)}, u32[]{:S(2)}, u32[]{:S(2)}) collective-permute-start(bf16[2,2,16,512]{3,2,1,0:T(8,128)(2,1)S(1)} %pad_maximum_fusion.1.refs_0_.refs_4_), channel_id=1, source_target_pairs={{0,6},{1,7},{2,4},{3,5},{4,2},{5,3},{6,0},{7,1},{8,14},{9,15},{10,... | collective-permute-start | bytes 196616 | tf_op jit(solution)/shard_map/ppermute | solution.py:428
  23.7 8.1 %collective-permute-start.8 = (bf16[2,2,16,512]{3,2,1,0:T(8,128)(2,1)S(1)}, bf16[2,2,16,512]{3,2,1,0:T(8,128)(2,1)S(1)}, u32[]{:S(2)}, u32[]{:S(2)}) collective-permute-start(bf16[2,2,16,512]{3,2,1,0:T(8,128)(2,1)S(1)} %pad_maximum_fusion.1.refs_0_.refs_4_), channel_id=1, source_target_pairs={{0,4},{1,5},{2,6},{3,7},{4,0},{5,1},{6,2},{7,3},{8,12},{9,13},{10,... | collective-permute-start | bytes 196616 | tf_op jit(solution)/shard_map/ppermute | solution.py:428
  36.4 5.0 %collective-permute-start.13 = (bf16[2,2,2,16,512]{4,3,2,1,0:T(8,128)(2,1)S(1)}, bf16[2,2,2,16,512]{4,3,2,1,0:T(8,128)(2,1)S(1)}, u32[]{:S(2)}, u32[]{:S(2)}) collective-permute-start(bf16[2,2,2,16,512]{4,3,2,1,0:T(8,128)(2,1)S(1)} %get-tuple-element.74), channel_id=1, source_target_pairs={{0,4},{1,5},{2,6},{3,7},{4,0},{5,1},{6,2},{7,3},{8,12},{9,13},{10,... | collective-permute-start | bytes 393224 | tf_op jit(solution)/shard_map/ppermute | solution.py:428
  41.5 8.3 %collective-permute-start.14 = (bf16[768,512]{1,0:T(8,128)(2,1)S(1)}, bf16[768,512]{1,0:T(8,128)(2,1)S(1)}, u32[]{:S(2)}, u32[]{:S(2)}) collective-permute-start(bf16[768,512]{1,0:T(8,128)(2,1)S(1)} %broadcast_add_fusion.sent_ref), channel_id=1, source_target_pairs={{0,1},{1,0},{2,3},{3,2},{4,5},{5,4},{6,7},{7,6},{8,9},{9,8},{10,11... | collective-permute-start | bytes 2359304 | tf_op jit(solution)/shard_map/ppermute | solution.py:428
  41.6 0.9 %copy-start = (bf16[768,512]{1,0:T(8,128)(2,1)}, bf16[768,512]{1,0:T(8,128)(2,1)S(1)}, u32[]{:S(2)}) copy-start(bf16[768,512]{1,0:T(8,128)(2,1)S(1)} %broadcast_add_fusion.sent_ref) | copy-start | bytes 2359300
  42.5 6.0 %collective-permute-start.15 = (bf16[2,2,2,16,512]{4,3,2,1,0:T(8,128)(2,1)S(1)}, bf16[2,2,2,16,512]{4,3,2,1,0:T(8,128)(2,1)S(1)}, u32[]{:S(2)}, u32[]{:S(2)}) collective-permute-start(bf16[2,2,2,16,512]{4,3,2,1,0:T(8,128)(2,1)S(1)} %get-tuple-element.83), channel_id=1, source_target_pairs={{0,4},{1,5},{2,6},{3,7},{4,0},{5,1},{6,2},{7,3},{8,12},{9,13},{10,... | collective-permute-start | bytes 393224 | tf_op jit(solution)/shard_map/ppermute | solution.py:428
  44.1 5.7 %collective-permute-start.12 = (bf16[512,512]{1,0:T(8,128)(2,1)S(1)}, bf16[512,512]{1,0:T(8,128)(2,1)S(1)}, u32[]{:S(2)}, u32[]{:S(2)}) collective-permute-start(bf16[512,512]{1,0:T(8,128)(2,1)S(1)} %get-tuple-element.67.att_ref), channel_id=1, source_target_pairs={{0,1},{1,0},{2,3},{3,2},{4,5},{5,4},{6,7},{7,6},{8,9},{9,8},{10,11... | collective-permute-start | bytes 1572872 | tf_op jit(solution)/shard_map/ppermute | solution.py:428
  44.3 10.2 %collective-permute-start.18 = (bf16[2,2,16,512]{3,2,1,0:T(8,128)(2,1)S(1)}, bf16[2,2,16,512]{3,2,1,0:T(8,128)(2,1)S(1)}, u32[]{:S(2)}, u32[]{:S(2)}) collective-permute-start(bf16[2,2,16,512]{3,2,1,0:T(8,128)(2,1)S(1)} %get-tuple-element.94), channel_id=1, source_target_pairs={{24,0},{28,4},{25,1},{29,5},{26,2},{30,6},{27,3},{31,7}} | collective-permute-start | bytes 196616 | tf_op jit(solution)/shard_map/ppermute | solution.py:436
  45.6 9.6 %collective-permute-start.17 = (bf16[2,2,16,512]{3,2,1,0:T(8,128)(2,1)S(1)}, bf16[2,2,16,512]{3,2,1,0:T(8,128)(2,1)S(1)}, u32[]{:S(2)}, u32[]{:S(2)}) collective-permute-start(bf16[2,2,16,512]{3,2,1,0:T(8,128)(2,1)S(1)} %get-tuple-element.95), channel_id=1, source_target_pairs={{16,0},{20,4},{24,8},{28,12},{17,1},{21,5},{25,9},{29,13},{18,2},{... | collective-permute-start | bytes 196616 | tf_op jit(solution)/shard_map/ppermute | solution.py:436
  48.5 7.3 %collective-permute-start.16 = (bf16[2,2,16,512]{3,2,1,0:T(8,128)(2,1)S(1)}, bf16[2,2,16,512]{3,2,1,0:T(8,128)(2,1)S(1)}, u32[]{:S(2)}, u32[]{:S(2)}) collective-permute-start(bf16[2,2,16,512]{3,2,1,0:T(8,128)(2,1)S(1)} %fusion.2), channel_id=1, source_target_pairs={{8,0},{12,4},{16,8},{20,12},{24,16},{28,20},{9,1},{13,5},{17,9},{2... | collective-permute-start | bytes 196616 | tf_op jit(solution)/shard_map/ppermute | solution.py:436
  49.8 0.9 %copy-start.2 = (bf16[768,512]{1,0:T(8,128)(2,1)}, bf16[768,512]{1,0:T(8,128)(2,1)S(1)}, u32[]{:S(2)}) copy-start(bf16[768,512]{1,0:T(8,128)(2,1)S(1)} %collective-permute-done.14.sent_far) | copy-start | bytes 2359300
  50.7 1.1 %copy-start.1 = (bf16[768,512]{1,0:T(8,128)(2,1)S(1)}, bf16[768,512]{1,0:T(8,128)(2,1)}, u32[]{:S(2)}) copy-start(bf16[768,512]{1,0:T(8,128)(2,1)} %copy-done) | copy-start | bytes 2359300
  51.9 1.1 %copy-start.3 = (bf16[768,512]{1,0:T(8,128)(2,1)S(1)}, bf16[768,512]{1,0:T(8,128)(2,1)}, u32[]{:S(2)}) copy-start(bf16[768,512]{1,0:T(8,128)(2,1)} %copy-done.2) | copy-start | bytes 2359300
  55.8 1.3 %collective-permute-start.19 = (bf16[2,16,512]{2,1,0:T(8,128)(2,1)S(1)}, bf16[2,16,512]{2,1,0:T(8,128)(2,1)S(1)}, u32[]{:S(2)}, u32[]{:S(2)}) collective-permute-start(bf16[2,16,512]{2,1,0:T(8,128)(2,1)S(1)} %fusion.3), channel_id=1, source_target_pairs={{0,1},{1,0},{2,3},{3,2},{4,5},{5,4},{6,7},{7,6},{8,9},{9,8},{10,11... | collective-permute-start | bytes 98312 | tf_op jit(solution)/shard_map/ppermute | solution.py:428

commit v4 on v3

--- a/solution.py
+++ b/solution.py
@@ -82,17 +82,16 @@
     )(*operands)
 
 
-def join_kernel(att_ref, att_far, sent_ref, sent_far, kept_ref, att_out, gq_out, gk_out, gv_out, sems):
+def join_kernel(att_ref, att_far, gq_ref, gq_far, kept_ref, near_far, att_out, gq_out, gk_out, gv_out, sems):
     core = lax.axis_index("kv") % CORES
-    rows, half = att_ref.shape
-    near = gk_out.shape[0]
-    own, gk, gv = pl.ds(0, rows), pl.ds(rows, near), pl.ds(rows + near, near)
+    half, near = att_ref.shape[1], gk_out.shape[0]
+    gk, gv = pl.ds(0, near), pl.ds(near, near)
     copies = []
     for out_ref, sides in (
         (att_out, (att_ref, att_far)),
-        (gq_out, (sent_ref.at[own], sent_far.at[own])),
-        (gk_out, (kept_ref.at[pl.ds(0, near)], sent_far.at[gk])),
-        (gv_out, (kept_ref.at[pl.ds(near, near)], sent_far.at[gv])),
+        (gq_out, (gq_ref, gq_far)),
+        (gk_out, (kept_ref.at[gk], near_far.at[gk])),
+        (gv_out, (kept_ref.at[gv], near_far.at[gv])),
     ):
         for side, ref in enumerate(sides):
             cols = pl.ds(pl.multiple_of((core ^ side) * half, half), half)
@@ -328,7 +327,7 @@
 
 def near_backward_kernel(members, head_dim, blocks, block_ref, bias_ref, q_ref, g_ref, level_ref, drift_ref, far_gq_ref, *refs):
     parts, outs = refs[:members], refs[members:]
-    chosen_ref, kept_ref, sent_ref, grad_ref = outs
+    chosen_ref, kept_ref, gq_ref, sent_ref, grad_ref = outs
     rows, half = q_ref.shape
     near = parts[0].shape[1]
     score_scale = 1.0 / math.sqrt(head_dim)
@@ -359,7 +358,7 @@
             for prob, grad_prob, (cols, here, used) in zip(probs, grad_probs, units)
         ]
         for (cols, here, used), part, key in zip(units, moved, keys):
-            sent_ref[here, cols] = (
+            gq_ref[here, cols] = (
                 dot(part.astype(jnp.bfloat16), key, NN) * score_scale + far_gq_ref[here, cols]
             ).astype(jnp.bfloat16)
         grads = []
@@ -376,8 +375,7 @@
                     bottom = late[which][core * near + low : (core + 1) * near]
                     grad_ref[core, which, :low, cols] = top
                     grad_ref[core, which, low:, cols] = bottom
-                    ref, first = ((kept_ref, 0), (sent_ref, rows))[core]
-                    first += which * near
+                    ref, first = (kept_ref, sent_ref)[core], which * near
                     ref[first : first + low, cols] = top.astype(ref.dtype)
                     ref[first + low : first + near, cols] = bottom.astype(ref.dtype)
 
@@ -498,30 +496,33 @@
         return (own.astype(jnp.float32) + cross.astype(jnp.float32)).astype(jnp.bfloat16)
 
     high = hop(cross_high, 1, 0)
-    chosen, near_kept, sent = call(
+    chosen, near_kept, grad_q, sent = call(
         functools.partial(near_backward_kernel, members, head_dim, blocks),
         [block, bias, queries, grad_out, level, drift, far_gq] + near_parts,
         [
             pltpu.VMEM((CORES, 2, part_tok, half), jnp.float32),
             pltpu.VMEM((2 * near, half), jnp.bfloat16),
-            pltpu.VMEM((tok_rows + 2 * near, half), jnp.bfloat16),
+            rows_out(jnp.bfloat16),
+            pltpu.VMEM((2 * near, half), jnp.bfloat16),
         ],
         near_pairs,
         4,
         head_dim,
         scratch=[pltpu.VMEM((CORES, 2, near, half), jnp.float32)],
     )
-    high, _ = lax.optimization_barrier((high, chosen))
+    att_far = hop(attended, 0, 1)
+    high, _, _ = lax.optimization_barrier((high, chosen, att_far))
     sums = [add(own_high[d - low], high[d - low]) for d in range(low, levels)]
     cross_low, _ = lax.optimization_barrier((cross_low, sums))
     crossed = hop(cross_low, 1, 0)
-    sent = sent + high[0, 0, 0, 0][None] * 0
-    sent_far = hop(sent, 0, 1)
-    att_far = hop(attended, 0, 1)
+    nothing = high[0, 0, 0, 0][None] * 0
+    grad_q = grad_q + nothing
+    gq_far = hop(grad_q, 0, 1)
+    sent_far = hop(sent + nothing, 0, 1)
     sums = [add(own_low[d], crossed[d]) for d in range(1, low)] + sums
     returned = [sink(part, d) for d, part in enumerate(sums, 1)] + [crossed[0]]
     attended, grad_q, grad_k, grad_v = join(
-        [attended, att_far, sent, sent_far, near_kept],
+        [attended, att_far, grad_q, gq_far, near_kept, sent_far],
         [(tok_rows, feat_width)] * 2 + [(near, feat_width)] * 2,
     )
     returned, grad_k, grad_v = lax.optimization_barrier((returned, grad_k, grad_v))

time: 58.2 us -> 58.7 us (level)
  waiting for transfers between devices: 11.6 us -> 15.8 us
  local copies, waits for them, and re-layouts: 4.02 us -> 0.01 us
    unnamed x8 -> x0, local copies, waits for them, and re-layouts: 4.01 us -> none
    ppermute x14 -> x15, waiting for transfers between devices: 8.48 us -> 10.7 us  [hop(): return lax.ppermute(part, ('seq', 'kv'), pairs)]
    ppermute x3, waiting for transfers between devices: 1.23 us -> 3.24 us  [sink(): lax.ppermute(part, 'seq', [(s, s - COLUMNS * d) for s in range(COLUMNS *...]
    ppermute x14 -> x15, starting transfers between devices: 14.6 us -> 15 us  [hop(): return lax.ppermute(part, ('seq', 'kv'), pairs)]
  transfers between devices with their start and end apart: 20 -> 21, of which waited for: 10 -> 9; matrix products, arithmetic and copies ran while one was open for 0% -> 0% of each run, Pallas kernels for 12% -> 12%
where the time goes in v4:
time: 58.7 us; the launch traced here: 58.4 us
  starting transfers between devices  28.2 us (48%)
  waiting for transfers between devices  15.8 us (27%)
  Pallas kernels  13.3 us (23%)
  between operations  0.86 us (1%)
    ppermute x15, starting transfers between devices, hop(): return lax.ppermute(part, ('seq', 'kv'), pairs)  15 us
    ppermute x15, waiting for transfers between devices, hop(): return lax.ppermute(part, ('seq', 'kv'), pairs)  10.7 us
    pallas_call x3, Pallas kernels, call(): pl.pallas_call(kernel, in_specs=in_specs or [WHOLE] * len(operands), out_...  9.81 us
    ppermute x3, starting transfers between devices, climb(): lax.ppermute(part, 'seq', [(s, s + COLUMNS * d) for s in range(seq_count...  9.27 us
    ppermute x3, starting transfers between devices, sink(): lax.ppermute(part, 'seq', [(s, s - COLUMNS * d) for s in range(COLUMNS *...  3.88 us
    ppermute x3, waiting for transfers between devices, sink(): lax.ppermute(part, 'seq', [(s, s - COLUMNS * d) for s in range(COLUMNS *...  3.24 us
    ppermute x3, waiting for transfers between devices, climb(): lax.ppermute(part, 'seq', [(s, s + COLUMNS * d) for s in range(seq_count...  1.87 us
    pallas_call x1, Pallas kernels, join(): pl.pallas_call(join_kernel, in_specs=[WHOLE] * len(operands), out_specs=[...  1.56 us
  transfers between devices with their start and end apart: 21, of which 9 were waited for; matrix products, arithmetic and copies ran while one was open for 0% of the time, Pallas kernels for 12%

profile of v4, /device:TPU:0, one launch (start us, length us, event | category | flops | bytes accessed | tf_op | source)
XLA Modules:
  0.0 58.4 jit_solution(15059792045288064732)
XLA Ops:
  0.6 1.2 %shard_map.84 = (bf16[2,8,16,512]{3,2,1,0:T(8,128)(2,1)S(1)}, bf16[2,8,16,512]{3,2,1,0:T(8,128)(2,1)S(1)}, bf16[2,16,512]{2,1,0:T(8,128)(2,1)S(1)}, bf16[2,16,512]{2,1,0:T(8,128)(2,1)S(1)}, f32[8,128]{1,0:T(8,128)S(1)}) custom-call(s32[15,64]{1,0:T(8,128)} %bitcast.37, bf16[8,16,1024]{2,1,0:T(8,128)(2,1)} %keys_hbm.1, bf16[8,16,1024]{2,1,0:T(8,128)(2,1)} %values_hbm.1), custom_call_target="tpu_custom_call" | custom-call | tf_op jit(solution)/shard_map/pallas_call | solution.py:74
  1.9 0.5 collective-permute-start.4
  2.5 2.9 %collective-permute-start.5 = (bf16[2,8,16,512]{3,2,1,0:T(8,128)(2,1)S(1)}, bf16[2,8,16,512]{3,2,1,0:T(8,128)(2,1)S(1)}, u32[]{:S(2)}, u32[]{:S(2)}) collective-permute-start(bf16[2,8,16,512]{3,2,1,0:T(8,128)(2,1)S(1)} %get-tuple-element.54), channel_id=1, source_target_pairs={{0,2},{1,3},{2,0},{3,1},{4,6},{5,7},{6,4},{7,5},{8,10},{9,11},{10,... | collective-permute-start | bytes 786440 | tf_op jit(solution)/shard_map/ppermute | solution.py:426
  5.4 1.0 %collective-permute-start.6 = (bf16[2,8,16,512]{3,2,1,0:T(8,128)(2,1)S(1)}, bf16[2,8,16,512]{3,2,1,0:T(8,128)(2,1)S(1)}, u32[]{:S(2)}, u32[]{:S(2)}) collective-permute-start(bf16[2,8,16,512]{3,2,1,0:T(8,128)(2,1)S(1)} %collective-permute-done.4), channel_id=1, source_target_pairs={{0,2},{1,3},{2,0},{3,1},{4,6},{5,7},{6,4},{7,5},{8,10},{9,11},{10,... | collective-permute-start | bytes 786440 | tf_op jit(solution)/shard_map/ppermute | solution.py:426
  6.4 5.5 %collective-permute-start.3 = (bf16[2,2,16,512]{3,2,1,0:T(8,128)(2,1)S(1)}, bf16[2,2,16,512]{3,2,1,0:T(8,128)(2,1)S(1)}, u32[]{:S(2)}, u32[]{:S(2)}) collective-permute-start(bf16[2,2,16,512]{3,2,1,0:T(8,128)(2,1)S(1)} %pad_maximum_fusion.1.refs_0_.refs_4_), channel_id=1, source_target_pairs={{0,24},{4,28},{1,25},{5,29},{2,26},{6,30},{3,27},{7,31}} | collective-permute-start | bytes 196616 | tf_op jit(solution)/shard_map/ppermute | solution.py:429
  12.0 1.3 %collective-permute-start.2 = (bf16[2,2,16,512]{3,2,1,0:T(8,128)(2,1)S(1)}, bf16[2,2,16,512]{3,2,1,0:T(8,128)(2,1)S(1)}, u32[]{:S(2)}, u32[]{:S(2)}) collective-permute-start(bf16[2,2,16,512]{3,2,1,0:T(8,128)(2,1)S(1)} %pad_maximum_fusion.1.refs_0_.refs_4_), channel_id=1, source_target_pairs={{0,16},{4,20},{8,24},{12,28},{1,17},{5,21},{9,25},{13,29},{2,18},{... | collective-permute-start | bytes 196616 | tf_op jit(solution)/shard_map/ppermute | solution.py:429
  13.3 2.5 %collective-permute-start.1 = (bf16[2,2,16,512]{3,2,1,0:T(8,128)(2,1)S(1)}, bf16[2,2,16,512]{3,2,1,0:T(8,128)(2,1)S(1)}, u32[]{:S(2)}, u32[]{:S(2)}) collective-permute-start(bf16[2,2,16,512]{3,2,1,0:T(8,128)(2,1)S(1)} %pad_maximum_fusion.1.refs_0_.refs_4_), channel_id=1, source_target_pairs={{0,8},{4,12},{8,16},{12,20},{16,24},{20,28},{1,9},{5,13},{9,17},{1... | collective-permute-start | bytes 196616 | tf_op jit(solution)/shard_map/ppermute | solution.py:429
  15.8 1.9 %collective-permute-done.1 = bf16[2,2,16,512]{3,2,1,0:T(8,128)(2,1)S(1)} collective-permute-done((bf16[2,2,16,512]{3,2,1,0:T(8,128)(2,1)S(1)}, bf16[2,2,16,512]{3,2,1,0:T(8,128)(2,1)S(1)}, u32[]{:S(2)}, u32[]{:S(2)}) %collective-permute-start.1) | collective-permute-done | bytes 65568 | tf_op jit(solution)/shard_map/ppermute | solution.py:429
  17.7 2.6 %collective-permute-start.10 = (bf16[3,2,2,16,512]{4,3,2,1,0:T(8,128)(2,1)S(1)}, bf16[3,2,2,16,512]{4,3,2,1,0:T(8,128)(2,1)S(1)}, u32[]{:S(2)}, u32[]{:S(2)}) collective-permute-start(bf16[3,2,2,16,512]{4,3,2,1,0:T(8,128)(2,1)S(1)} %pad_maximum_fusion.refs_1_), channel_id=1, source_target_pairs={{0,6},{1,7},{2,4},{3,5},{4,2},{5,3},{6,0},{7,1},{8,14},{9,15},{10,... | collective-permute-start | bytes 589832 | tf_op jit(solution)/shard_map/ppermute | solution.py:426
  20.2 0.5 collective-permute-start.9
  20.7 0.5 collective-permute-start.7
  21.2 2.5 %collective-permute-start.11 = (bf16[2,2,16,512]{3,2,1,0:T(8,128)(2,1)S(1)}, bf16[2,2,16,512]{3,2,1,0:T(8,128)(2,1)S(1)}, u32[]{:S(2)}, u32[]{:S(2)}) collective-permute-start(bf16[2,2,16,512]{3,2,1,0:T(8,128)(2,1)S(1)} %pad_maximum_fusion.1.refs_0_.refs_4_), channel_id=1, source_target_pairs={{0,6},{1,7},{2,4},{3,5},{4,2},{5,3},{6,0},{7,1},{8,14},{9,15},{10,... | collective-permute-start | bytes 196616 | tf_op jit(solution)/shard_map/ppermute | solution.py:426
  23.7 0.5 collective-permute-start.8
  24.3 2.7 %shard_map.85 = (f32[512,512]{1,0:T(8,128)S(1)}, f32[512,512]{1,0:T(8,128)S(1)}, f32[512,512]{1,0:T(8,128)S(1)}, bf16[512,512]{1,0:T(8,128)(2,1)S(1)}, bf16[512,512]{1,0:T(8,128)(2,1)S(1)}) custom-call(bf16[512,1024]{1,0:T(8,128)(2,1)} %q_hbm.1, bf16[512,1024]{1,0:T(8,128)(2,1)} %g_hbm.1, bf16[2,128,512]{2,1,0:T(8,128)(2,1)S(1)} %bitcast.23, ...), custom_call_target="tpu_custom_call" | custom-call | flops 1073741824 | bytes 3145728 | tf_op jit(solution)/shard_map/pallas_call | solution.py:395
  27.0 2.7 %collective-permute-done.9.refs_5_ = bf16[3,2,2,16,512]{4,3,2,1,0:T(8,128)(2,1)S(1)} collective-permute-done((bf16[3,2,2,16,512]{4,3,2,1,0:T(8,128)(2,1)S(1)}, bf16[3,2,2,16,512]{4,3,2,1,0:T(8,128)(2,1)S(1)}, u32[]{:S(2)}, u32[]{:S(2)}) %collective-permute-start.9) | collective-permute-done | bytes 196640 | tf_op jit(solution)/shard_map/ppermute | solution.py:426
  29.7 0.7 %collective-permute-done.7.refs_3_ = bf16[3,2,2,16,512]{4,3,2,1,0:T(8,128)(2,1)S(1)} collective-permute-done((bf16[3,2,2,16,512]{4,3,2,1,0:T(8,128)(2,1)S(1)}, bf16[3,2,2,16,512]{4,3,2,1,0:T(8,128)(2,1)S(1)}, u32[]{:S(2)}, u32[]{:S(2)}) %collective-permute-start.7) | collective-permute-done | bytes 196640 | tf_op jit(solution)/shard_map/ppermute | solution.py:426
  30.5 0.7 %collective-permute-done.11.refs_6_ = bf16[2,2,16,512]{3,2,1,0:T(8,128)(2,1)S(1)} collective-permute-done((bf16[2,2,16,512]{3,2,1,0:T(8,128)(2,1)S(1)}, bf16[2,2,16,512]{3,2,1,0:T(8,128)(2,1)S(1)}, u32[]{:S(2)}, u32[]{:S(2)}) %collective-permute-start.11) | collective-permute-done | bytes 65568 | tf_op jit(solution)/shard_map/ppermute | solution.py:426
  31.2 0.7 %collective-permute-done.8.refs_2_ = bf16[2,2,16,512]{3,2,1,0:T(8,128)(2,1)S(1)} collective-permute-done((bf16[2,2,16,512]{3,2,1,0:T(8,128)(2,1)S(1)}, bf16[2,2,16,512]{3,2,1,0:T(8,128)(2,1)S(1)}, u32[]{:S(2)}, u32[]{:S(2)}) %collective-permute-start.8) | collective-permute-done | bytes 65568 | tf_op jit(solution)/shard_map/ppermute | solution.py:426
  31.9 4.5 %shard_map.86 = (bf16[512,512]{1,0:T(8,128)(2,1)S(1)}, f32[512,512]{1,0:T(8,128)S(1)}, f32[512,512]{1,0:T(8,128)S(1)}, f32[512,512]{1,0:T(8,128)S(1)}, bf16[2,2,...) custom-call(bf16[512,512]{1,0:T(8,128)(2,1)S(1)} %get-tuple-element., ...), custom_call_target="tpu_custom_call" | custom-call | flops 2684354560 | bytes 4194304 | tf_op jit(solution)/shard_map/pallas_call | solution.py:395
  36.5 1.6 %collective-permute-start.13 = (bf16[2,2,2,16,512]{4,3,2,1,0:T(8,128)(2,1)S(1)}, bf16[2,2,2,16,512]{4,3,2,1,0:T(8,128)(2,1)S(1)}, u32[]{:S(2)}, u32[]{:S(2)}) collective-permute-start(bf16[2,2,2,16,512]{4,3,2,1,0:T(8,128)(2,1)S(1)} %get-tuple-element.75), channel_id=1, source_target_pairs={{0,4},{1,5},{2,6},{3,7},{4,0},{5,1},{6,2},{7,3},{8,12},{9,13},{10,... | collective-permute-start | bytes 393224 | tf_op jit(solution)/shard_map/ppermute | solution.py:426
  38.0 2.5 %shard_map.87 = (f32[2,2,16,512]{3,2,1,0:T(8,128)S(1)}, bf16[256,512]{1,0:T(8,128)(2,1)S(1)}, bf16[512,512]{1,0:T(8,128)(2,1)S(1)}, bf16[256,512]{1,0:T(8,128)(2,1)S(1)}) custom-call(f32[8,128]{1,0:T(8,128)S(1)} %get-tuple-element.69.block_ref, f32[512,512]{1,0:T(8,128)S(1)} %get-tuple-element.70.bias_ref, bf16[512,512]{1,0:T(8,128)(2,1)S(1)} %get-tuple-element.58.q_ref, ...), custom_call_target="tpu_custom_call" | custom-call | flops 2147483648 | bytes 6295552 | tf_op jit(solution)/shard_map/pallas_call | solution.py:395
  40.6 1.8 %collective-permute-done.13 = bf16[2,2,2,16,512]{4,3,2,1,0:T(8,128)(2,1)S(1)} collective-permute-done((bf16[2,2,2,16,512]{4,3,2,1,0:T(8,128)(2,1)S(1)}, bf16[2,2,2,16,512]{4,3,2,1,0:T(8,128)(2,1)S(1)}, u32[]{:S(2)}, u32[]{:S(2)}) %collective-permute-start.13) | collective-permute-done | bytes 131104 | tf_op jit(solution)/shard_map/ppermute | solution.py:426
  42.5 1.3 %collective-permute-start.19 = (bf16[2,2,16,512]{3,2,1,0:T(8,128)(2,1)S(1)}, bf16[2,2,16,512]{3,2,1,0:T(8,128)(2,1)S(1)}, u32[]{:S(2)}, u32[]{:S(2)}) collective-permute-start(bf16[2,2,16,512]{3,2,1,0:T(8,128)(2,1)S(1)} %get-tuple-element.96), channel_id=1, source_target_pairs={{24,0},{28,4},{25,1},{29,5},{26,2},{30,6},{27,3},{31,7}} | collective-permute-start | bytes 196616 | tf_op jit(solution)/shard_map/ppermute | solution.py:434
  43.8 1.3 %collective-permute-start.18 = (bf16[2,2,16,512]{3,2,1,0:T(8,128)(2,1)S(1)}, bf16[2,2,16,512]{3,2,1,0:T(8,128)(2,1)S(1)}, u32[]{:S(2)}, u32[]{:S(2)}) collective-permute-start(bf16[2,2,16,512]{3,2,1,0:T(8,128)(2,1)S(1)} %get-tuple-element.97), channel_id=1, source_target_pairs={{16,0},{20,4},{24,8},{28,12},{17,1},{21,5},{25,9},{29,13},{18,2},{... | collective-permute-start | bytes 196616 | tf_op jit(solution)/shard_map/ppermute | solution.py:434
  45.1 1.6 %collective-permute-start.16 = (bf16[2,2,2,16,512]{4,3,2,1,0:T(8,128)(2,1)S(1)}, bf16[2,2,2,16,512]{4,3,2,1,0:T(8,128)(2,1)S(1)}, u32[]{:S(2)}, u32[]{:S(2)}) collective-permute-start(bf16[2,2,2,16,512]{4,3,2,1,0:T(8,128)(2,1)S(1)} %get-tuple-element.85), channel_id=1, source_target_pairs={{0,4},{1,5},{2,6},{3,7},{4,0},{5,1},{6,2},{7,3},{8,12},{9,13},{10,... | collective-permute-start | bytes 393224 | tf_op jit(solution)/shard_map/ppermute | solution.py:426
  46.8 0.6 collective-permute-start.15
  47.3 2.9 %collective-permute-done.16 = bf16[2,2,2,16,512]{4,3,2,1,0:T(8,128)(2,1)S(1)} collective-permute-done((bf16[2,2,2,16,512]{4,3,2,1,0:T(8,128)(2,1)S(1)}, bf16[2,2,2,16,512]{4,3,2,1,0:T(8,128)(2,1)S(1)}, u32[]{:S(2)}, u32[]{:S(2)}) %collective-permute-start.16) | collective-permute-done | bytes 131104 | tf_op jit(solution)/shard_map/ppermute | solution.py:426
  50.2 1.3 %collective-permute-start.17 = (bf16[2,2,16,512]{3,2,1,0:T(8,128)(2,1)S(1)}, bf16[2,2,16,512]{3,2,1,0:T(8,128)(2,1)S(1)}, u32[]{:S(2)}, u32[]{:S(2)}) collective-permute-start(bf16[2,2,16,512]{3,2,1,0:T(8,128)(2,1)S(1)} %fusion.2), channel_id=1, source_target_pairs={{8,0},{12,4},{16,8},{20,12},{24,16},{28,20},{9,1},{13,5},{17,9},{2... | collective-permute-start | bytes 196616 | tf_op jit(solution)/shard_map/ppermute | solution.py:434
  51.6 1.6 %shard_map.88 = (bf16[512,1024]{1,0:T(8,128)(2,1)}, bf16[512,1024]{1,0:T(8,128)(2,1)}, bf16[128,1024]{1,0:T(8,128)(2,1)}, bf16[128,1024]{1,0:T(8,128)(2,1)}) custom-call(bf16[512,512]{1,0:T(8,128)(2,1)S(1)} %get-tuple-element.68.att_ref, bf16[512,512]{1,0:T(8,128)(2,1)S(1)} %collective-permute-done.12.att_far, ...), custom_call_target="tpu_custom_call" | custom-call | tf_op jit(solution)/shard_map/pallas_call | solution.py:107
  53.1 3.2 %collective-permute-done.17.refs_0_ = bf16[2,2,16,512]{3,2,1,0:T(8,128)(2,1)S(1)} collective-permute-done((bf16[2,2,16,512]{3,2,1,0:T(8,128)(2,1)S(1)}, bf16[2,2,16,512]{3,2,1,0:T(8,128)(2,1)S(1)}, u32[]{:S(2)}, u32[]{:S(2)}) %collective-permute-start.17) | collective-permute-done | bytes 65568 | tf_op jit(solution)/shard_map/ppermute | solution.py:434
  56.5 1.2 %collective-permute-done.20.far_ref = bf16[2,16,512]{2,1,0:T(8,128)(2,1)S(1)} collective-permute-done((bf16[2,16,512]{2,1,0:T(8,128)(2,1)S(1)}, bf16[2,16,512]{2,1,0:T(8,128)(2,1)S(1)}, u32[]{:S(2)}, u32[]{:S(2)}) %collective-permute-start.20) | collective-permute-done | bytes 32800 | tf_op jit(solution)/shard_map/ppermute | solution.py:426
  57.7 0.8 %shard_map.89 = (bf16[128,1024]{1,0:T(8,128)(2,1)}, bf16[128,1024]{1,0:T(8,128)(2,1)}) custom-call(f32[8,128]{1,0:T(8,128)S(1)} %get-tuple-element.69.block_ref, f32[2,2,16,512]{3,2,1,0:T(8,128)S(1)} %get-tuple-element.76.chosen_ref, bf16[2,16,512]{2,1,0:T(8,128)(2,1)S(1)} %collective-permute-done.20.far_ref, ...), custom_call_target="tpu_custom_call", output_to_operand_aliasing={{0}: (7, {}), {1}: (8, {})} | custom-call | tf_op jit(solution)/shard_map/pallas_call | solution.py:142
  (25 shorter events, 0.5 us)
Async XLA Ops:
  1.9 3.5 %collective-permute-start.4 = (bf16[2,8,16,512]{3,2,1,0:T(8,128)(2,1)S(1)}, bf16[2,8,16,512]{3,2,1,0:T(8,128)(2,1)S(1)}, u32[]{:S(2)}, u32[]{:S(2)}) collective-permute-start(bf16[2,8,16,512]{3,2,1,0:T(8,128)(2,1)S(1)} %get-tuple-element.53), channel_id=1, source_target_pairs={{0,1},{1,0},{2,3},{3,2},{4,5},{5,4},{6,7},{7,6},{8,9},{9,8},{10,11... | collective-permute-start | bytes 786440 | tf_op jit(solution)/shard_map/ppermute | solution.py:426
  2.4 4.1 %collective-permute-start = (bf16[2,16,512]{2,1,0:T(8,128)(2,1)S(1)}, bf16[2,16,512]{2,1,0:T(8,128)(2,1)S(1)}, u32[]{:S(2)}, u32[]{:S(2)}) collective-permute-start(bf16[2,16,512]{2,1,0:T(8,128)(2,1)S(1)} %get-tuple-element.51), channel_id=1, source_target_pairs={{0,1},{1,0},{2,3},{3,2},{4,5},{5,4},{6,7},{7,6},{8,9},{9,8},{10,11... | collective-permute-start | bytes 98312 | tf_op jit(solution)/shard_map/ppermute | solution.py:426
  2.5 15.2 %collective-permute-start.5 = (bf16[2,8,16,512]{3,2,1,0:T(8,128)(2,1)S(1)}, bf16[2,8,16,512]{3,2,1,0:T(8,128)(2,1)S(1)}, u32[]{:S(2)}, u32[]{:S(2)}) collective-permute-start(bf16[2,8,16,512]{3,2,1,0:T(8,128)(2,1)S(1)} %get-tuple-element.54), channel_id=1, source_target_pairs={{0,2},{1,3},{2,0},{3,1},{4,6},{5,7},{6,4},{7,5},{8,10},{9,11},{10,... | collective-permute-start | bytes 786440 | tf_op jit(solution)/shard_map/ppermute | solution.py:426
  5.4 12.3 %collective-permute-start.6 = (bf16[2,8,16,512]{3,2,1,0:T(8,128)(2,1)S(1)}, bf16[2,8,16,512]{3,2,1,0:T(8,128)(2,1)S(1)}, u32[]{:S(2)}, u32[]{:S(2)}) collective-permute-start(bf16[2,8,16,512]{3,2,1,0:T(8,128)(2,1)S(1)} %collective-permute-done.4), channel_id=1, source_target_pairs={{0,2},{1,3},{2,0},{3,1},{4,6},{5,7},{6,4},{7,5},{8,10},{9,11},{10,... | collective-permute-start | bytes 786440 | tf_op jit(solution)/shard_map/ppermute | solution.py:426
  6.4 9.3 %collective-permute-start.3 = (bf16[2,2,16,512]{3,2,1,0:T(8,128)(2,1)S(1)}, bf16[2,2,16,512]{3,2,1,0:T(8,128)(2,1)S(1)}, u32[]{:S(2)}, u32[]{:S(2)}) collective-permute-start(bf16[2,2,16,512]{3,2,1,0:T(8,128)(2,1)S(1)} %pad_maximum_fusion.1.refs_0_.refs_4_), channel_id=1, source_target_pairs={{0,24},{4,28},{1,25},{5,29},{2,26},{6,30},{3,27},{7,31}} | collective-permute-start | bytes 196616 | tf_op jit(solution)/shard_map/ppermute | solution.py:429
  12.0 3.8 %collective-permute-start.2 = (bf16[2,2,16,512]{3,2,1,0:T(8,128)(2,1)S(1)}, bf16[2,2,16,512]{3,2,1,0:T(8,128)(2,1)S(1)}, u32[]{:S(2)}, u32[]{:S(2)}) collective-permute-start(bf16[2,2,16,512]{3,2,1,0:T(8,128)(2,1)S(1)} %pad_maximum_fusion.1.refs_0_.refs_4_), channel_id=1, source_target_pairs={{0,16},{4,20},{8,24},{12,28},{1,17},{5,21},{9,25},{13,29},{2,18},{... | collective-permute-start | bytes 196616 | tf_op jit(solution)/shard_map/ppermute | solution.py:429
  13.3 4.4 %collective-permute-start.1 = (bf16[2,2,16,512]{3,2,1,0:T(8,128)(2,1)S(1)}, bf16[2,2,16,512]{3,2,1,0:T(8,128)(2,1)S(1)}, u32[]{:S(2)}, u32[]{:S(2)}) collective-permute-start(bf16[2,2,16,512]{3,2,1,0:T(8,128)(2,1)S(1)} %pad_maximum_fusion.1.refs_0_.refs_4_), channel_id=1, source_target_pairs={{0,8},{4,12},{8,16},{12,20},{16,24},{20,28},{1,9},{5,13},{9,17},{1... | collective-permute-start | bytes 196616 | tf_op jit(solution)/shard_map/ppermute | solution.py:429
  17.7 9.3 %collective-permute-start.10 = (bf16[3,2,2,16,512]{4,3,2,1,0:T(8,128)(2,1)S(1)}, bf16[3,2,2,16,512]{4,3,2,1,0:T(8,128)(2,1)S(1)}, u32[]{:S(2)}, u32[]{:S(2)}) collective-permute-start(bf16[3,2,2,16,512]{4,3,2,1,0:T(8,128)(2,1)S(1)} %pad_maximum_fusion.refs_1_), channel_id=1, source_target_pairs={{0,6},{1,7},{2,4},{3,5},{4,2},{5,3},{6,0},{7,1},{8,14},{9,15},{10,... | collective-permute-start | bytes 589832 | tf_op jit(solution)/shard_map/ppermute | solution.py:426
  20.2 9.5 %collective-permute-start.9 = (bf16[3,2,2,16,512]{4,3,2,1,0:T(8,128)(2,1)S(1)}, bf16[3,2,2,16,512]{4,3,2,1,0:T(8,128)(2,1)S(1)}, u32[]{:S(2)}, u32[]{:S(2)}) collective-permute-start(bf16[3,2,2,16,512]{4,3,2,1,0:T(8,128)(2,1)S(1)} %pad_maximum_fusion.refs_1_), channel_id=1, source_target_pairs={{0,2},{1,3},{2,0},{3,1},{4,6},{5,7},{6,4},{7,5},{8,10},{9,11},{10,... | collective-permute-start | bytes 589832 | tf_op jit(solution)/shard_map/ppermute | solution.py:426
  20.7 9.7 %collective-permute-start.7 = (bf16[3,2,2,16,512]{4,3,2,1,0:T(8,128)(2,1)S(1)}, bf16[3,2,2,16,512]{4,3,2,1,0:T(8,128)(2,1)S(1)}, u32[]{:S(2)}, u32[]{:S(2)}) collective-permute-start(bf16[3,2,2,16,512]{4,3,2,1,0:T(8,128)(2,1)S(1)} %pad_maximum_fusion.refs_1_), channel_id=1, source_target_pairs={{0,4},{1,5},{2,6},{3,7},{4,0},{5,1},{6,2},{7,3},{8,12},{9,13},{10,... | collective-permute-start | bytes 589832 | tf_op jit(solution)/shard_map/ppermute | solution.py:426
  21.2 9.9 %collective-permute-start.11 = (bf16[2,2,16,512]{3,2,1,0:T(8,128)(2,1)S(1)}, bf16[2,2,16,512]{3,2,1,0:T(8,128)(2,1)S(1)}, u32[]{:S(2)}, u32[]{:S(2)}) collective-permute-start(bf16[2,2,16,512]{3,2,1,0:T(8,128)(2,1)S(1)} %pad_maximum_fusion.1.refs_0_.refs_4_), channel_id=1, source_target_pairs={{0,6},{1,7},{2,4},{3,5},{4,2},{5,3},{6,0},{7,1},{8,14},{9,15},{10,... | collective-permute-start | bytes 196616 | tf_op jit(solution)/shard_map/ppermute | solution.py:426
  23.7 8.1 %collective-permute-start.8 = (bf16[2,2,16,512]{3,2,1,0:T(8,128)(2,1)S(1)}, bf16[2,2,16,512]{3,2,1,0:T(8,128)(2,1)S(1)}, u32[]{:S(2)}, u32[]{:S(2)}) collective-permute-start(bf16[2,2,16,512]{3,2,1,0:T(8,128)(2,1)S(1)} %pad_maximum_fusion.1.refs_0_.refs_4_), channel_id=1, source_target_pairs={{0,4},{1,5},{2,6},{3,7},{4,0},{5,1},{6,2},{7,3},{8,12},{9,13},{10,... | collective-permute-start | bytes 196616 | tf_op jit(solution)/shard_map/ppermute | solution.py:426
  36.4 6.0 %collective-permute-start.12 = (bf16[512,512]{1,0:T(8,128)(2,1)S(1)}, bf16[512,512]{1,0:T(8,128)(2,1)S(1)}, u32[]{:S(2)}, u32[]{:S(2)}) collective-permute-start(bf16[512,512]{1,0:T(8,128)(2,1)S(1)} %get-tuple-element.68.att_ref), channel_id=1, source_target_pairs={{0,1},{1,0},{2,3},{3,2},{4,5},{5,4},{6,7},{7,6},{8,9},{9,8},{10,11... | collective-permute-start | bytes 1572872 | tf_op jit(solution)/shard_map/ppermute | solution.py:426
  36.5 5.9 %collective-permute-start.13 = (bf16[2,2,2,16,512]{4,3,2,1,0:T(8,128)(2,1)S(1)}, bf16[2,2,2,16,512]{4,3,2,1,0:T(8,128)(2,1)S(1)}, u32[]{:S(2)}, u32[]{:S(2)}) collective-permute-start(bf16[2,2,2,16,512]{4,3,2,1,0:T(8,128)(2,1)S(1)} %get-tuple-element.75), channel_id=1, source_target_pairs={{0,4},{1,5},{2,6},{3,7},{4,0},{5,1},{6,2},{7,3},{8,12},{9,13},{10,... | collective-permute-start | bytes 393224 | tf_op jit(solution)/shard_map/ppermute | solution.py:426
  42.5 10.7 %collective-permute-start.19 = (bf16[2,2,16,512]{3,2,1,0:T(8,128)(2,1)S(1)}, bf16[2,2,16,512]{3,2,1,0:T(8,128)(2,1)S(1)}, u32[]{:S(2)}, u32[]{:S(2)}) collective-permute-start(bf16[2,2,16,512]{3,2,1,0:T(8,128)(2,1)S(1)} %get-tuple-element.96), channel_id=1, source_target_pairs={{24,0},{28,4},{25,1},{29,5},{26,2},{30,6},{27,3},{31,7}} | collective-permute-start | bytes 196616 | tf_op jit(solution)/shard_map/ppermute | solution.py:434
  43.8 9.4 %collective-permute-start.18 = (bf16[2,2,16,512]{3,2,1,0:T(8,128)(2,1)S(1)}, bf16[2,2,16,512]{3,2,1,0:T(8,128)(2,1)S(1)}, u32[]{:S(2)}, u32[]{:S(2)}) collective-permute-start(bf16[2,2,16,512]{3,2,1,0:T(8,128)(2,1)S(1)} %get-tuple-element.97), channel_id=1, source_target_pairs={{16,0},{20,4},{24,8},{28,12},{17,1},{21,5},{25,9},{29,13},{18,2},{... | collective-permute-start | bytes 196616 | tf_op jit(solution)/shard_map/ppermute | solution.py:434
  45.1 5.1 %collective-permute-start.16 = (bf16[2,2,2,16,512]{4,3,2,1,0:T(8,128)(2,1)S(1)}, bf16[2,2,2,16,512]{4,3,2,1,0:T(8,128)(2,1)S(1)}, u32[]{:S(2)}, u32[]{:S(2)}) collective-permute-start(bf16[2,2,2,16,512]{4,3,2,1,0:T(8,128)(2,1)S(1)} %get-tuple-element.85), channel_id=1, source_target_pairs={{0,4},{1,5},{2,6},{3,7},{4,0},{5,1},{6,2},{7,3},{8,12},{9,13},{10,... | collective-permute-start | bytes 393224 | tf_op jit(solution)/shard_map/ppermute | solution.py:426
  46.7 4.9 %collective-permute-start.14 = (bf16[512,512]{1,0:T(8,128)(2,1)S(1)}, bf16[512,512]{1,0:T(8,128)(2,1)S(1)}, u32[]{:S(2)}, u32[]{:S(2)}) collective-permute-start(bf16[512,512]{1,0:T(8,128)(2,1)S(1)} %broadcast_add_fusion.gq_ref), channel_id=1, source_target_pairs={{0,1},{1,0},{2,3},{3,2},{4,5},{5,4},{6,7},{7,6},{8,9},{9,8},{10,11... | collective-permute-start | bytes 1572872 | tf_op jit(solution)/shard_map/ppermute | solution.py:426
  46.8 4.8 %collective-permute-start.15 = (bf16[256,512]{1,0:T(8,128)(2,1)S(1)}, bf16[256,512]{1,0:T(8,128)(2,1)S(1)}, u32[]{:S(2)}, u32[]{:S(2)}) collective-permute-start(bf16[256,512]{1,0:T(8,128)(2,1)S(1)} %broadcast_add_fusion.1), channel_id=1, source_target_pairs={{0,1},{1,0},{2,3},{3,2},{4,5},{5,4},{6,7},{7,6},{8,9},{9,8},{10,11... | collective-permute-start | bytes 786440 | tf_op jit(solution)/shard_map/ppermute | solution.py:426
  50.2 6.2 %collective-permute-start.17 = (bf16[2,2,16,512]{3,2,1,0:T(8,128)(2,1)S(1)}, bf16[2,2,16,512]{3,2,1,0:T(8,128)(2,1)S(1)}, u32[]{:S(2)}, u32[]{:S(2)}) collective-permute-start(bf16[2,2,16,512]{3,2,1,0:T(8,128)(2,1)S(1)} %fusion.2), channel_id=1, source_target_pairs={{8,0},{12,4},{16,8},{20,12},{24,16},{28,20},{9,1},{13,5},{17,9},{2... | collective-permute-start | bytes 196616 | tf_op jit(solution)/shard_map/ppermute | solution.py:434
  56.4 1.3 %collective-permute-start.20 = (bf16[2,16,512]{2,1,0:T(8,128)(2,1)S(1)}, bf16[2,16,512]{2,1,0:T(8,128)(2,1)S(1)}, u32[]{:S(2)}, u32[]{:S(2)}) collective-permute-start(bf16[2,16,512]{2,1,0:T(8,128)(2,1)S(1)} %fusion.3), channel_id=1, source_target_pairs={{0,1},{1,0},{2,3},{3,2},{4,5},{5,4},{6,7},{7,6},{8,9},{9,8},{10,11... | collective-permute-start | bytes 98312 | tf_op jit(solution)/shard_map/ppermute | solution.py:426

commit v5 on v4

--- a/solution.py
+++ b/solution.py
@@ -458,7 +458,7 @@
     def far_out(count):
         return pltpu.VMEM((count,) + own_pair.shape, jnp.bfloat16)
 
-    low = (levels + 1) // 2
+    low = 1
     near_pairs = HEADS // CORES * tok_rows * members * near
     far_width = members * seq_count * part_tok
     far_pairs = HEADS // CORES * tok_rows * far_width
@@ -481,12 +481,12 @@
     for group, cross_pair in zip(crossing, cross_pairs):
         (same, other), _ = lax.optimization_barrier((group, near_stat))
         far_parts += [own_pair, same, cross_pair, other]
-    attended, far_gq, level, drift, own_low, own_high, cross_low, cross_high = call(
+    attended, far_gq, level, drift, own_grad, cross_grad = call(
         functools.partial(far_kernel, groups, levels, head_dim, *far_plan),
         [queries, grad_out, near_sum, near_stat] + far_parts,
         [rows_out(jnp.bfloat16)]
         + [rows_out(jnp.float32)] * 3
-        + [far_out(low), far_out(levels - low)] * COLUMNS,
+        + [far_out(levels)] * COLUMNS,
         far_pairs,
         5,
         head_dim,
@@ -495,6 +495,7 @@
     def add(own, cross):
         return (own.astype(jnp.float32) + cross.astype(jnp.float32)).astype(jnp.bfloat16)
 
+    cross_low, cross_high = cross_grad[:low], cross_grad[low:]
     high = hop(cross_high, 1, 0)
     chosen, near_kept, grad_q, sent = call(
         functools.partial(near_backward_kernel, members, head_dim, blocks),
@@ -512,14 +513,14 @@
     )
     att_far = hop(attended, 0, 1)
     high, _, _ = lax.optimization_barrier((high, chosen, att_far))
-    sums = [add(own_high[d - low], high[d - low]) for d in range(low, levels)]
+    sums = [add(own_grad[d], high[d - low]) for d in range(low, levels)]
     cross_low, _ = lax.optimization_barrier((cross_low, sums))
     crossed = hop(cross_low, 1, 0)
     nothing = high[0, 0, 0, 0][None] * 0
     grad_q = grad_q + nothing
     gq_far = hop(grad_q, 0, 1)
     sent_far = hop(sent + nothing, 0, 1)
-    sums = [add(own_low[d], crossed[d]) for d in range(1, low)] + sums
+    sums = [add(own_grad[d], crossed[d]) for d in range(1, low)] + sums
     returned = [sink(part, d) for d, part in enumerate(sums, 1)] + [crossed[0]]
     attended, grad_q, grad_k, grad_v = join(
         [attended, att_far, grad_q, gq_far, near_kept, sent_far],

time: 58.7 us -> 58.4 us (level)
    ppermute x15, waiting for transfers between devices: 10.7 us -> 9.32 us  [hop(): return lax.ppermute(part, ('seq', 'kv'), pairs)]
    ppermute x3, waiting for transfers between devices: 3.24 us -> 4.3 us  [sink(): lax.ppermute(part, 'seq', [(s, s - COLUMNS * d) for s in range(COLUMNS *...]
where the time goes in v5:
time: 58.4 us; the launch traced here: 58.1 us
  starting transfers between devices  28.2 us (48%)
  waiting for transfers between devices  15.5 us (27%)
  Pallas kernels  13.3 us (23%)
  between operations  0.85 us (1%)
    ppermute x15, starting transfers between devices, hop(): return lax.ppermute(part, ('seq', 'kv'), pairs)  15 us
    pallas_call x3, Pallas kernels, call(): pl.pallas_call(kernel, in_specs=in_specs or [WHOLE] * len(operands), out_...  9.81 us
    ppermute x15, waiting for transfers between devices, hop(): return lax.ppermute(part, ('seq', 'kv'), pairs)  9.32 us
    ppermute x3, starting transfers between devices, climb(): lax.ppermute(part, 'seq', [(s, s + COLUMNS * d) for s in range(seq_count...  9.27 us
    ppermute x3, waiting for transfers between devices, sink(): lax.ppermute(part, 'seq', [(s, s - COLUMNS * d) for s in range(COLUMNS *...  4.3 us
    ppermute x3, starting transfers between devices, sink(): lax.ppermute(part, 'seq', [(s, s - COLUMNS * d) for s in range(COLUMNS *...  3.86 us
    ppermute x3, waiting for transfers between devices, climb(): lax.ppermute(part, 'seq', [(s, s + COLUMNS * d) for s in range(seq_count...  1.87 us
    pallas_call x1, Pallas kernels, join(): pl.pallas_call(join_kernel, in_specs=[WHOLE] * len(operands), out_specs=[...  1.56 us
  transfers between devices with their start and end apart: 21, of which 9 were waited for; matrix products, arithmetic and copies ran while one was open for 0% of the time, Pallas kernels for 12%

profile of v5, /device:TPU:0, one launch (start us, length us, event | category | flops | bytes accessed | tf_op | source)
XLA Modules:
  0.0 58.1 jit_solution(18075953511581864775)
XLA Ops:
  0.6 1.2 %shard_map.84 = (bf16[2,8,16,512]{3,2,1,0:T(8,128)(2,1)S(1)}, bf16[2,8,16,512]{3,2,1,0:T(8,128)(2,1)S(1)}, bf16[2,16,512]{2,1,0:T(8,128)(2,1)S(1)}, bf16[2,16,512]{2,1,0:T(8,128)(2,1)S(1)}, f32[8,128]{1,0:T(8,128)S(1)}) custom-call(s32[15,64]{1,0:T(8,128)} %bitcast.38, bf16[8,16,1024]{2,1,0:T(8,128)(2,1)} %keys_hbm.1, bf16[8,16,1024]{2,1,0:T(8,128)(2,1)} %values_hbm.1), custom_call_target="tpu_custom_call" | custom-call | tf_op jit(solution)/shard_map/pallas_call | solution.py:74
  1.9 0.5 collective-permute-start.4
  2.5 2.9 %collective-permute-start.5 = (bf16[2,8,16,512]{3,2,1,0:T(8,128)(2,1)S(1)}, bf16[2,8,16,512]{3,2,1,0:T(8,128)(2,1)S(1)}, u32[]{:S(2)}, u32[]{:S(2)}) collective-permute-start(bf16[2,8,16,512]{3,2,1,0:T(8,128)(2,1)S(1)} %get-tuple-element.52), channel_id=1, source_target_pairs={{0,2},{1,3},{2,0},{3,1},{4,6},{5,7},{6,4},{7,5},{8,10},{9,11},{10,... | collective-permute-start | bytes 786440 | tf_op jit(solution)/shard_map/ppermute | solution.py:426
  5.4 1.0 %collective-permute-start.6 = (bf16[2,8,16,512]{3,2,1,0:T(8,128)(2,1)S(1)}, bf16[2,8,16,512]{3,2,1,0:T(8,128)(2,1)S(1)}, u32[]{:S(2)}, u32[]{:S(2)}) collective-permute-start(bf16[2,8,16,512]{3,2,1,0:T(8,128)(2,1)S(1)} %collective-permute-done.4), channel_id=1, source_target_pairs={{0,2},{1,3},{2,0},{3,1},{4,6},{5,7},{6,4},{7,5},{8,10},{9,11},{10,... | collective-permute-start | bytes 786440 | tf_op jit(solution)/shard_map/ppermute | solution.py:426
  6.4 5.5 %collective-permute-start.3 = (bf16[2,2,16,512]{3,2,1,0:T(8,128)(2,1)S(1)}, bf16[2,2,16,512]{3,2,1,0:T(8,128)(2,1)S(1)}, u32[]{:S(2)}, u32[]{:S(2)}) collective-permute-start(bf16[2,2,16,512]{3,2,1,0:T(8,128)(2,1)S(1)} %pad_maximum_fusion.1.refs_0_.refs_4_), channel_id=1, source_target_pairs={{0,24},{4,28},{1,25},{5,29},{2,26},{6,30},{3,27},{7,31}} | collective-permute-start | bytes 196616 | tf_op jit(solution)/shard_map/ppermute | solution.py:429
  12.0 1.3 %collective-permute-start.2 = (bf16[2,2,16,512]{3,2,1,0:T(8,128)(2,1)S(1)}, bf16[2,2,16,512]{3,2,1,0:T(8,128)(2,1)S(1)}, u32[]{:S(2)}, u32[]{:S(2)}) collective-permute-start(bf16[2,2,16,512]{3,2,1,0:T(8,128)(2,1)S(1)} %pad_maximum_fusion.1.refs_0_.refs_4_), channel_id=1, source_target_pairs={{0,16},{4,20},{8,24},{12,28},{1,17},{5,21},{9,25},{13,29},{2,18},{... | collective-permute-start | bytes 196616 | tf_op jit(solution)/shard_map/ppermute | solution.py:429
  13.3 2.5 %collective-permute-start.1 = (bf16[2,2,16,512]{3,2,1,0:T(8,128)(2,1)S(1)}, bf16[2,2,16,512]{3,2,1,0:T(8,128)(2,1)S(1)}, u32[]{:S(2)}, u32[]{:S(2)}) collective-permute-start(bf16[2,2,16,512]{3,2,1,0:T(8,128)(2,1)S(1)} %pad_maximum_fusion.1.refs_0_.refs_4_), channel_id=1, source_target_pairs={{0,8},{4,12},{8,16},{12,20},{16,24},{20,28},{1,9},{5,13},{9,17},{1... | collective-permute-start | bytes 196616 | tf_op jit(solution)/shard_map/ppermute | solution.py:429
  15.8 1.9 %collective-permute-done.1 = bf16[2,2,16,512]{3,2,1,0:T(8,128)(2,1)S(1)} collective-permute-done((bf16[2,2,16,512]{3,2,1,0:T(8,128)(2,1)S(1)}, bf16[2,2,16,512]{3,2,1,0:T(8,128)(2,1)S(1)}, u32[]{:S(2)}, u32[]{:S(2)}) %collective-permute-start.1) | collective-permute-done | bytes 65568 | tf_op jit(solution)/shard_map/ppermute | solution.py:429
  17.7 2.6 %collective-permute-start.10 = (bf16[3,2,2,16,512]{4,3,2,1,0:T(8,128)(2,1)S(1)}, bf16[3,2,2,16,512]{4,3,2,1,0:T(8,128)(2,1)S(1)}, u32[]{:S(2)}, u32[]{:S(2)}) collective-permute-start(bf16[3,2,2,16,512]{4,3,2,1,0:T(8,128)(2,1)S(1)} %pad_maximum_fusion.refs_1_), channel_id=1, source_target_pairs={{0,6},{1,7},{2,4},{3,5},{4,2},{5,3},{6,0},{7,1},{8,14},{9,15},{10,... | collective-permute-start | bytes 589832 | tf_op jit(solution)/shard_map/ppermute | solution.py:426
  20.2 0.5 collective-permute-start.9
  20.7 0.5 collective-permute-start.7
  21.2 2.5 %collective-permute-start.11 = (bf16[2,2,16,512]{3,2,1,0:T(8,128)(2,1)S(1)}, bf16[2,2,16,512]{3,2,1,0:T(8,128)(2,1)S(1)}, u32[]{:S(2)}, u32[]{:S(2)}) collective-permute-start(bf16[2,2,16,512]{3,2,1,0:T(8,128)(2,1)S(1)} %pad_maximum_fusion.1.refs_0_.refs_4_), channel_id=1, source_target_pairs={{0,6},{1,7},{2,4},{3,5},{4,2},{5,3},{6,0},{7,1},{8,14},{9,15},{10,... | collective-permute-start | bytes 196616 | tf_op jit(solution)/shard_map/ppermute | solution.py:426
  23.7 0.5 collective-permute-start.8
  24.3 2.7 %shard_map.85 = (f32[512,512]{1,0:T(8,128)S(1)}, f32[512,512]{1,0:T(8,128)S(1)}, f32[512,512]{1,0:T(8,128)S(1)}, bf16[512,512]{1,0:T(8,128)(2,1)S(1)}, bf16[512,512]{1,0:T(8,128)(2,1)S(1)}) custom-call(bf16[512,1024]{1,0:T(8,128)(2,1)} %q_hbm.1, bf16[512,1024]{1,0:T(8,128)(2,1)} %g_hbm.1, bf16[2,128,512]{2,1,0:T(8,128)(2,1)S(1)} %bitcast.24, ...), custom_call_target="tpu_custom_call" | custom-call | flops 1073741824 | bytes 3145728 | tf_op jit(solution)/shard_map/pallas_call | solution.py:395
  27.0 2.7 %collective-permute-done.9.refs_5_ = bf16[3,2,2,16,512]{4,3,2,1,0:T(8,128)(2,1)S(1)} collective-permute-done((bf16[3,2,2,16,512]{4,3,2,1,0:T(8,128)(2,1)S(1)}, bf16[3,2,2,16,512]{4,3,2,1,0:T(8,128)(2,1)S(1)}, u32[]{:S(2)}, u32[]{:S(2)}) %collective-permute-start.9) | collective-permute-done | bytes 196640 | tf_op jit(solution)/shard_map/ppermute | solution.py:426
  29.7 0.7 %collective-permute-done.7.refs_3_ = bf16[3,2,2,16,512]{4,3,2,1,0:T(8,128)(2,1)S(1)} collective-permute-done((bf16[3,2,2,16,512]{4,3,2,1,0:T(8,128)(2,1)S(1)}, bf16[3,2,2,16,512]{4,3,2,1,0:T(8,128)(2,1)S(1)}, u32[]{:S(2)}, u32[]{:S(2)}) %collective-permute-start.7) | collective-permute-done | bytes 196640 | tf_op jit(solution)/shard_map/ppermute | solution.py:426
  30.5 0.7 %collective-permute-done.11.refs_6_ = bf16[2,2,16,512]{3,2,1,0:T(8,128)(2,1)S(1)} collective-permute-done((bf16[2,2,16,512]{3,2,1,0:T(8,128)(2,1)S(1)}, bf16[2,2,16,512]{3,2,1,0:T(8,128)(2,1)S(1)}, u32[]{:S(2)}, u32[]{:S(2)}) %collective-permute-start.11) | collective-permute-done | bytes 65568 | tf_op jit(solution)/shard_map/ppermute | solution.py:426
  31.2 0.7 %collective-permute-done.8.refs_2_ = bf16[2,2,16,512]{3,2,1,0:T(8,128)(2,1)S(1)} collective-permute-done((bf16[2,2,16,512]{3,2,1,0:T(8,128)(2,1)S(1)}, bf16[2,2,16,512]{3,2,1,0:T(8,128)(2,1)S(1)}, u32[]{:S(2)}, u32[]{:S(2)}) %collective-permute-start.8) | collective-permute-done | bytes 65568 | tf_op jit(solution)/shard_map/ppermute | solution.py:426
  31.9 4.5 %shard_map.86 = (bf16[512,512]{1,0:T(8,128)(2,1)S(1)}, f32[512,512]{1,0:T(8,128)S(1)}, f32[512,512]{1,0:T(8,128)S(1)}, f32[512,512]{1,0:T(8,128)S(1)}, bf16[4,2,...) custom-call(bf16[512,512]{1,0:T(8,128)(2,1)S(1)} %get-tuple-element.56.q_ref, ...), custom_call_target="tpu_custom_call" | custom-call | flops 2684354560 | bytes 4194304 | tf_op jit(solution)/shard_map/pallas_call | solution.py:395
  36.5 1.6 %collective-permute-start.13 = (bf16[3,2,2,16,512]{4,3,2,1,0:T(8,128)(2,1)S(1)}, bf16[3,2,2,16,512]{4,3,2,1,0:T(8,128)(2,1)S(1)}, u32[]{:S(2)}, u32[]{:S(2)}) collective-permute-start(bf16[3,2,2,16,512]{4,3,2,1,0:T(8,128)(2,1)S(1)} %slice.42), channel_id=1, source_target_pairs={{0,4},{1,5},{2,6},{3,7},{4,0},{5,1},{6,2},{7,3},{8,12},{9,13},{10,... | collective-permute-start | bytes 589832 | tf_op jit(solution)/shard_map/ppermute | solution.py:426
  38.1 2.5 %shard_map.87 = (f32[2,2,16,512]{3,2,1,0:T(8,128)S(1)}, bf16[256,512]{1,0:T(8,128)(2,1)S(1)}, bf16[512,512]{1,0:T(8,128)(2,1)S(1)}, bf16[256,512]{1,0:T(8,128)(2,1)S(1)}) custom-call(f32[8,128]{1,0:T(8,128)S(1)} %get-tuple-element.67.block_ref, f32[512,512]{1,0:T(8,128)S(1)} %get-tuple-element.68.bias_ref, bf16[512,512]{1,0:T(8,128)(2,1)S(1)} %get-tuple-element.56.q_ref, ...), custom_call_target="tpu_custom_call" | custom-call | flops 2147483648 | bytes 6295552 | tf_op jit(solution)/shard_map/pallas_call | solution.py:395
  40.6 3.3 %collective-permute-done.13 = bf16[3,2,2,16,512]{4,3,2,1,0:T(8,128)(2,1)S(1)} collective-permute-done((bf16[3,2,2,16,512]{4,3,2,1,0:T(8,128)(2,1)S(1)}, bf16[3,2,2,16,512]{4,3,2,1,0:T(8,128)(2,1)S(1)}, u32[]{:S(2)}, u32[]{:S(2)}) %collective-permute-start.13) | collective-permute-done | bytes 196640 | tf_op jit(solution)/shard_map/ppermute | solution.py:426
  44.1 0.6 collective-permute-start.15
  44.7 1.3 %collective-permute-start.18 = (bf16[2,2,16,512]{3,2,1,0:T(8,128)(2,1)S(1)}, bf16[2,2,16,512]{3,2,1,0:T(8,128)(2,1)S(1)}, u32[]{:S(2)}, u32[]{:S(2)}) collective-permute-start(bf16[2,2,16,512]{3,2,1,0:T(8,128)(2,1)S(1)} %get-tuple-element.92), channel_id=1, source_target_pairs={{24,0},{28,4},{25,1},{29,5},{26,2},{30,6},{27,3},{31,7}} | collective-permute-start | bytes 196616 | tf_op jit(solution)/shard_map/ppermute | solution.py:434
  46.0 1.6 %collective-permute-start.19 = (bf16[1,2,2,16,512]{4,3,2,1,0:T(8,128)(2,1)S(1)}, bf16[1,2,2,16,512]{4,3,2,1,0:T(8,128)(2,1)S(1)}, u32[]{:S(2)}, u32[]{:S(2)}) collective-permute-start(bf16[1,2,2,16,512]{4,3,2,1,0:T(8,128)(2,1)S(1)} %slice.51), channel_id=1, source_target_pairs={{0,4},{1,5},{2,6},{3,7},{4,0},{5,1},{6,2},{7,3},{8,12},{9,13},{10,... | collective-permute-start | bytes 196616 | tf_op jit(solution)/shard_map/ppermute | solution.py:426
  47.5 1.3 %collective-permute-start.17 = (bf16[2,2,16,512]{3,2,1,0:T(8,128)(2,1)S(1)}, bf16[2,2,16,512]{3,2,1,0:T(8,128)(2,1)S(1)}, u32[]{:S(2)}, u32[]{:S(2)}) collective-permute-start(bf16[2,2,16,512]{3,2,1,0:T(8,128)(2,1)S(1)} %get-tuple-element.93), channel_id=1, source_target_pairs={{16,0},{20,4},{24,8},{28,12},{17,1},{21,5},{25,9},{29,13},{18,2},{... | collective-permute-start | bytes 196616 | tf_op jit(solution)/shard_map/ppermute | solution.py:434
  48.8 1.3 %collective-permute-start.16 = (bf16[2,2,16,512]{3,2,1,0:T(8,128)(2,1)S(1)}, bf16[2,2,16,512]{3,2,1,0:T(8,128)(2,1)S(1)}, u32[]{:S(2)}, u32[]{:S(2)}) collective-permute-start(bf16[2,2,16,512]{3,2,1,0:T(8,128)(2,1)S(1)} %get-tuple-element.94), channel_id=1, source_target_pairs={{8,0},{12,4},{16,8},{20,12},{24,16},{28,20},{9,1},{13,5},{17,9},{2... | collective-permute-start | bytes 196616 | tf_op jit(solution)/shard_map/ppermute | solution.py:434
  50.1 1.6 %shard_map.88 = (bf16[512,1024]{1,0:T(8,128)(2,1)}, bf16[512,1024]{1,0:T(8,128)(2,1)}, bf16[128,1024]{1,0:T(8,128)(2,1)}, bf16[128,1024]{1,0:T(8,128)(2,1)}) custom-call(bf16[512,512]{1,0:T(8,128)(2,1)S(1)} %get-tuple-element.66.att_ref, bf16[512,512]{1,0:T(8,128)(2,1)S(1)} %collective-permute-done.12.att_far, ...), custom_call_target="tpu_custom_call" | custom-call | tf_op jit(solution)/shard_map/pallas_call | solution.py:107
  51.7 0.9 %collective-permute-done.18.refs_2_ = bf16[2,2,16,512]{3,2,1,0:T(8,128)(2,1)S(1)} collective-permute-done((bf16[2,2,16,512]{3,2,1,0:T(8,128)(2,1)S(1)}, bf16[2,2,16,512]{3,2,1,0:T(8,128)(2,1)S(1)}, u32[]{:S(2)}, u32[]{:S(2)}) %collective-permute-start.18) | collective-permute-done | bytes 65568 | tf_op jit(solution)/shard_map/ppermute | solution.py:434
  52.6 3.4 %collective-permute-done.17.refs_1_ = bf16[2,2,16,512]{3,2,1,0:T(8,128)(2,1)S(1)} collective-permute-done((bf16[2,2,16,512]{3,2,1,0:T(8,128)(2,1)S(1)}, bf16[2,2,16,512]{3,2,1,0:T(8,128)(2,1)S(1)}, u32[]{:S(2)}, u32[]{:S(2)}) %collective-permute-start.17) | collective-permute-done | bytes 65568 | tf_op jit(solution)/shard_map/ppermute | solution.py:434
  56.1 1.2 %collective-permute-done.20.far_ref = bf16[2,16,512]{2,1,0:T(8,128)(2,1)S(1)} collective-permute-done((bf16[2,16,512]{2,1,0:T(8,128)(2,1)S(1)}, bf16[2,16,512]{2,1,0:T(8,128)(2,1)S(1)}, u32[]{:S(2)}, u32[]{:S(2)}) %collective-permute-start.20) | collective-permute-done | bytes 32800 | tf_op jit(solution)/shard_map/ppermute | solution.py:426
  57.3 0.8 %shard_map.89 = (bf16[128,1024]{1,0:T(8,128)(2,1)}, bf16[128,1024]{1,0:T(8,128)(2,1)}) custom-call(f32[8,128]{1,0:T(8,128)S(1)} %get-tuple-element.67.block_ref, f32[2,2,16,512]{3,2,1,0:T(8,128)S(1)} %get-tuple-element.74.chosen_ref, bf16[2,16,512]{2,1,0:T(8,128)(2,1)S(1)} %collective-permute-done.20.far_ref, ...), custom_call_target="tpu_custom_call", output_to_operand_aliasing={{0}: (7, {}), {1}: (8, {})} | custom-call | tf_op jit(solution)/shard_map/pallas_call | solution.py:142
  (25 shorter events, 0.5 us)
Async XLA Ops:
  1.9 3.5 %collective-permute-start.4 = (bf16[2,8,16,512]{3,2,1,0:T(8,128)(2,1)S(1)}, bf16[2,8,16,512]{3,2,1,0:T(8,128)(2,1)S(1)}, u32[]{:S(2)}, u32[]{:S(2)}) collective-permute-start(bf16[2,8,16,512]{3,2,1,0:T(8,128)(2,1)S(1)} %get-tuple-element.51), channel_id=1, source_target_pairs={{0,1},{1,0},{2,3},{3,2},{4,5},{5,4},{6,7},{7,6},{8,9},{9,8},{10,11... | collective-permute-start | bytes 786440 | tf_op jit(solution)/shard_map/ppermute | solution.py:426
  2.4 4.1 %collective-permute-start = (bf16[2,16,512]{2,1,0:T(8,128)(2,1)S(1)}, bf16[2,16,512]{2,1,0:T(8,128)(2,1)S(1)}, u32[]{:S(2)}, u32[]{:S(2)}) collective-permute-start(bf16[2,16,512]{2,1,0:T(8,128)(2,1)S(1)} %get-tuple-element.49), channel_id=1, source_target_pairs={{0,1},{1,0},{2,3},{3,2},{4,5},{5,4},{6,7},{7,6},{8,9},{9,8},{10,11... | collective-permute-start | bytes 98312 | tf_op jit(solution)/shard_map/ppermute | solution.py:426
  2.5 15.2 %collective-permute-start.5 = (bf16[2,8,16,512]{3,2,1,0:T(8,128)(2,1)S(1)}, bf16[2,8,16,512]{3,2,1,0:T(8,128)(2,1)S(1)}, u32[]{:S(2)}, u32[]{:S(2)}) collective-permute-start(bf16[2,8,16,512]{3,2,1,0:T(8,128)(2,1)S(1)} %get-tuple-element.52), channel_id=1, source_target_pairs={{0,2},{1,3},{2,0},{3,1},{4,6},{5,7},{6,4},{7,5},{8,10},{9,11},{10,... | collective-permute-start | bytes 786440 | tf_op jit(solution)/shard_map/ppermute | solution.py:426
  5.4 12.3 %collective-permute-start.6 = (bf16[2,8,16,512]{3,2,1,0:T(8,128)(2,1)S(1)}, bf16[2,8,16,512]{3,2,1,0:T(8,128)(2,1)S(1)}, u32[]{:S(2)}, u32[]{:S(2)}) collective-permute-start(bf16[2,8,16,512]{3,2,1,0:T(8,128)(2,1)S(1)} %collective-permute-done.4), channel_id=1, source_target_pairs={{0,2},{1,3},{2,0},{3,1},{4,6},{5,7},{6,4},{7,5},{8,10},{9,11},{10,... | collective-permute-start | bytes 786440 | tf_op jit(solution)/shard_map/ppermute | solution.py:426
  6.4 9.3 %collective-permute-start.3 = (bf16[2,2,16,512]{3,2,1,0:T(8,128)(2,1)S(1)}, bf16[2,2,16,512]{3,2,1,0:T(8,128)(2,1)S(1)}, u32[]{:S(2)}, u32[]{:S(2)}) collective-permute-start(bf16[2,2,16,512]{3,2,1,0:T(8,128)(2,1)S(1)} %pad_maximum_fusion.1.refs_0_.refs_4_), channel_id=1, source_target_pairs={{0,24},{4,28},{1,25},{5,29},{2,26},{6,30},{3,27},{7,31}} | collective-permute-start | bytes 196616 | tf_op jit(solution)/shard_map/ppermute | solution.py:429
  12.0 3.8 %collective-permute-start.2 = (bf16[2,2,16,512]{3,2,1,0:T(8,128)(2,1)S(1)}, bf16[2,2,16,512]{3,2,1,0:T(8,128)(2,1)S(1)}, u32[]{:S(2)}, u32[]{:S(2)}) collective-permute-start(bf16[2,2,16,512]{3,2,1,0:T(8,128)(2,1)S(1)} %pad_maximum_fusion.1.refs_0_.refs_4_), channel_id=1, source_target_pairs={{0,16},{4,20},{8,24},{12,28},{1,17},{5,21},{9,25},{13,29},{2,18},{... | collective-permute-start | bytes 196616 | tf_op jit(solution)/shard_map/ppermute | solution.py:429
  13.3 4.4 %collective-permute-start.1 = (bf16[2,2,16,512]{3,2,1,0:T(8,128)(2,1)S(1)}, bf16[2,2,16,512]{3,2,1,0:T(8,128)(2,1)S(1)}, u32[]{:S(2)}, u32[]{:S(2)}) collective-permute-start(bf16[2,2,16,512]{3,2,1,0:T(8,128)(2,1)S(1)} %pad_maximum_fusion.1.refs_0_.refs_4_), channel_id=1, source_target_pairs={{0,8},{4,12},{8,16},{12,20},{16,24},{20,28},{1,9},{5,13},{9,17},{1... | collective-permute-start | bytes 196616 | tf_op jit(solution)/shard_map/ppermute | solution.py:429
  17.7 9.3 %collective-permute-start.10 = (bf16[3,2,2,16,512]{4,3,2,1,0:T(8,128)(2,1)S(1)}, bf16[3,2,2,16,512]{4,3,2,1,0:T(8,128)(2,1)S(1)}, u32[]{:S(2)}, u32[]{:S(2)}) collective-permute-start(bf16[3,2,2,16,512]{4,3,2,1,0:T(8,128)(2,1)S(1)} %pad_maximum_fusion.refs_1_), channel_id=1, source_target_pairs={{0,6},{1,7},{2,4},{3,5},{4,2},{5,3},{6,0},{7,1},{8,14},{9,15},{10,... | collective-permute-start | bytes 589832 | tf_op jit(solution)/shard_map/ppermute | solution.py:426
  20.2 9.5 %collective-permute-start.9 = (bf16[3,2,2,16,512]{4,3,2,1,0:T(8,128)(2,1)S(1)}, bf16[3,2,2,16,512]{4,3,2,1,0:T(8,128)(2,1)S(1)}, u32[]{:S(2)}, u32[]{:S(2)}) collective-permute-start(bf16[3,2,2,16,512]{4,3,2,1,0:T(8,128)(2,1)S(1)} %pad_maximum_fusion.refs_1_), channel_id=1, source_target_pairs={{0,2},{1,3},{2,0},{3,1},{4,6},{5,7},{6,4},{7,5},{8,10},{9,11},{10,... | collective-permute-start | bytes 589832 | tf_op jit(solution)/shard_map/ppermute | solution.py:426
  20.7 9.7 %collective-permute-start.7 = (bf16[3,2,2,16,512]{4,3,2,1,0:T(8,128)(2,1)S(1)}, bf16[3,2,2,16,512]{4,3,2,1,0:T(8,128)(2,1)S(1)}, u32[]{:S(2)}, u32[]{:S(2)}) collective-permute-start(bf16[3,2,2,16,512]{4,3,2,1,0:T(8,128)(2,1)S(1)} %pad_maximum_fusion.refs_1_), channel_id=1, source_target_pairs={{0,4},{1,5},{2,6},{3,7},{4,0},{5,1},{6,2},{7,3},{8,12},{9,13},{10,... | collective-permute-start | bytes 589832 | tf_op jit(solution)/shard_map/ppermute | solution.py:426
  21.2 9.9 %collective-permute-start.11 = (bf16[2,2,16,512]{3,2,1,0:T(8,128)(2,1)S(1)}, bf16[2,2,16,512]{3,2,1,0:T(8,128)(2,1)S(1)}, u32[]{:S(2)}, u32[]{:S(2)}) collective-permute-start(bf16[2,2,16,512]{3,2,1,0:T(8,128)(2,1)S(1)} %pad_maximum_fusion.1.refs_0_.refs_4_), channel_id=1, source_target_pairs={{0,6},{1,7},{2,4},{3,5},{4,2},{5,3},{6,0},{7,1},{8,14},{9,15},{10,... | collective-permute-start | bytes 196616 | tf_op jit(solution)/shard_map/ppermute | solution.py:426
  23.7 8.1 %collective-permute-start.8 = (bf16[2,2,16,512]{3,2,1,0:T(8,128)(2,1)S(1)}, bf16[2,2,16,512]{3,2,1,0:T(8,128)(2,1)S(1)}, u32[]{:S(2)}, u32[]{:S(2)}) collective-permute-start(bf16[2,2,16,512]{3,2,1,0:T(8,128)(2,1)S(1)} %pad_maximum_fusion.1.refs_0_.refs_4_), channel_id=1, source_target_pairs={{0,4},{1,5},{2,6},{3,7},{4,0},{5,1},{6,2},{7,3},{8,12},{9,13},{10,... | collective-permute-start | bytes 196616 | tf_op jit(solution)/shard_map/ppermute | solution.py:426
  36.4 7.5 %collective-permute-start.12 = (bf16[512,512]{1,0:T(8,128)(2,1)S(1)}, bf16[512,512]{1,0:T(8,128)(2,1)S(1)}, u32[]{:S(2)}, u32[]{:S(2)}) collective-permute-start(bf16[512,512]{1,0:T(8,128)(2,1)S(1)} %get-tuple-element.66.att_ref), channel_id=1, source_target_pairs={{0,1},{1,0},{2,3},{3,2},{4,5},{5,4},{6,7},{7,6},{8,9},{9,8},{10,11... | collective-permute-start | bytes 1572872 | tf_op jit(solution)/shard_map/ppermute | solution.py:426
  36.5 7.4 %collective-permute-start.13 = (bf16[3,2,2,16,512]{4,3,2,1,0:T(8,128)(2,1)S(1)}, bf16[3,2,2,16,512]{4,3,2,1,0:T(8,128)(2,1)S(1)}, u32[]{:S(2)}, u32[]{:S(2)}) collective-permute-start(bf16[3,2,2,16,512]{4,3,2,1,0:T(8,128)(2,1)S(1)} %slice.42), channel_id=1, source_target_pairs={{0,4},{1,5},{2,6},{3,7},{4,0},{5,1},{6,2},{7,3},{8,12},{9,13},{10,... | collective-permute-start | bytes 589832 | tf_op jit(solution)/shard_map/ppermute | solution.py:426
  43.9 6.2 %collective-permute-start.14 = (bf16[512,512]{1,0:T(8,128)(2,1)S(1)}, bf16[512,512]{1,0:T(8,128)(2,1)S(1)}, u32[]{:S(2)}, u32[]{:S(2)}) collective-permute-start(bf16[512,512]{1,0:T(8,128)(2,1)S(1)} %broadcast_add_fusion.gq_ref), channel_id=1, source_target_pairs={{0,1},{1,0},{2,3},{3,2},{4,5},{5,4},{6,7},{7,6},{8,9},{9,8},{10,11... | collective-permute-start | bytes 1572872 | tf_op jit(solution)/shard_map/ppermute | solution.py:426
  44.1 4.8 %collective-permute-start.15 = (bf16[256,512]{1,0:T(8,128)(2,1)S(1)}, bf16[256,512]{1,0:T(8,128)(2,1)S(1)}, u32[]{:S(2)}, u32[]{:S(2)}) collective-permute-start(bf16[256,512]{1,0:T(8,128)(2,1)S(1)} %broadcast_add_fusion.1), channel_id=1, source_target_pairs={{0,1},{1,0},{2,3},{3,2},{4,5},{5,4},{6,7},{7,6},{8,9},{9,8},{10,11... | collective-permute-start | bytes 786440 | tf_op jit(solution)/shard_map/ppermute | solution.py:426
  44.7 8.0 %collective-permute-start.18 = (bf16[2,2,16,512]{3,2,1,0:T(8,128)(2,1)S(1)}, bf16[2,2,16,512]{3,2,1,0:T(8,128)(2,1)S(1)}, u32[]{:S(2)}, u32[]{:S(2)}) collective-permute-start(bf16[2,2,16,512]{3,2,1,0:T(8,128)(2,1)S(1)} %get-tuple-element.92), channel_id=1, source_target_pairs={{24,0},{28,4},{25,1},{29,5},{26,2},{30,6},{27,3},{31,7}} | collective-permute-start | bytes 196616 | tf_op jit(solution)/shard_map/ppermute | solution.py:434
  46.0 5.7 %collective-permute-start.19 = (bf16[1,2,2,16,512]{4,3,2,1,0:T(8,128)(2,1)S(1)}, bf16[1,2,2,16,512]{4,3,2,1,0:T(8,128)(2,1)S(1)}, u32[]{:S(2)}, u32[]{:S(2)}) collective-permute-start(bf16[1,2,2,16,512]{4,3,2,1,0:T(8,128)(2,1)S(1)} %slice.51), channel_id=1, source_target_pairs={{0,4},{1,5},{2,6},{3,7},{4,0},{5,1},{6,2},{7,3},{8,12},{9,13},{10,... | collective-permute-start | bytes 196616 | tf_op jit(solution)/shard_map/ppermute | solution.py:426
  47.5 8.5 %collective-permute-start.17 = (bf16[2,2,16,512]{3,2,1,0:T(8,128)(2,1)S(1)}, bf16[2,2,16,512]{3,2,1,0:T(8,128)(2,1)S(1)}, u32[]{:S(2)}, u32[]{:S(2)}) collective-permute-start(bf16[2,2,16,512]{3,2,1,0:T(8,128)(2,1)S(1)} %get-tuple-element.93), channel_id=1, source_target_pairs={{16,0},{20,4},{24,8},{28,12},{17,1},{21,5},{25,9},{29,13},{18,2},{... | collective-permute-start | bytes 196616 | tf_op jit(solution)/shard_map/ppermute | solution.py:434
  48.8 7.2 %collective-permute-start.16 = (bf16[2,2,16,512]{3,2,1,0:T(8,128)(2,1)S(1)}, bf16[2,2,16,512]{3,2,1,0:T(8,128)(2,1)S(1)}, u32[]{:S(2)}, u32[]{:S(2)}) collective-permute-start(bf16[2,2,16,512]{3,2,1,0:T(8,128)(2,1)S(1)} %get-tuple-element.94), channel_id=1, source_target_pairs={{8,0},{12,4},{16,8},{20,12},{24,16},{28,20},{9,1},{13,5},{17,9},{2... | collective-permute-start | bytes 196616 | tf_op jit(solution)/shard_map/ppermute | solution.py:434
  56.1 1.3 %collective-permute-start.20 = (bf16[2,16,512]{2,1,0:T(8,128)(2,1)S(1)}, bf16[2,16,512]{2,1,0:T(8,128)(2,1)S(1)}, u32[]{:S(2)}, u32[]{:S(2)}) collective-permute-start(bf16[2,16,512]{2,1,0:T(8,128)(2,1)S(1)} %fusion.3), channel_id=1, source_target_pairs={{0,1},{1,0},{2,3},{3,2},{4,5},{5,4},{6,7},{7,6},{8,9},{9,8},{10,11... | collective-permute-start | bytes 98312 | tf_op jit(solution)/shard_map/ppermute | solution.py:426

commit v6 on v5

--- a/solution.py
+++ b/solution.py
@@ -514,12 +514,12 @@
     att_far = hop(attended, 0, 1)
     high, _, _ = lax.optimization_barrier((high, chosen, att_far))
     sums = [add(own_grad[d], high[d - low]) for d in range(low, levels)]
-    cross_low, _ = lax.optimization_barrier((cross_low, sums))
-    crossed = hop(cross_low, 1, 0)
     nothing = high[0, 0, 0, 0][None] * 0
     grad_q = grad_q + nothing
     gq_far = hop(grad_q, 0, 1)
     sent_far = hop(sent + nothing, 0, 1)
+    cross_low, _ = lax.optimization_barrier((cross_low, sent_far))
+    crossed = hop(cross_low, 1, 0)
     sums = [add(own_grad[d], crossed[d]) for d in range(1, low)] + sums
     returned = [sink(part, d) for d, part in enumerate(sums, 1)] + [crossed[0]]
     attended, grad_q, grad_k, grad_v = join(

time: 58.4 us -> 57.8 us (0.990)
  waiting for transfers between devices: 15.5 us -> 14.9 us
where the time goes in v6:
time: 57.8 us; the launch traced here: 57.5 us
  starting transfers between devices  28.2 us (49%)
  waiting for transfers between devices  14.9 us (26%)
  Pallas kernels  13.3 us (23%)
  between operations  0.84 us (1%)
    ppermute x15, starting transfers between devices, hop(): return lax.ppermute(part, ('seq', 'kv'), pairs)  15 us
    pallas_call x3, Pallas kernels, call(): pl.pallas_call(kernel, in_specs=in_specs or [WHOLE] * len(operands), out_...  9.81 us
    ppermute x15, waiting for transfers between devices, hop(): return lax.ppermute(part, ('seq', 'kv'), pairs)  9.32 us
    ppermute x3, starting transfers between devices, climb(): lax.ppermute(part, 'seq', [(s, s + COLUMNS * d) for s in range(seq_count...  9.27 us
    ppermute x3, starting transfers between devices, sink(): lax.ppermute(part, 'seq', [(s, s - COLUMNS * d) for s in range(COLUMNS *...  3.88 us
    ppermute x3, waiting for transfers between devices, sink(): lax.ppermute(part, 'seq', [(s, s - COLUMNS * d) for s in range(COLUMNS *...  3.74 us
    ppermute x3, waiting for transfers between devices, climb(): lax.ppermute(part, 'seq', [(s, s + COLUMNS * d) for s in range(seq_count...  1.87 us
    pallas_call x1, Pallas kernels, join(): pl.pallas_call(join_kernel, in_specs=[WHOLE] * len(operands), out_specs=[...  1.54 us
  transfers between devices with their start and end apart: 21, of which 9 were waited for; matrix products, arithmetic and copies ran while one was open for 0% of the time, Pallas kernels for 12%

profile of v6, /device:TPU:0, one launch (start us, length us, event | category | flops | bytes accessed | tf_op | source)
XLA Modules:
  0.0 57.5 jit_solution(17062923093785729185)
XLA Ops:
  0.6 1.2 %shard_map.84 = (bf16[2,8,16,512]{3,2,1,0:T(8,128)(2,1)S(1)}, bf16[2,8,16,512]{3,2,1,0:T(8,128)(2,1)S(1)}, bf16[2,16,512]{2,1,0:T(8,128)(2,1)S(1)}, bf16[2,16,512]{2,1,0:T(8,128)(2,1)S(1)}, f32[8,128]{1,0:T(8,128)S(1)}) custom-call(s32[15,64]{1,0:T(8,128)} %bitcast.38, bf16[8,16,1024]{2,1,0:T(8,128)(2,1)} %keys_hbm.1, bf16[8,16,1024]{2,1,0:T(8,128)(2,1)} %values_hbm.1), custom_call_target="tpu_custom_call" | custom-call | tf_op jit(solution)/shard_map/pallas_call | solution.py:74
  1.9 0.5 collective-permute-start.4
  2.5 2.9 %collective-permute-start.5 = (bf16[2,8,16,512]{3,2,1,0:T(8,128)(2,1)S(1)}, bf16[2,8,16,512]{3,2,1,0:T(8,128)(2,1)S(1)}, u32[]{:S(2)}, u32[]{:S(2)}) collective-permute-start(bf16[2,8,16,512]{3,2,1,0:T(8,128)(2,1)S(1)} %get-tuple-element.52), channel_id=1, source_target_pairs={{0,2},{1,3},{2,0},{3,1},{4,6},{5,7},{6,4},{7,5},{8,10},{9,11},{10,... | collective-permute-start | bytes 786440 | tf_op jit(solution)/shard_map/ppermute | solution.py:426
  5.4 1.0 %collective-permute-start.6 = (bf16[2,8,16,512]{3,2,1,0:T(8,128)(2,1)S(1)}, bf16[2,8,16,512]{3,2,1,0:T(8,128)(2,1)S(1)}, u32[]{:S(2)}, u32[]{:S(2)}) collective-permute-start(bf16[2,8,16,512]{3,2,1,0:T(8,128)(2,1)S(1)} %collective-permute-done.4), channel_id=1, source_target_pairs={{0,2},{1,3},{2,0},{3,1},{4,6},{5,7},{6,4},{7,5},{8,10},{9,11},{10,... | collective-permute-start | bytes 786440 | tf_op jit(solution)/shard_map/ppermute | solution.py:426
  6.4 5.5 %collective-permute-start.3 = (bf16[2,2,16,512]{3,2,1,0:T(8,128)(2,1)S(1)}, bf16[2,2,16,512]{3,2,1,0:T(8,128)(2,1)S(1)}, u32[]{:S(2)}, u32[]{:S(2)}) collective-permute-start(bf16[2,2,16,512]{3,2,1,0:T(8,128)(2,1)S(1)} %pad_maximum_fusion.1.refs_0_.refs_4_), channel_id=1, source_target_pairs={{0,24},{4,28},{1,25},{5,29},{2,26},{6,30},{3,27},{7,31}} | collective-permute-start | bytes 196616 | tf_op jit(solution)/shard_map/ppermute | solution.py:429
  12.0 1.3 %collective-permute-start.2 = (bf16[2,2,16,512]{3,2,1,0:T(8,128)(2,1)S(1)}, bf16[2,2,16,512]{3,2,1,0:T(8,128)(2,1)S(1)}, u32[]{:S(2)}, u32[]{:S(2)}) collective-permute-start(bf16[2,2,16,512]{3,2,1,0:T(8,128)(2,1)S(1)} %pad_maximum_fusion.1.refs_0_.refs_4_), channel_id=1, source_target_pairs={{0,16},{4,20},{8,24},{12,28},{1,17},{5,21},{9,25},{13,29},{2,18},{... | collective-permute-start | bytes 196616 | tf_op jit(solution)/shard_map/ppermute | solution.py:429
  13.3 2.5 %collective-permute-start.1 = (bf16[2,2,16,512]{3,2,1,0:T(8,128)(2,1)S(1)}, bf16[2,2,16,512]{3,2,1,0:T(8,128)(2,1)S(1)}, u32[]{:S(2)}, u32[]{:S(2)}) collective-permute-start(bf16[2,2,16,512]{3,2,1,0:T(8,128)(2,1)S(1)} %pad_maximum_fusion.1.refs_0_.refs_4_), channel_id=1, source_target_pairs={{0,8},{4,12},{8,16},{12,20},{16,24},{20,28},{1,9},{5,13},{9,17},{1... | collective-permute-start | bytes 196616 | tf_op jit(solution)/shard_map/ppermute | solution.py:429
  15.8 1.9 %collective-permute-done.1 = bf16[2,2,16,512]{3,2,1,0:T(8,128)(2,1)S(1)} collective-permute-done((bf16[2,2,16,512]{3,2,1,0:T(8,128)(2,1)S(1)}, bf16[2,2,16,512]{3,2,1,0:T(8,128)(2,1)S(1)}, u32[]{:S(2)}, u32[]{:S(2)}) %collective-permute-start.1) | collective-permute-done | bytes 65568 | tf_op jit(solution)/shard_map/ppermute | solution.py:429
  17.7 2.6 %collective-permute-start.10 = (bf16[3,2,2,16,512]{4,3,2,1,0:T(8,128)(2,1)S(1)}, bf16[3,2,2,16,512]{4,3,2,1,0:T(8,128)(2,1)S(1)}, u32[]{:S(2)}, u32[]{:S(2)}) collective-permute-start(bf16[3,2,2,16,512]{4,3,2,1,0:T(8,128)(2,1)S(1)} %pad_maximum_fusion.refs_1_), channel_id=1, source_target_pairs={{0,6},{1,7},{2,4},{3,5},{4,2},{5,3},{6,0},{7,1},{8,14},{9,15},{10,... | collective-permute-start | bytes 589832 | tf_op jit(solution)/shard_map/ppermute | solution.py:426
  20.2 0.5 collective-permute-start.9
  20.7 0.5 collective-permute-start.7
  21.2 2.5 %collective-permute-start.11 = (bf16[2,2,16,512]{3,2,1,0:T(8,128)(2,1)S(1)}, bf16[2,2,16,512]{3,2,1,0:T(8,128)(2,1)S(1)}, u32[]{:S(2)}, u32[]{:S(2)}) collective-permute-start(bf16[2,2,16,512]{3,2,1,0:T(8,128)(2,1)S(1)} %pad_maximum_fusion.1.refs_0_.refs_4_), channel_id=1, source_target_pairs={{0,6},{1,7},{2,4},{3,5},{4,2},{5,3},{6,0},{7,1},{8,14},{9,15},{10,... | collective-permute-start | bytes 196616 | tf_op jit(solution)/shard_map/ppermute | solution.py:426
  23.7 0.5 collective-permute-start.8
  24.3 2.7 %shard_map.85 = (f32[512,512]{1,0:T(8,128)S(1)}, f32[512,512]{1,0:T(8,128)S(1)}, f32[512,512]{1,0:T(8,128)S(1)}, bf16[512,512]{1,0:T(8,128)(2,1)S(1)}, bf16[512,512]{1,0:T(8,128)(2,1)S(1)}) custom-call(bf16[512,1024]{1,0:T(8,128)(2,1)} %q_hbm.1, bf16[512,1024]{1,0:T(8,128)(2,1)} %g_hbm.1, bf16[2,128,512]{2,1,0:T(8,128)(2,1)S(1)} %bitcast.24, ...), custom_call_target="tpu_custom_call" | custom-call | flops 1073741824 | bytes 3145728 | tf_op jit(solution)/shard_map/pallas_call | solution.py:395
  27.0 2.7 %collective-permute-done.9.refs_5_ = bf16[3,2,2,16,512]{4,3,2,1,0:T(8,128)(2,1)S(1)} collective-permute-done((bf16[3,2,2,16,512]{4,3,2,1,0:T(8,128)(2,1)S(1)}, bf16[3,2,2,16,512]{4,3,2,1,0:T(8,128)(2,1)S(1)}, u32[]{:S(2)}, u32[]{:S(2)}) %collective-permute-start.9) | collective-permute-done | bytes 196640 | tf_op jit(solution)/shard_map/ppermute | solution.py:426
  29.7 0.7 %collective-permute-done.7.refs_3_ = bf16[3,2,2,16,512]{4,3,2,1,0:T(8,128)(2,1)S(1)} collective-permute-done((bf16[3,2,2,16,512]{4,3,2,1,0:T(8,128)(2,1)S(1)}, bf16[3,2,2,16,512]{4,3,2,1,0:T(8,128)(2,1)S(1)}, u32[]{:S(2)}, u32[]{:S(2)}) %collective-permute-start.7) | collective-permute-done | bytes 196640 | tf_op jit(solution)/shard_map/ppermute | solution.py:426
  30.5 0.7 %collective-permute-done.11.refs_6_ = bf16[2,2,16,512]{3,2,1,0:T(8,128)(2,1)S(1)} collective-permute-done((bf16[2,2,16,512]{3,2,1,0:T(8,128)(2,1)S(1)}, bf16[2,2,16,512]{3,2,1,0:T(8,128)(2,1)S(1)}, u32[]{:S(2)}, u32[]{:S(2)}) %collective-permute-start.11) | collective-permute-done | bytes 65568 | tf_op jit(solution)/shard_map/ppermute | solution.py:426
  31.2 0.7 %collective-permute-done.8.refs_2_ = bf16[2,2,16,512]{3,2,1,0:T(8,128)(2,1)S(1)} collective-permute-done((bf16[2,2,16,512]{3,2,1,0:T(8,128)(2,1)S(1)}, bf16[2,2,16,512]{3,2,1,0:T(8,128)(2,1)S(1)}, u32[]{:S(2)}, u32[]{:S(2)}) %collective-permute-start.8) | collective-permute-done | bytes 65568 | tf_op jit(solution)/shard_map/ppermute | solution.py:426
  31.9 4.5 %shard_map.86 = (bf16[512,512]{1,0:T(8,128)(2,1)S(1)}, f32[512,512]{1,0:T(8,128)S(1)}, f32[512,512]{1,0:T(8,128)S(1)}, f32[512,512]{1,0:T(8,128)S(1)}, bf16[4,2,...) custom-call(bf16[512,512]{1,0:T(8,128)(2,1)S(1)} %get-tuple-element.56.q_ref, ...), custom_call_target="tpu_custom_call" | custom-call | flops 2684354560 | bytes 4194304 | tf_op jit(solution)/shard_map/pallas_call | solution.py:395
  36.5 1.6 %collective-permute-start.13 = (bf16[3,2,2,16,512]{4,3,2,1,0:T(8,128)(2,1)S(1)}, bf16[3,2,2,16,512]{4,3,2,1,0:T(8,128)(2,1)S(1)}, u32[]{:S(2)}, u32[]{:S(2)}) collective-permute-start(bf16[3,2,2,16,512]{4,3,2,1,0:T(8,128)(2,1)S(1)} %slice.42), channel_id=1, source_target_pairs={{0,4},{1,5},{2,6},{3,7},{4,0},{5,1},{6,2},{7,3},{8,12},{9,13},{10,... | collective-permute-start | bytes 589832 | tf_op jit(solution)/shard_map/ppermute | solution.py:426
  38.1 2.5 %shard_map.87 = (f32[2,2,16,512]{3,2,1,0:T(8,128)S(1)}, bf16[256,512]{1,0:T(8,128)(2,1)S(1)}, bf16[512,512]{1,0:T(8,128)(2,1)S(1)}, bf16[256,512]{1,0:T(8,128)(2,1)S(1)}) custom-call(f32[8,128]{1,0:T(8,128)S(1)} %get-tuple-element.67.block_ref, f32[512,512]{1,0:T(8,128)S(1)} %get-tuple-element.68.bias_ref, bf16[512,512]{1,0:T(8,128)(2,1)S(1)} %get-tuple-element.56.q_ref, ...), custom_call_target="tpu_custom_call" | custom-call | flops 2147483648 | bytes 6295552 | tf_op jit(solution)/shard_map/pallas_call | solution.py:395
  40.6 3.3 %collective-permute-done.13 = bf16[3,2,2,16,512]{4,3,2,1,0:T(8,128)(2,1)S(1)} collective-permute-done((bf16[3,2,2,16,512]{4,3,2,1,0:T(8,128)(2,1)S(1)}, bf16[3,2,2,16,512]{4,3,2,1,0:T(8,128)(2,1)S(1)}, u32[]{:S(2)}, u32[]{:S(2)}) %collective-permute-start.13) | collective-permute-done | bytes 196640 | tf_op jit(solution)/shard_map/ppermute | solution.py:426
  44.1 0.6 collective-permute-start.15
  44.7 1.3 %collective-permute-start.18 = (bf16[2,2,16,512]{3,2,1,0:T(8,128)(2,1)S(1)}, bf16[2,2,16,512]{3,2,1,0:T(8,128)(2,1)S(1)}, u32[]{:S(2)}, u32[]{:S(2)}) collective-permute-start(bf16[2,2,16,512]{3,2,1,0:T(8,128)(2,1)S(1)} %get-tuple-element.92), channel_id=1, source_target_pairs={{24,0},{28,4},{25,1},{29,5},{26,2},{30,6},{27,3},{31,7}} | collective-permute-start | bytes 196616 | tf_op jit(solution)/shard_map/ppermute | solution.py:434
  46.0 1.3 %collective-permute-start.17 = (bf16[2,2,16,512]{3,2,1,0:T(8,128)(2,1)S(1)}, bf16[2,2,16,512]{3,2,1,0:T(8,128)(2,1)S(1)}, u32[]{:S(2)}, u32[]{:S(2)}) collective-permute-start(bf16[2,2,16,512]{3,2,1,0:T(8,128)(2,1)S(1)} %get-tuple-element.93), channel_id=1, source_target_pairs={{16,0},{20,4},{24,8},{28,12},{17,1},{21,5},{25,9},{29,13},{18,2},{... | collective-permute-start | bytes 196616 | tf_op jit(solution)/shard_map/ppermute | solution.py:434
  47.3 1.3 %collective-permute-start.16 = (bf16[2,2,16,512]{3,2,1,0:T(8,128)(2,1)S(1)}, bf16[2,2,16,512]{3,2,1,0:T(8,128)(2,1)S(1)}, u32[]{:S(2)}, u32[]{:S(2)}) collective-permute-start(bf16[2,2,16,512]{3,2,1,0:T(8,128)(2,1)S(1)} %get-tuple-element.94), channel_id=1, source_target_pairs={{8,0},{12,4},{16,8},{20,12},{24,16},{28,20},{9,1},{13,5},{17,9},{2... | collective-permute-start | bytes 196616 | tf_op jit(solution)/shard_map/ppermute | solution.py:434
  48.6 1.6 %collective-permute-start.19 = (bf16[1,2,2,16,512]{4,3,2,1,0:T(8,128)(2,1)S(1)}, bf16[1,2,2,16,512]{4,3,2,1,0:T(8,128)(2,1)S(1)}, u32[]{:S(2)}, u32[]{:S(2)}) collective-permute-start(bf16[1,2,2,16,512]{4,3,2,1,0:T(8,128)(2,1)S(1)} %slice.51), channel_id=1, source_target_pairs={{0,4},{1,5},{2,6},{3,7},{4,0},{5,1},{6,2},{7,3},{8,12},{9,13},{10,... | collective-permute-start | bytes 196616 | tf_op jit(solution)/shard_map/ppermute | solution.py:426
  50.2 1.5 %shard_map.88 = (bf16[512,1024]{1,0:T(8,128)(2,1)}, bf16[512,1024]{1,0:T(8,128)(2,1)}, bf16[128,1024]{1,0:T(8,128)(2,1)}, bf16[128,1024]{1,0:T(8,128)(2,1)}) custom-call(bf16[512,512]{1,0:T(8,128)(2,1)S(1)} %get-tuple-element.66.att_ref, bf16[512,512]{1,0:T(8,128)(2,1)S(1)} %collective-permute-done.12.att_far, ...), custom_call_target="tpu_custom_call" | custom-call | tf_op jit(solution)/shard_map/pallas_call | solution.py:107
  51.7 1.4 %collective-permute-done.18.refs_2_ = bf16[2,2,16,512]{3,2,1,0:T(8,128)(2,1)S(1)} collective-permute-done((bf16[2,2,16,512]{3,2,1,0:T(8,128)(2,1)S(1)}, bf16[2,2,16,512]{3,2,1,0:T(8,128)(2,1)S(1)}, u32[]{:S(2)}, u32[]{:S(2)}) %collective-permute-start.18) | collective-permute-done | bytes 65568 | tf_op jit(solution)/shard_map/ppermute | solution.py:434
  53.1 2.4 %collective-permute-done.17.refs_1_ = bf16[2,2,16,512]{3,2,1,0:T(8,128)(2,1)S(1)} collective-permute-done((bf16[2,2,16,512]{3,2,1,0:T(8,128)(2,1)S(1)}, bf16[2,2,16,512]{3,2,1,0:T(8,128)(2,1)S(1)}, u32[]{:S(2)}, u32[]{:S(2)}) %collective-permute-start.17) | collective-permute-done | bytes 65568 | tf_op jit(solution)/shard_map/ppermute | solution.py:434
  55.6 1.2 %collective-permute-done.20.far_ref = bf16[2,16,512]{2,1,0:T(8,128)(2,1)S(1)} collective-permute-done((bf16[2,16,512]{2,1,0:T(8,128)(2,1)S(1)}, bf16[2,16,512]{2,1,0:T(8,128)(2,1)S(1)}, u32[]{:S(2)}, u32[]{:S(2)}) %collective-permute-start.20) | collective-permute-done | bytes 32800 | tf_op jit(solution)/shard_map/ppermute | solution.py:426
  56.7 0.8 %shard_map.89 = (bf16[128,1024]{1,0:T(8,128)(2,1)}, bf16[128,1024]{1,0:T(8,128)(2,1)}) custom-call(f32[8,128]{1,0:T(8,128)S(1)} %get-tuple-element.67.block_ref, f32[2,2,16,512]{3,2,1,0:T(8,128)S(1)} %get-tuple-element.74.chosen_ref, bf16[2,16,512]{2,1,0:T(8,128)(2,1)S(1)} %collective-permute-done.20.far_ref, ...), custom_call_target="tpu_custom_call", output_to_operand_aliasing={{0}: (7, {}), {1}: (8, {})} | custom-call | tf_op jit(solution)/shard_map/pallas_call | solution.py:142
  (25 shorter events, 0.5 us)
Async XLA Ops:
  1.9 3.5 %collective-permute-start.4 = (bf16[2,8,16,512]{3,2,1,0:T(8,128)(2,1)S(1)}, bf16[2,8,16,512]{3,2,1,0:T(8,128)(2,1)S(1)}, u32[]{:S(2)}, u32[]{:S(2)}) collective-permute-start(bf16[2,8,16,512]{3,2,1,0:T(8,128)(2,1)S(1)} %get-tuple-element.51), channel_id=1, source_target_pairs={{0,1},{1,0},{2,3},{3,2},{4,5},{5,4},{6,7},{7,6},{8,9},{9,8},{10,11... | collective-permute-start | bytes 786440 | tf_op jit(solution)/shard_map/ppermute | solution.py:426
  2.4 4.1 %collective-permute-start = (bf16[2,16,512]{2,1,0:T(8,128)(2,1)S(1)}, bf16[2,16,512]{2,1,0:T(8,128)(2,1)S(1)}, u32[]{:S(2)}, u32[]{:S(2)}) collective-permute-start(bf16[2,16,512]{2,1,0:T(8,128)(2,1)S(1)} %get-tuple-element.49), channel_id=1, source_target_pairs={{0,1},{1,0},{2,3},{3,2},{4,5},{5,4},{6,7},{7,6},{8,9},{9,8},{10,11... | collective-permute-start | bytes 98312 | tf_op jit(solution)/shard_map/ppermute | solution.py:426
  2.5 15.2 %collective-permute-start.5 = (bf16[2,8,16,512]{3,2,1,0:T(8,128)(2,1)S(1)}, bf16[2,8,16,512]{3,2,1,0:T(8,128)(2,1)S(1)}, u32[]{:S(2)}, u32[]{:S(2)}) collective-permute-start(bf16[2,8,16,512]{3,2,1,0:T(8,128)(2,1)S(1)} %get-tuple-element.52), channel_id=1, source_target_pairs={{0,2},{1,3},{2,0},{3,1},{4,6},{5,7},{6,4},{7,5},{8,10},{9,11},{10,... | collective-permute-start | bytes 786440 | tf_op jit(solution)/shard_map/ppermute | solution.py:426
  5.4 12.3 %collective-permute-start.6 = (bf16[2,8,16,512]{3,2,1,0:T(8,128)(2,1)S(1)}, bf16[2,8,16,512]{3,2,1,0:T(8,128)(2,1)S(1)}, u32[]{:S(2)}, u32[]{:S(2)}) collective-permute-start(bf16[2,8,16,512]{3,2,1,0:T(8,128)(2,1)S(1)} %collective-permute-done.4), channel_id=1, source_target_pairs={{0,2},{1,3},{2,0},{3,1},{4,6},{5,7},{6,4},{7,5},{8,10},{9,11},{10,... | collective-permute-start | bytes 786440 | tf_op jit(solution)/shard_map/ppermute | solution.py:426
  6.4 9.3 %collective-permute-start.3 = (bf16[2,2,16,512]{3,2,1,0:T(8,128)(2,1)S(1)}, bf16[2,2,16,512]{3,2,1,0:T(8,128)(2,1)S(1)}, u32[]{:S(2)}, u32[]{:S(2)}) collective-permute-start(bf16[2,2,16,512]{3,2,1,0:T(8,128)(2,1)S(1)} %pad_maximum_fusion.1.refs_0_.refs_4_), channel_id=1, source_target_pairs={{0,24},{4,28},{1,25},{5,29},{2,26},{6,30},{3,27},{7,31}} | collective-permute-start | bytes 196616 | tf_op jit(solution)/shard_map/ppermute | solution.py:429
  12.0 3.8 %collective-permute-start.2 = (bf16[2,2,16,512]{3,2,1,0:T(8,128)(2,1)S(1)}, bf16[2,2,16,512]{3,2,1,0:T(8,128)(2,1)S(1)}, u32[]{:S(2)}, u32[]{:S(2)}) collective-permute-start(bf16[2,2,16,512]{3,2,1,0:T(8,128)(2,1)S(1)} %pad_maximum_fusion.1.refs_0_.refs_4_), channel_id=1, source_target_pairs={{0,16},{4,20},{8,24},{12,28},{1,17},{5,21},{9,25},{13,29},{2,18},{... | collective-permute-start | bytes 196616 | tf_op jit(solution)/shard_map/ppermute | solution.py:429
  13.3 4.4 %collective-permute-start.1 = (bf16[2,2,16,512]{3,2,1,0:T(8,128)(2,1)S(1)}, bf16[2,2,16,512]{3,2,1,0:T(8,128)(2,1)S(1)}, u32[]{:S(2)}, u32[]{:S(2)}) collective-permute-start(bf16[2,2,16,512]{3,2,1,0:T(8,128)(2,1)S(1)} %pad_maximum_fusion.1.refs_0_.refs_4_), channel_id=1, source_target_pairs={{0,8},{4,12},{8,16},{12,20},{16,24},{20,28},{1,9},{5,13},{9,17},{1... | collective-permute-start | bytes 196616 | tf_op jit(solution)/shard_map/ppermute | solution.py:429
  17.7 9.3 %collective-permute-start.10 = (bf16[3,2,2,16,512]{4,3,2,1,0:T(8,128)(2,1)S(1)}, bf16[3,2,2,16,512]{4,3,2,1,0:T(8,128)(2,1)S(1)}, u32[]{:S(2)}, u32[]{:S(2)}) collective-permute-start(bf16[3,2,2,16,512]{4,3,2,1,0:T(8,128)(2,1)S(1)} %pad_maximum_fusion.refs_1_), channel_id=1, source_target_pairs={{0,6},{1,7},{2,4},{3,5},{4,2},{5,3},{6,0},{7,1},{8,14},{9,15},{10,... | collective-permute-start | bytes 589832 | tf_op jit(solution)/shard_map/ppermute | solution.py:426
  20.2 9.5 %collective-permute-start.9 = (bf16[3,2,2,16,512]{4,3,2,1,0:T(8,128)(2,1)S(1)}, bf16[3,2,2,16,512]{4,3,2,1,0:T(8,128)(2,1)S(1)}, u32[]{:S(2)}, u32[]{:S(2)}) collective-permute-start(bf16[3,2,2,16,512]{4,3,2,1,0:T(8,128)(2,1)S(1)} %pad_maximum_fusion.refs_1_), channel_id=1, source_target_pairs={{0,2},{1,3},{2,0},{3,1},{4,6},{5,7},{6,4},{7,5},{8,10},{9,11},{10,... | collective-permute-start | bytes 589832 | tf_op jit(solution)/shard_map/ppermute | solution.py:426
  20.7 9.7 %collective-permute-start.7 = (bf16[3,2,2,16,512]{4,3,2,1,0:T(8,128)(2,1)S(1)}, bf16[3,2,2,16,512]{4,3,2,1,0:T(8,128)(2,1)S(1)}, u32[]{:S(2)}, u32[]{:S(2)}) collective-permute-start(bf16[3,2,2,16,512]{4,3,2,1,0:T(8,128)(2,1)S(1)} %pad_maximum_fusion.refs_1_), channel_id=1, source_target_pairs={{0,4},{1,5},{2,6},{3,7},{4,0},{5,1},{6,2},{7,3},{8,12},{9,13},{10,... | collective-permute-start | bytes 589832 | tf_op jit(solution)/shard_map/ppermute | solution.py:426
  21.2 9.9 %collective-permute-start.11 = (bf16[2,2,16,512]{3,2,1,0:T(8,128)(2,1)S(1)}, bf16[2,2,16,512]{3,2,1,0:T(8,128)(2,1)S(1)}, u32[]{:S(2)}, u32[]{:S(2)}) collective-permute-start(bf16[2,2,16,512]{3,2,1,0:T(8,128)(2,1)S(1)} %pad_maximum_fusion.1.refs_0_.refs_4_), channel_id=1, source_target_pairs={{0,6},{1,7},{2,4},{3,5},{4,2},{5,3},{6,0},{7,1},{8,14},{9,15},{10,... | collective-permute-start | bytes 196616 | tf_op jit(solution)/shard_map/ppermute | solution.py:426
  23.7 8.1 %collective-permute-start.8 = (bf16[2,2,16,512]{3,2,1,0:T(8,128)(2,1)S(1)}, bf16[2,2,16,512]{3,2,1,0:T(8,128)(2,1)S(1)}, u32[]{:S(2)}, u32[]{:S(2)}) collective-permute-start(bf16[2,2,16,512]{3,2,1,0:T(8,128)(2,1)S(1)} %pad_maximum_fusion.1.refs_0_.refs_4_), channel_id=1, source_target_pairs={{0,4},{1,5},{2,6},{3,7},{4,0},{5,1},{6,2},{7,3},{8,12},{9,13},{10,... | collective-permute-start | bytes 196616 | tf_op jit(solution)/shard_map/ppermute | solution.py:426
  36.4 7.5 %collective-permute-start.12 = (bf16[512,512]{1,0:T(8,128)(2,1)S(1)}, bf16[512,512]{1,0:T(8,128)(2,1)S(1)}, u32[]{:S(2)}, u32[]{:S(2)}) collective-permute-start(bf16[512,512]{1,0:T(8,128)(2,1)S(1)} %get-tuple-element.66.att_ref), channel_id=1, source_target_pairs={{0,1},{1,0},{2,3},{3,2},{4,5},{5,4},{6,7},{7,6},{8,9},{9,8},{10,11... | collective-permute-start | bytes 1572872 | tf_op jit(solution)/shard_map/ppermute | solution.py:426
  36.5 7.4 %collective-permute-start.13 = (bf16[3,2,2,16,512]{4,3,2,1,0:T(8,128)(2,1)S(1)}, bf16[3,2,2,16,512]{4,3,2,1,0:T(8,128)(2,1)S(1)}, u32[]{:S(2)}, u32[]{:S(2)}) collective-permute-start(bf16[3,2,2,16,512]{4,3,2,1,0:T(8,128)(2,1)S(1)} %slice.42), channel_id=1, source_target_pairs={{0,4},{1,5},{2,6},{3,7},{4,0},{5,1},{6,2},{7,3},{8,12},{9,13},{10,... | collective-permute-start | bytes 589832 | tf_op jit(solution)/shard_map/ppermute | solution.py:426
  43.9 6.2 %collective-permute-start.14 = (bf16[512,512]{1,0:T(8,128)(2,1)S(1)}, bf16[512,512]{1,0:T(8,128)(2,1)S(1)}, u32[]{:S(2)}, u32[]{:S(2)}) collective-permute-start(bf16[512,512]{1,0:T(8,128)(2,1)S(1)} %broadcast_add_fusion.gq_ref), channel_id=1, source_target_pairs={{0,1},{1,0},{2,3},{3,2},{4,5},{5,4},{6,7},{7,6},{8,9},{9,8},{10,11... | collective-permute-start | bytes 1572872 | tf_op jit(solution)/shard_map/ppermute | solution.py:426
  44.1 4.5 %collective-permute-start.15 = (bf16[256,512]{1,0:T(8,128)(2,1)S(1)}, bf16[256,512]{1,0:T(8,128)(2,1)S(1)}, u32[]{:S(2)}, u32[]{:S(2)}) collective-permute-start(bf16[256,512]{1,0:T(8,128)(2,1)S(1)} %broadcast_add_fusion.1), channel_id=1, source_target_pairs={{0,1},{1,0},{2,3},{3,2},{4,5},{5,4},{6,7},{7,6},{8,9},{9,8},{10,11... | collective-permute-start | bytes 786440 | tf_op jit(solution)/shard_map/ppermute | solution.py:426
  44.7 8.4 %collective-permute-start.18 = (bf16[2,2,16,512]{3,2,1,0:T(8,128)(2,1)S(1)}, bf16[2,2,16,512]{3,2,1,0:T(8,128)(2,1)S(1)}, u32[]{:S(2)}, u32[]{:S(2)}) collective-permute-start(bf16[2,2,16,512]{3,2,1,0:T(8,128)(2,1)S(1)} %get-tuple-element.92), channel_id=1, source_target_pairs={{24,0},{28,4},{25,1},{29,5},{26,2},{30,6},{27,3},{31,7}} | collective-permute-start | bytes 196616 | tf_op jit(solution)/shard_map/ppermute | solution.py:434
  46.0 9.5 %collective-permute-start.17 = (bf16[2,2,16,512]{3,2,1,0:T(8,128)(2,1)S(1)}, bf16[2,2,16,512]{3,2,1,0:T(8,128)(2,1)S(1)}, u32[]{:S(2)}, u32[]{:S(2)}) collective-permute-start(bf16[2,2,16,512]{3,2,1,0:T(8,128)(2,1)S(1)} %get-tuple-element.93), channel_id=1, source_target_pairs={{16,0},{20,4},{24,8},{28,12},{17,1},{21,5},{25,9},{29,13},{18,2},{... | collective-permute-start | bytes 196616 | tf_op jit(solution)/shard_map/ppermute | solution.py:434
  47.3 8.2 %collective-permute-start.16 = (bf16[2,2,16,512]{3,2,1,0:T(8,128)(2,1)S(1)}, bf16[2,2,16,512]{3,2,1,0:T(8,128)(2,1)S(1)}, u32[]{:S(2)}, u32[]{:S(2)}) collective-permute-start(bf16[2,2,16,512]{3,2,1,0:T(8,128)(2,1)S(1)} %get-tuple-element.94), channel_id=1, source_target_pairs={{8,0},{12,4},{16,8},{20,12},{24,16},{28,20},{9,1},{13,5},{17,9},{2... | collective-permute-start | bytes 196616 | tf_op jit(solution)/shard_map/ppermute | solution.py:434
  48.6 6.9 %collective-permute-start.19 = (bf16[1,2,2,16,512]{4,3,2,1,0:T(8,128)(2,1)S(1)}, bf16[1,2,2,16,512]{4,3,2,1,0:T(8,128)(2,1)S(1)}, u32[]{:S(2)}, u32[]{:S(2)}) collective-permute-start(bf16[1,2,2,16,512]{4,3,2,1,0:T(8,128)(2,1)S(1)} %slice.51), channel_id=1, source_target_pairs={{0,4},{1,5},{2,6},{3,7},{4,0},{5,1},{6,2},{7,3},{8,12},{9,13},{10,... | collective-permute-start | bytes 196616 | tf_op jit(solution)/shard_map/ppermute | solution.py:426
  55.5 1.3 %collective-permute-start.20 = (bf16[2,16,512]{2,1,0:T(8,128)(2,1)S(1)}, bf16[2,16,512]{2,1,0:T(8,128)(2,1)S(1)}, u32[]{:S(2)}, u32[]{:S(2)}) collective-permute-start(bf16[2,16,512]{2,1,0:T(8,128)(2,1)S(1)} %fusion.3), channel_id=1, source_target_pairs={{0,1},{1,0},{2,3},{3,2},{4,5},{5,4},{6,7},{7,6},{8,9},{9,8},{10,11... | collective-permute-start | bytes 98312 | tf_op jit(solution)/shard_map/ppermute | solution.py:426

commit v7 on v6

--- a/solution.py
+++ b/solution.py
@@ -463,7 +463,7 @@
     far_width = members * seq_count * part_tok
     far_pairs = HEADS // CORES * tok_rows * far_width
     roomy = far_width <= 512
-    far_plan = (tok_rows // 2, GROUP, 2 * GROUP) if roomy else (tok_rows // 8, 1, 1)
+    far_plan = (tok_rows // 2, HEADS // CORES, 2 * GROUP) if roomy else (tok_rows // 8, 1, 1)
 
     near_sum, near_stat, bias, queries, grad_out = call(
         functools.partial(near_forward_kernel, members, blk_len, part_tok, head_dim),

time: 57.8 us -> 57.3 us (level)
  no operation moved by 1% of the time
where the time goes in v7:
time: 57.3 us; the launch traced here: 57 us
  starting transfers between devices  28.2 us (49%)
  waiting for transfers between devices  14.9 us (26%)
  Pallas kernels  12.8 us (22%)
  between operations  0.84 us (1%)
    ppermute x15, starting transfers between devices, hop(): return lax.ppermute(part, ('seq', 'kv'), pairs)  15.1 us
    ppermute x15, waiting for transfers between devices, hop(): return lax.ppermute(part, ('seq', 'kv'), pairs)  9.31 us
    ppermute x3, starting transfers between devices, climb(): lax.ppermute(part, 'seq', [(s, s + COLUMNS * d) for s in range(seq_count...  9.27 us
    pallas_call x3, Pallas kernels, call(): pl.pallas_call(kernel, in_specs=in_specs or [WHOLE] * len(operands), out_...  9.26 us
    ppermute x3, starting transfers between devices, sink(): lax.ppermute(part, 'seq', [(s, s - COLUMNS * d) for s in range(COLUMNS *...  3.88 us
    ppermute x3, waiting for transfers between devices, sink(): lax.ppermute(part, 'seq', [(s, s - COLUMNS * d) for s in range(COLUMNS *...  3.73 us
    ppermute x3, waiting for transfers between devices, climb(): lax.ppermute(part, 'seq', [(s, s + COLUMNS * d) for s in range(seq_count...  1.87 us
    pallas_call x1, Pallas kernels, join(): pl.pallas_call(join_kernel, in_specs=[WHOLE] * len(operands), out_specs=[...  1.54 us
  transfers between devices with their start and end apart: 21, of which 9 were waited for; matrix products, arithmetic and copies ran while one was open for 0% of the time, Pallas kernels for 12%

profile of v7, /device:TPU:0, one launch (start us, length us, event | category | flops | bytes accessed | tf_op | source)
XLA Modules:
  0.0 57.0 jit_solution(6352096498497072248)
XLA Ops:
  0.6 1.2 %shard_map.84 = (bf16[2,8,16,512]{3,2,1,0:T(8,128)(2,1)S(1)}, bf16[2,8,16,512]{3,2,1,0:T(8,128)(2,1)S(1)}, bf16[2,16,512]{2,1,0:T(8,128)(2,1)S(1)}, bf16[2,16,512]{2,1,0:T(8,128)(2,1)S(1)}, f32[8,128]{1,0:T(8,128)S(1)}) custom-call(s32[15,64]{1,0:T(8,128)} %bitcast.38, bf16[8,16,1024]{2,1,0:T(8,128)(2,1)} %keys_hbm.1, bf16[8,16,1024]{2,1,0:T(8,128)(2,1)} %values_hbm.1), custom_call_target="tpu_custom_call" | custom-call | tf_op jit(solution)/shard_map/pallas_call | solution.py:74
  1.9 0.5 collective-permute-start.4
  2.5 2.9 %collective-permute-start.5 = (bf16[2,8,16,512]{3,2,1,0:T(8,128)(2,1)S(1)}, bf16[2,8,16,512]{3,2,1,0:T(8,128)(2,1)S(1)}, u32[]{:S(2)}, u32[]{:S(2)}) collective-permute-start(bf16[2,8,16,512]{3,2,1,0:T(8,128)(2,1)S(1)} %get-tuple-element.52), channel_id=1, source_target_pairs={{0,2},{1,3},{2,0},{3,1},{4,6},{5,7},{6,4},{7,5},{8,10},{9,11},{10,... | collective-permute-start | bytes 786440 | tf_op jit(solution)/shard_map/ppermute | solution.py:426
  5.4 1.0 %collective-permute-start.6 = (bf16[2,8,16,512]{3,2,1,0:T(8,128)(2,1)S(1)}, bf16[2,8,16,512]{3,2,1,0:T(8,128)(2,1)S(1)}, u32[]{:S(2)}, u32[]{:S(2)}) collective-permute-start(bf16[2,8,16,512]{3,2,1,0:T(8,128)(2,1)S(1)} %collective-permute-done.4), channel_id=1, source_target_pairs={{0,2},{1,3},{2,0},{3,1},{4,6},{5,7},{6,4},{7,5},{8,10},{9,11},{10,... | collective-permute-start | bytes 786440 | tf_op jit(solution)/shard_map/ppermute | solution.py:426
  6.4 5.5 %collective-permute-start.3 = (bf16[2,2,16,512]{3,2,1,0:T(8,128)(2,1)S(1)}, bf16[2,2,16,512]{3,2,1,0:T(8,128)(2,1)S(1)}, u32[]{:S(2)}, u32[]{:S(2)}) collective-permute-start(bf16[2,2,16,512]{3,2,1,0:T(8,128)(2,1)S(1)} %pad_maximum_fusion.1.refs_0_.refs_4_), channel_id=1, source_target_pairs={{0,24},{4,28},{1,25},{5,29},{2,26},{6,30},{3,27},{7,31}} | collective-permute-start | bytes 196616 | tf_op jit(solution)/shard_map/ppermute | solution.py:429
  12.0 1.3 %collective-permute-start.2 = (bf16[2,2,16,512]{3,2,1,0:T(8,128)(2,1)S(1)}, bf16[2,2,16,512]{3,2,1,0:T(8,128)(2,1)S(1)}, u32[]{:S(2)}, u32[]{:S(2)}) collective-permute-start(bf16[2,2,16,512]{3,2,1,0:T(8,128)(2,1)S(1)} %pad_maximum_fusion.1.refs_0_.refs_4_), channel_id=1, source_target_pairs={{0,16},{4,20},{8,24},{12,28},{1,17},{5,21},{9,25},{13,29},{2,18},{... | collective-permute-start | bytes 196616 | tf_op jit(solution)/shard_map/ppermute | solution.py:429
  13.3 2.5 %collective-permute-start.1 = (bf16[2,2,16,512]{3,2,1,0:T(8,128)(2,1)S(1)}, bf16[2,2,16,512]{3,2,1,0:T(8,128)(2,1)S(1)}, u32[]{:S(2)}, u32[]{:S(2)}) collective-permute-start(bf16[2,2,16,512]{3,2,1,0:T(8,128)(2,1)S(1)} %pad_maximum_fusion.1.refs_0_.refs_4_), channel_id=1, source_target_pairs={{0,8},{4,12},{8,16},{12,20},{16,24},{20,28},{1,9},{5,13},{9,17},{1... | collective-permute-start | bytes 196616 | tf_op jit(solution)/shard_map/ppermute | solution.py:429
  15.8 1.9 %collective-permute-done.1 = bf16[2,2,16,512]{3,2,1,0:T(8,128)(2,1)S(1)} collective-permute-done((bf16[2,2,16,512]{3,2,1,0:T(8,128)(2,1)S(1)}, bf16[2,2,16,512]{3,2,1,0:T(8,128)(2,1)S(1)}, u32[]{:S(2)}, u32[]{:S(2)}) %collective-permute-start.1) | collective-permute-done | bytes 65568 | tf_op jit(solution)/shard_map/ppermute | solution.py:429
  17.7 2.6 %collective-permute-start.10 = (bf16[3,2,2,16,512]{4,3,2,1,0:T(8,128)(2,1)S(1)}, bf16[3,2,2,16,512]{4,3,2,1,0:T(8,128)(2,1)S(1)}, u32[]{:S(2)}, u32[]{:S(2)}) collective-permute-start(bf16[3,2,2,16,512]{4,3,2,1,0:T(8,128)(2,1)S(1)} %pad_maximum_fusion.refs_1_), channel_id=1, source_target_pairs={{0,6},{1,7},{2,4},{3,5},{4,2},{5,3},{6,0},{7,1},{8,14},{9,15},{10,... | collective-permute-start | bytes 589832 | tf_op jit(solution)/shard_map/ppermute | solution.py:426
  20.2 0.5 collective-permute-start.9
  20.7 0.5 collective-permute-start.7
  21.2 2.5 %collective-permute-start.11 = (bf16[2,2,16,512]{3,2,1,0:T(8,128)(2,1)S(1)}, bf16[2,2,16,512]{3,2,1,0:T(8,128)(2,1)S(1)}, u32[]{:S(2)}, u32[]{:S(2)}) collective-permute-start(bf16[2,2,16,512]{3,2,1,0:T(8,128)(2,1)S(1)} %pad_maximum_fusion.1.refs_0_.refs_4_), channel_id=1, source_target_pairs={{0,6},{1,7},{2,4},{3,5},{4,2},{5,3},{6,0},{7,1},{8,14},{9,15},{10,... | collective-permute-start | bytes 196616 | tf_op jit(solution)/shard_map/ppermute | solution.py:426
  23.7 0.5 collective-permute-start.8
  24.3 2.7 %shard_map.85 = (f32[512,512]{1,0:T(8,128)S(1)}, f32[512,512]{1,0:T(8,128)S(1)}, f32[512,512]{1,0:T(8,128)S(1)}, bf16[512,512]{1,0:T(8,128)(2,1)S(1)}, bf16[512,512]{1,0:T(8,128)(2,1)S(1)}) custom-call(bf16[512,1024]{1,0:T(8,128)(2,1)} %q_hbm.1, bf16[512,1024]{1,0:T(8,128)(2,1)} %g_hbm.1, bf16[2,128,512]{2,1,0:T(8,128)(2,1)S(1)} %bitcast.24, ...), custom_call_target="tpu_custom_call" | custom-call | flops 1073741824 | bytes 3145728 | tf_op jit(solution)/shard_map/pallas_call | solution.py:395
  27.0 2.7 %collective-permute-done.9.refs_5_ = bf16[3,2,2,16,512]{4,3,2,1,0:T(8,128)(2,1)S(1)} collective-permute-done((bf16[3,2,2,16,512]{4,3,2,1,0:T(8,128)(2,1)S(1)}, bf16[3,2,2,16,512]{4,3,2,1,0:T(8,128)(2,1)S(1)}, u32[]{:S(2)}, u32[]{:S(2)}) %collective-permute-start.9) | collective-permute-done | bytes 196640 | tf_op jit(solution)/shard_map/ppermute | solution.py:426
  29.7 0.7 %collective-permute-done.7.refs_3_ = bf16[3,2,2,16,512]{4,3,2,1,0:T(8,128)(2,1)S(1)} collective-permute-done((bf16[3,2,2,16,512]{4,3,2,1,0:T(8,128)(2,1)S(1)}, bf16[3,2,2,16,512]{4,3,2,1,0:T(8,128)(2,1)S(1)}, u32[]{:S(2)}, u32[]{:S(2)}) %collective-permute-start.7) | collective-permute-done | bytes 196640 | tf_op jit(solution)/shard_map/ppermute | solution.py:426
  30.5 0.7 %collective-permute-done.11.refs_6_ = bf16[2,2,16,512]{3,2,1,0:T(8,128)(2,1)S(1)} collective-permute-done((bf16[2,2,16,512]{3,2,1,0:T(8,128)(2,1)S(1)}, bf16[2,2,16,512]{3,2,1,0:T(8,128)(2,1)S(1)}, u32[]{:S(2)}, u32[]{:S(2)}) %collective-permute-start.11) | collective-permute-done | bytes 65568 | tf_op jit(solution)/shard_map/ppermute | solution.py:426
  31.2 0.7 %collective-permute-done.8.refs_2_ = bf16[2,2,16,512]{3,2,1,0:T(8,128)(2,1)S(1)} collective-permute-done((bf16[2,2,16,512]{3,2,1,0:T(8,128)(2,1)S(1)}, bf16[2,2,16,512]{3,2,1,0:T(8,128)(2,1)S(1)}, u32[]{:S(2)}, u32[]{:S(2)}) %collective-permute-start.8) | collective-permute-done | bytes 65568 | tf_op jit(solution)/shard_map/ppermute | solution.py:426
  31.9 4.0 %shard_map.86 = (bf16[512,512]{1,0:T(8,128)(2,1)S(1)}, f32[512,512]{1,0:T(8,128)S(1)}, f32[512,512]{1,0:T(8,128)S(1)}, f32[512,512]{1,0:T(8,128)S(1)}, bf16[4,2,...) custom-call(bf16[512,512]{1,0:T(8,128)(2,1)S(1)} %get-tuple-element.56.q_ref, ...), custom_call_target="tpu_custom_call" | custom-call | flops 2684354560 | bytes 4194304 | tf_op jit(solution)/shard_map/pallas_call | solution.py:395
  36.0 1.6 %collective-permute-start.13 = (bf16[3,2,2,16,512]{4,3,2,1,0:T(8,128)(2,1)S(1)}, bf16[3,2,2,16,512]{4,3,2,1,0:T(8,128)(2,1)S(1)}, u32[]{:S(2)}, u32[]{:S(2)}) collective-permute-start(bf16[3,2,2,16,512]{4,3,2,1,0:T(8,128)(2,1)S(1)} %slice.42), channel_id=1, source_target_pairs={{0,4},{1,5},{2,6},{3,7},{4,0},{5,1},{6,2},{7,3},{8,12},{9,13},{10,... | collective-permute-start | bytes 589832 | tf_op jit(solution)/shard_map/ppermute | solution.py:426
  37.5 2.5 %shard_map.87 = (f32[2,2,16,512]{3,2,1,0:T(8,128)S(1)}, bf16[256,512]{1,0:T(8,128)(2,1)S(1)}, bf16[512,512]{1,0:T(8,128)(2,1)S(1)}, bf16[256,512]{1,0:T(8,128)(2,1)S(1)}) custom-call(f32[8,128]{1,0:T(8,128)S(1)} %get-tuple-element.67.block_ref, f32[512,512]{1,0:T(8,128)S(1)} %get-tuple-element.68.bias_ref, bf16[512,512]{1,0:T(8,128)(2,1)S(1)} %get-tuple-element.56.q_ref, ...), custom_call_target="tpu_custom_call" | custom-call | flops 2147483648 | bytes 6295552 | tf_op jit(solution)/shard_map/pallas_call | solution.py:395
  40.1 3.2 %collective-permute-done.13 = bf16[3,2,2,16,512]{4,3,2,1,0:T(8,128)(2,1)S(1)} collective-permute-done((bf16[3,2,2,16,512]{4,3,2,1,0:T(8,128)(2,1)S(1)}, bf16[3,2,2,16,512]{4,3,2,1,0:T(8,128)(2,1)S(1)}, u32[]{:S(2)}, u32[]{:S(2)}) %collective-permute-start.13) | collective-permute-done | bytes 196640 | tf_op jit(solution)/shard_map/ppermute | solution.py:426
  43.5 0.6 collective-permute-start.15
  44.1 1.3 %collective-permute-start.18 = (bf16[2,2,16,512]{3,2,1,0:T(8,128)(2,1)S(1)}, bf16[2,2,16,512]{3,2,1,0:T(8,128)(2,1)S(1)}, u32[]{:S(2)}, u32[]{:S(2)}) collective-permute-start(bf16[2,2,16,512]{3,2,1,0:T(8,128)(2,1)S(1)} %get-tuple-element.92), channel_id=1, source_target_pairs={{24,0},{28,4},{25,1},{29,5},{26,2},{30,6},{27,3},{31,7}} | collective-permute-start | bytes 196616 | tf_op jit(solution)/shard_map/ppermute | solution.py:434
  45.4 1.3 %collective-permute-start.17 = (bf16[2,2,16,512]{3,2,1,0:T(8,128)(2,1)S(1)}, bf16[2,2,16,512]{3,2,1,0:T(8,128)(2,1)S(1)}, u32[]{:S(2)}, u32[]{:S(2)}) collective-permute-start(bf16[2,2,16,512]{3,2,1,0:T(8,128)(2,1)S(1)} %get-tuple-element.93), channel_id=1, source_target_pairs={{16,0},{20,4},{24,8},{28,12},{17,1},{21,5},{25,9},{29,13},{18,2},{... | collective-permute-start | bytes 196616 | tf_op jit(solution)/shard_map/ppermute | solution.py:434
  46.7 1.3 %collective-permute-start.16 = (bf16[2,2,16,512]{3,2,1,0:T(8,128)(2,1)S(1)}, bf16[2,2,16,512]{3,2,1,0:T(8,128)(2,1)S(1)}, u32[]{:S(2)}, u32[]{:S(2)}) collective-permute-start(bf16[2,2,16,512]{3,2,1,0:T(8,128)(2,1)S(1)} %get-tuple-element.94), channel_id=1, source_target_pairs={{8,0},{12,4},{16,8},{20,12},{24,16},{28,20},{9,1},{13,5},{17,9},{2... | collective-permute-start | bytes 196616 | tf_op jit(solution)/shard_map/ppermute | solution.py:434
  48.0 1.6 %collective-permute-start.19 = (bf16[1,2,2,16,512]{4,3,2,1,0:T(8,128)(2,1)S(1)}, bf16[1,2,2,16,512]{4,3,2,1,0:T(8,128)(2,1)S(1)}, u32[]{:S(2)}, u32[]{:S(2)}) collective-permute-start(bf16[1,2,2,16,512]{4,3,2,1,0:T(8,128)(2,1)S(1)} %slice.51), channel_id=1, source_target_pairs={{0,4},{1,5},{2,6},{3,7},{4,0},{5,1},{6,2},{7,3},{8,12},{9,13},{10,... | collective-permute-start | bytes 196616 | tf_op jit(solution)/shard_map/ppermute | solution.py:426
  49.6 1.5 %shard_map.88 = (bf16[512,1024]{1,0:T(8,128)(2,1)}, bf16[512,1024]{1,0:T(8,128)(2,1)}, bf16[128,1024]{1,0:T(8,128)(2,1)}, bf16[128,1024]{1,0:T(8,128)(2,1)}) custom-call(bf16[512,512]{1,0:T(8,128)(2,1)S(1)} %get-tuple-element.66.att_ref, bf16[512,512]{1,0:T(8,128)(2,1)S(1)} %collective-permute-done.12.att_far, ...), custom_call_target="tpu_custom_call" | custom-call | tf_op jit(solution)/shard_map/pallas_call | solution.py:107
  51.2 1.4 %collective-permute-done.18.refs_2_ = bf16[2,2,16,512]{3,2,1,0:T(8,128)(2,1)S(1)} collective-permute-done((bf16[2,2,16,512]{3,2,1,0:T(8,128)(2,1)S(1)}, bf16[2,2,16,512]{3,2,1,0:T(8,128)(2,1)S(1)}, u32[]{:S(2)}, u32[]{:S(2)}) %collective-permute-start.18) | collective-permute-done | bytes 65568 | tf_op jit(solution)/shard_map/ppermute | solution.py:434
  52.5 2.4 %collective-permute-done.17.refs_1_ = bf16[2,2,16,512]{3,2,1,0:T(8,128)(2,1)S(1)} collective-permute-done((bf16[2,2,16,512]{3,2,1,0:T(8,128)(2,1)S(1)}, bf16[2,2,16,512]{3,2,1,0:T(8,128)(2,1)S(1)}, u32[]{:S(2)}, u32[]{:S(2)}) %collective-permute-start.17) | collective-permute-done | bytes 65568 | tf_op jit(solution)/shard_map/ppermute | solution.py:434
  55.0 1.2 %collective-permute-done.20.far_ref = bf16[2,16,512]{2,1,0:T(8,128)(2,1)S(1)} collective-permute-done((bf16[2,16,512]{2,1,0:T(8,128)(2,1)S(1)}, bf16[2,16,512]{2,1,0:T(8,128)(2,1)S(1)}, u32[]{:S(2)}, u32[]{:S(2)}) %collective-permute-start.20) | collective-permute-done | bytes 32800 | tf_op jit(solution)/shard_map/ppermute | solution.py:426
  56.2 0.8 %shard_map.89 = (bf16[128,1024]{1,0:T(8,128)(2,1)}, bf16[128,1024]{1,0:T(8,128)(2,1)}) custom-call(f32[8,128]{1,0:T(8,128)S(1)} %get-tuple-element.67.block_ref, f32[2,2,16,512]{3,2,1,0:T(8,128)S(1)} %get-tuple-element.74.chosen_ref, bf16[2,16,512]{2,1,0:T(8,128)(2,1)S(1)} %collective-permute-done.20.far_ref, ...), custom_call_target="tpu_custom_call", output_to_operand_aliasing={{0}: (7, {}), {1}: (8, {})} | custom-call | tf_op jit(solution)/shard_map/pallas_call | solution.py:142
  (25 shorter events, 0.5 us)
Async XLA Ops:
  1.9 3.5 %collective-permute-start.4 = (bf16[2,8,16,512]{3,2,1,0:T(8,128)(2,1)S(1)}, bf16[2,8,16,512]{3,2,1,0:T(8,128)(2,1)S(1)}, u32[]{:S(2)}, u32[]{:S(2)}) collective-permute-start(bf16[2,8,16,512]{3,2,1,0:T(8,128)(2,1)S(1)} %get-tuple-element.51), channel_id=1, source_target_pairs={{0,1},{1,0},{2,3},{3,2},{4,5},{5,4},{6,7},{7,6},{8,9},{9,8},{10,11... | collective-permute-start | bytes 786440 | tf_op jit(solution)/shard_map/ppermute | solution.py:426
  2.4 4.1 %collective-permute-start = (bf16[2,16,512]{2,1,0:T(8,128)(2,1)S(1)}, bf16[2,16,512]{2,1,0:T(8,128)(2,1)S(1)}, u32[]{:S(2)}, u32[]{:S(2)}) collective-permute-start(bf16[2,16,512]{2,1,0:T(8,128)(2,1)S(1)} %get-tuple-element.49), channel_id=1, source_target_pairs={{0,1},{1,0},{2,3},{3,2},{4,5},{5,4},{6,7},{7,6},{8,9},{9,8},{10,11... | collective-permute-start | bytes 98312 | tf_op jit(solution)/shard_map/ppermute | solution.py:426
  2.5 15.2 %collective-permute-start.5 = (bf16[2,8,16,512]{3,2,1,0:T(8,128)(2,1)S(1)}, bf16[2,8,16,512]{3,2,1,0:T(8,128)(2,1)S(1)}, u32[]{:S(2)}, u32[]{:S(2)}) collective-permute-start(bf16[2,8,16,512]{3,2,1,0:T(8,128)(2,1)S(1)} %get-tuple-element.52), channel_id=1, source_target_pairs={{0,2},{1,3},{2,0},{3,1},{4,6},{5,7},{6,4},{7,5},{8,10},{9,11},{10,... | collective-permute-start | bytes 786440 | tf_op jit(solution)/shard_map/ppermute | solution.py:426
  5.4 12.3 %collective-permute-start.6 = (bf16[2,8,16,512]{3,2,1,0:T(8,128)(2,1)S(1)}, bf16[2,8,16,512]{3,2,1,0:T(8,128)(2,1)S(1)}, u32[]{:S(2)}, u32[]{:S(2)}) collective-permute-start(bf16[2,8,16,512]{3,2,1,0:T(8,128)(2,1)S(1)} %collective-permute-done.4), channel_id=1, source_target_pairs={{0,2},{1,3},{2,0},{3,1},{4,6},{5,7},{6,4},{7,5},{8,10},{9,11},{10,... | collective-permute-start | bytes 786440 | tf_op jit(solution)/shard_map/ppermute | solution.py:426
  6.4 9.3 %collective-permute-start.3 = (bf16[2,2,16,512]{3,2,1,0:T(8,128)(2,1)S(1)}, bf16[2,2,16,512]{3,2,1,0:T(8,128)(2,1)S(1)}, u32[]{:S(2)}, u32[]{:S(2)}) collective-permute-start(bf16[2,2,16,512]{3,2,1,0:T(8,128)(2,1)S(1)} %pad_maximum_fusion.1.refs_0_.refs_4_), channel_id=1, source_target_pairs={{0,24},{4,28},{1,25},{5,29},{2,26},{6,30},{3,27},{7,31}} | collective-permute-start | bytes 196616 | tf_op jit(solution)/shard_map/ppermute | solution.py:429
  12.0 3.8 %collective-permute-start.2 = (bf16[2,2,16,512]{3,2,1,0:T(8,128)(2,1)S(1)}, bf16[2,2,16,512]{3,2,1,0:T(8,128)(2,1)S(1)}, u32[]{:S(2)}, u32[]{:S(2)}) collective-permute-start(bf16[2,2,16,512]{3,2,1,0:T(8,128)(2,1)S(1)} %pad_maximum_fusion.1.refs_0_.refs_4_), channel_id=1, source_target_pairs={{0,16},{4,20},{8,24},{12,28},{1,17},{5,21},{9,25},{13,29},{2,18},{... | collective-permute-start | bytes 196616 | tf_op jit(solution)/shard_map/ppermute | solution.py:429
  13.3 4.4 %collective-permute-start.1 = (bf16[2,2,16,512]{3,2,1,0:T(8,128)(2,1)S(1)}, bf16[2,2,16,512]{3,2,1,0:T(8,128)(2,1)S(1)}, u32[]{:S(2)}, u32[]{:S(2)}) collective-permute-start(bf16[2,2,16,512]{3,2,1,0:T(8,128)(2,1)S(1)} %pad_maximum_fusion.1.refs_0_.refs_4_), channel_id=1, source_target_pairs={{0,8},{4,12},{8,16},{12,20},{16,24},{20,28},{1,9},{5,13},{9,17},{1... | collective-permute-start | bytes 196616 | tf_op jit(solution)/shard_map/ppermute | solution.py:429
  17.7 9.3 %collective-permute-start.10 = (bf16[3,2,2,16,512]{4,3,2,1,0:T(8,128)(2,1)S(1)}, bf16[3,2,2,16,512]{4,3,2,1,0:T(8,128)(2,1)S(1)}, u32[]{:S(2)}, u32[]{:S(2)}) collective-permute-start(bf16[3,2,2,16,512]{4,3,2,1,0:T(8,128)(2,1)S(1)} %pad_maximum_fusion.refs_1_), channel_id=1, source_target_pairs={{0,6},{1,7},{2,4},{3,5},{4,2},{5,3},{6,0},{7,1},{8,14},{9,15},{10,... | collective-permute-start | bytes 589832 | tf_op jit(solution)/shard_map/ppermute | solution.py:426
  20.2 9.5 %collective-permute-start.9 = (bf16[3,2,2,16,512]{4,3,2,1,0:T(8,128)(2,1)S(1)}, bf16[3,2,2,16,512]{4,3,2,1,0:T(8,128)(2,1)S(1)}, u32[]{:S(2)}, u32[]{:S(2)}) collective-permute-start(bf16[3,2,2,16,512]{4,3,2,1,0:T(8,128)(2,1)S(1)} %pad_maximum_fusion.refs_1_), channel_id=1, source_target_pairs={{0,2},{1,3},{2,0},{3,1},{4,6},{5,7},{6,4},{7,5},{8,10},{9,11},{10,... | collective-permute-start | bytes 589832 | tf_op jit(solution)/shard_map/ppermute | solution.py:426
  20.7 9.7 %collective-permute-start.7 = (bf16[3,2,2,16,512]{4,3,2,1,0:T(8,128)(2,1)S(1)}, bf16[3,2,2,16,512]{4,3,2,1,0:T(8,128)(2,1)S(1)}, u32[]{:S(2)}, u32[]{:S(2)}) collective-permute-start(bf16[3,2,2,16,512]{4,3,2,1,0:T(8,128)(2,1)S(1)} %pad_maximum_fusion.refs_1_), channel_id=1, source_target_pairs={{0,4},{1,5},{2,6},{3,7},{4,0},{5,1},{6,2},{7,3},{8,12},{9,13},{10,... | collective-permute-start | bytes 589832 | tf_op jit(solution)/shard_map/ppermute | solution.py:426
  21.2 9.9 %collective-permute-start.11 = (bf16[2,2,16,512]{3,2,1,0:T(8,128)(2,1)S(1)}, bf16[2,2,16,512]{3,2,1,0:T(8,128)(2,1)S(1)}, u32[]{:S(2)}, u32[]{:S(2)}) collective-permute-start(bf16[2,2,16,512]{3,2,1,0:T(8,128)(2,1)S(1)} %pad_maximum_fusion.1.refs_0_.refs_4_), channel_id=1, source_target_pairs={{0,6},{1,7},{2,4},{3,5},{4,2},{5,3},{6,0},{7,1},{8,14},{9,15},{10,... | collective-permute-start | bytes 196616 | tf_op jit(solution)/shard_map/ppermute | solution.py:426
  23.7 8.1 %collective-permute-start.8 = (bf16[2,2,16,512]{3,2,1,0:T(8,128)(2,1)S(1)}, bf16[2,2,16,512]{3,2,1,0:T(8,128)(2,1)S(1)}, u32[]{:S(2)}, u32[]{:S(2)}) collective-permute-start(bf16[2,2,16,512]{3,2,1,0:T(8,128)(2,1)S(1)} %pad_maximum_fusion.1.refs_0_.refs_4_), channel_id=1, source_target_pairs={{0,4},{1,5},{2,6},{3,7},{4,0},{5,1},{6,2},{7,3},{8,12},{9,13},{10,... | collective-permute-start | bytes 196616 | tf_op jit(solution)/shard_map/ppermute | solution.py:426
  35.9 7.5 %collective-permute-start.12 = (bf16[512,512]{1,0:T(8,128)(2,1)S(1)}, bf16[512,512]{1,0:T(8,128)(2,1)S(1)}, u32[]{:S(2)}, u32[]{:S(2)}) collective-permute-start(bf16[512,512]{1,0:T(8,128)(2,1)S(1)} %get-tuple-element.66.att_ref), channel_id=1, source_target_pairs={{0,1},{1,0},{2,3},{3,2},{4,5},{5,4},{6,7},{7,6},{8,9},{9,8},{10,11... | collective-permute-start | bytes 1572872 | tf_op jit(solution)/shard_map/ppermute | solution.py:426
  36.0 7.4 %collective-permute-start.13 = (bf16[3,2,2,16,512]{4,3,2,1,0:T(8,128)(2,1)S(1)}, bf16[3,2,2,16,512]{4,3,2,1,0:T(8,128)(2,1)S(1)}, u32[]{:S(2)}, u32[]{:S(2)}) collective-permute-start(bf16[3,2,2,16,512]{4,3,2,1,0:T(8,128)(2,1)S(1)} %slice.42), channel_id=1, source_target_pairs={{0,4},{1,5},{2,6},{3,7},{4,0},{5,1},{6,2},{7,3},{8,12},{9,13},{10,... | collective-permute-start | bytes 589832 | tf_op jit(solution)/shard_map/ppermute | solution.py:426
  43.4 6.2 %collective-permute-start.14 = (bf16[512,512]{1,0:T(8,128)(2,1)S(1)}, bf16[512,512]{1,0:T(8,128)(2,1)S(1)}, u32[]{:S(2)}, u32[]{:S(2)}) collective-permute-start(bf16[512,512]{1,0:T(8,128)(2,1)S(1)} %broadcast_add_fusion.gq_ref), channel_id=1, source_target_pairs={{0,1},{1,0},{2,3},{3,2},{4,5},{5,4},{6,7},{7,6},{8,9},{9,8},{10,11... | collective-permute-start | bytes 1572872 | tf_op jit(solution)/shard_map/ppermute | solution.py:426
  43.5 4.5 %collective-permute-start.15 = (bf16[256,512]{1,0:T(8,128)(2,1)S(1)}, bf16[256,512]{1,0:T(8,128)(2,1)S(1)}, u32[]{:S(2)}, u32[]{:S(2)}) collective-permute-start(bf16[256,512]{1,0:T(8,128)(2,1)S(1)} %broadcast_add_fusion.1), channel_id=1, source_target_pairs={{0,1},{1,0},{2,3},{3,2},{4,5},{5,4},{6,7},{7,6},{8,9},{9,8},{10,11... | collective-permute-start | bytes 786440 | tf_op jit(solution)/shard_map/ppermute | solution.py:426
  44.1 8.4 %collective-permute-start.18 = (bf16[2,2,16,512]{3,2,1,0:T(8,128)(2,1)S(1)}, bf16[2,2,16,512]{3,2,1,0:T(8,128)(2,1)S(1)}, u32[]{:S(2)}, u32[]{:S(2)}) collective-permute-start(bf16[2,2,16,512]{3,2,1,0:T(8,128)(2,1)S(1)} %get-tuple-element.92), channel_id=1, source_target_pairs={{24,0},{28,4},{25,1},{29,5},{26,2},{30,6},{27,3},{31,7}} | collective-permute-start | bytes 196616 | tf_op jit(solution)/shard_map/ppermute | solution.py:434
  45.4 9.5 %collective-permute-start.17 = (bf16[2,2,16,512]{3,2,1,0:T(8,128)(2,1)S(1)}, bf16[2,2,16,512]{3,2,1,0:T(8,128)(2,1)S(1)}, u32[]{:S(2)}, u32[]{:S(2)}) collective-permute-start(bf16[2,2,16,512]{3,2,1,0:T(8,128)(2,1)S(1)} %get-tuple-element.93), channel_id=1, source_target_pairs={{16,0},{20,4},{24,8},{28,12},{17,1},{21,5},{25,9},{29,13},{18,2},{... | collective-permute-start | bytes 196616 | tf_op jit(solution)/shard_map/ppermute | solution.py:434
  46.7 8.2 %collective-permute-start.16 = (bf16[2,2,16,512]{3,2,1,0:T(8,128)(2,1)S(1)}, bf16[2,2,16,512]{3,2,1,0:T(8,128)(2,1)S(1)}, u32[]{:S(2)}, u32[]{:S(2)}) collective-permute-start(bf16[2,2,16,512]{3,2,1,0:T(8,128)(2,1)S(1)} %get-tuple-element.94), channel_id=1, source_target_pairs={{8,0},{12,4},{16,8},{20,12},{24,16},{28,20},{9,1},{13,5},{17,9},{2... | collective-permute-start | bytes 196616 | tf_op jit(solution)/shard_map/ppermute | solution.py:434
  48.0 6.9 %collective-permute-start.19 = (bf16[1,2,2,16,512]{4,3,2,1,0:T(8,128)(2,1)S(1)}, bf16[1,2,2,16,512]{4,3,2,1,0:T(8,128)(2,1)S(1)}, u32[]{:S(2)}, u32[]{:S(2)}) collective-permute-start(bf16[1,2,2,16,512]{4,3,2,1,0:T(8,128)(2,1)S(1)} %slice.51), channel_id=1, source_target_pairs={{0,4},{1,5},{2,6},{3,7},{4,0},{5,1},{6,2},{7,3},{8,12},{9,13},{10,... | collective-permute-start | bytes 196616 | tf_op jit(solution)/shard_map/ppermute | solution.py:426
  54.9 1.3 %collective-permute-start.20 = (bf16[2,16,512]{2,1,0:T(8,128)(2,1)S(1)}, bf16[2,16,512]{2,1,0:T(8,128)(2,1)S(1)}, u32[]{:S(2)}, u32[]{:S(2)}) collective-permute-start(bf16[2,16,512]{2,1,0:T(8,128)(2,1)S(1)} %fusion.3), channel_id=1, source_target_pairs={{0,1},{1,0},{2,3},{3,2},{4,5},{5,4},{6,7},{7,6},{8,9},{9,8},{10,11... | collective-permute-start | bytes 98312 | tf_op jit(solution)/shard_map/ppermute | solution.py:426

commit v8 on v7

--- a/solution.py
+++ b/solution.py
@@ -463,7 +463,7 @@
     far_width = members * seq_count * part_tok
     far_pairs = HEADS // CORES * tok_rows * far_width
     roomy = far_width <= 512
-    far_plan = (tok_rows // 2, HEADS // CORES, 2 * GROUP) if roomy else (tok_rows // 8, 1, 1)
+    far_plan = (tok_rows // 2, HEADS // CORES, GROUP) if roomy else (tok_rows // 8, 1, 1)
 
     near_sum, near_stat, bias, queries, grad_out = call(
         functools.partial(near_forward_kernel, members, blk_len, part_tok, head_dim),

time: 57.3 us -> 57.3 us (level)
  no operation moved by 1% of the time
where the time goes in v8:
time: 57.3 us; the launch traced here: 57 us
  starting transfers between devices  28.2 us (49%)
  waiting for transfers between devices  14.9 us (26%)
  Pallas kernels  12.8 us (22%)
  between operations  0.84 us (1%)
    ppermute x15, starting transfers between devices, hop(): return lax.ppermute(part, ('seq', 'kv'), pairs)  15 us
    ppermute x15, waiting for transfers between devices, hop(): return lax.ppermute(part, ('seq', 'kv'), pairs)  9.33 us
    pallas_call x3, Pallas kernels, call(): pl.pallas_call(kernel, in_specs=in_specs or [WHOLE] * len(operands), out_...  9.29 us
    ppermute x3, starting transfers between devices, climb(): lax.ppermute(part, 'seq', [(s, s + COLUMNS * d) for s in range(seq_count...  9.27 us
    ppermute x3, starting transfers between devices, sink(): lax.ppermute(part, 'seq', [(s, s - COLUMNS * d) for s in range(COLUMNS *...  3.88 us
    ppermute x3, waiting for transfers between devices, sink(): lax.ppermute(part, 'seq', [(s, s - COLUMNS * d) for s in range(COLUMNS *...  3.75 us
    ppermute x3, waiting for transfers between devices, climb(): lax.ppermute(part, 'seq', [(s, s + COLUMNS * d) for s in range(seq_count...  1.87 us
    pallas_call x1, Pallas kernels, join(): pl.pallas_call(join_kernel, in_specs=[WHOLE] * len(operands), out_specs=[...  1.54 us
  transfers between devices with their start and end apart: 21, of which 9 were waited for; matrix products, arithmetic and copies ran while one was open for 0% of the time, Pallas kernels for 12%

profile of v8, /device:TPU:0, one launch (start us, length us, event | category | flops | bytes accessed | tf_op | source)
XLA Modules:
  0.0 57.0 jit_solution(4765013928678065526)
XLA Ops:
  0.6 1.2 %shard_map.84 = (bf16[2,8,16,512]{3,2,1,0:T(8,128)(2,1)S(1)}, bf16[2,8,16,512]{3,2,1,0:T(8,128)(2,1)S(1)}, bf16[2,16,512]{2,1,0:T(8,128)(2,1)S(1)}, bf16[2,16,512]{2,1,0:T(8,128)(2,1)S(1)}, f32[8,128]{1,0:T(8,128)S(1)}) custom-call(s32[15,64]{1,0:T(8,128)} %bitcast.38, bf16[8,16,1024]{2,1,0:T(8,128)(2,1)} %keys_hbm.1, bf16[8,16,1024]{2,1,0:T(8,128)(2,1)} %values_hbm.1), custom_call_target="tpu_custom_call" | custom-call | tf_op jit(solution)/shard_map/pallas_call | solution.py:74
  1.9 0.5 collective-permute-start.4
  2.5 2.9 %collective-permute-start.5 = (bf16[2,8,16,512]{3,2,1,0:T(8,128)(2,1)S(1)}, bf16[2,8,16,512]{3,2,1,0:T(8,128)(2,1)S(1)}, u32[]{:S(2)}, u32[]{:S(2)}) collective-permute-start(bf16[2,8,16,512]{3,2,1,0:T(8,128)(2,1)S(1)} %get-tuple-element.52), channel_id=1, source_target_pairs={{0,2},{1,3},{2,0},{3,1},{4,6},{5,7},{6,4},{7,5},{8,10},{9,11},{10,... | collective-permute-start | bytes 786440 | tf_op jit(solution)/shard_map/ppermute | solution.py:426
  5.4 1.0 %collective-permute-start.6 = (bf16[2,8,16,512]{3,2,1,0:T(8,128)(2,1)S(1)}, bf16[2,8,16,512]{3,2,1,0:T(8,128)(2,1)S(1)}, u32[]{:S(2)}, u32[]{:S(2)}) collective-permute-start(bf16[2,8,16,512]{3,2,1,0:T(8,128)(2,1)S(1)} %collective-permute-done.4), channel_id=1, source_target_pairs={{0,2},{1,3},{2,0},{3,1},{4,6},{5,7},{6,4},{7,5},{8,10},{9,11},{10,... | collective-permute-start | bytes 786440 | tf_op jit(solution)/shard_map/ppermute | solution.py:426
  6.4 5.5 %collective-permute-start.3 = (bf16[2,2,16,512]{3,2,1,0:T(8,128)(2,1)S(1)}, bf16[2,2,16,512]{3,2,1,0:T(8,128)(2,1)S(1)}, u32[]{:S(2)}, u32[]{:S(2)}) collective-permute-start(bf16[2,2,16,512]{3,2,1,0:T(8,128)(2,1)S(1)} %pad_maximum_fusion.1.refs_0_.refs_4_), channel_id=1, source_target_pairs={{0,24},{4,28},{1,25},{5,29},{2,26},{6,30},{3,27},{7,31}} | collective-permute-start | bytes 196616 | tf_op jit(solution)/shard_map/ppermute | solution.py:429
  12.0 1.3 %collective-permute-start.2 = (bf16[2,2,16,512]{3,2,1,0:T(8,128)(2,1)S(1)}, bf16[2,2,16,512]{3,2,1,0:T(8,128)(2,1)S(1)}, u32[]{:S(2)}, u32[]{:S(2)}) collective-permute-start(bf16[2,2,16,512]{3,2,1,0:T(8,128)(2,1)S(1)} %pad_maximum_fusion.1.refs_0_.refs_4_), channel_id=1, source_target_pairs={{0,16},{4,20},{8,24},{12,28},{1,17},{5,21},{9,25},{13,29},{2,18},{... | collective-permute-start | bytes 196616 | tf_op jit(solution)/shard_map/ppermute | solution.py:429
  13.3 2.5 %collective-permute-start.1 = (bf16[2,2,16,512]{3,2,1,0:T(8,128)(2,1)S(1)}, bf16[2,2,16,512]{3,2,1,0:T(8,128)(2,1)S(1)}, u32[]{:S(2)}, u32[]{:S(2)}) collective-permute-start(bf16[2,2,16,512]{3,2,1,0:T(8,128)(2,1)S(1)} %pad_maximum_fusion.1.refs_0_.refs_4_), channel_id=1, source_target_pairs={{0,8},{4,12},{8,16},{12,20},{16,24},{20,28},{1,9},{5,13},{9,17},{1... | collective-permute-start | bytes 196616 | tf_op jit(solution)/shard_map/ppermute | solution.py:429
  15.8 1.9 %collective-permute-done.1 = bf16[2,2,16,512]{3,2,1,0:T(8,128)(2,1)S(1)} collective-permute-done((bf16[2,2,16,512]{3,2,1,0:T(8,128)(2,1)S(1)}, bf16[2,2,16,512]{3,2,1,0:T(8,128)(2,1)S(1)}, u32[]{:S(2)}, u32[]{:S(2)}) %collective-permute-start.1) | collective-permute-done | bytes 65568 | tf_op jit(solution)/shard_map/ppermute | solution.py:429
  17.7 2.6 %collective-permute-start.10 = (bf16[3,2,2,16,512]{4,3,2,1,0:T(8,128)(2,1)S(1)}, bf16[3,2,2,16,512]{4,3,2,1,0:T(8,128)(2,1)S(1)}, u32[]{:S(2)}, u32[]{:S(2)}) collective-permute-start(bf16[3,2,2,16,512]{4,3,2,1,0:T(8,128)(2,1)S(1)} %pad_maximum_fusion.refs_1_), channel_id=1, source_target_pairs={{0,6},{1,7},{2,4},{3,5},{4,2},{5,3},{6,0},{7,1},{8,14},{9,15},{10,... | collective-permute-start | bytes 589832 | tf_op jit(solution)/shard_map/ppermute | solution.py:426
  20.2 0.5 collective-permute-start.9
  20.7 0.5 collective-permute-start.7
  21.2 2.5 %collective-permute-start.11 = (bf16[2,2,16,512]{3,2,1,0:T(8,128)(2,1)S(1)}, bf16[2,2,16,512]{3,2,1,0:T(8,128)(2,1)S(1)}, u32[]{:S(2)}, u32[]{:S(2)}) collective-permute-start(bf16[2,2,16,512]{3,2,1,0:T(8,128)(2,1)S(1)} %pad_maximum_fusion.1.refs_0_.refs_4_), channel_id=1, source_target_pairs={{0,6},{1,7},{2,4},{3,5},{4,2},{5,3},{6,0},{7,1},{8,14},{9,15},{10,... | collective-permute-start | bytes 196616 | tf_op jit(solution)/shard_map/ppermute | solution.py:426
  23.7 0.5 collective-permute-start.8
  24.3 2.7 %shard_map.85 = (f32[512,512]{1,0:T(8,128)S(1)}, f32[512,512]{1,0:T(8,128)S(1)}, f32[512,512]{1,0:T(8,128)S(1)}, bf16[512,512]{1,0:T(8,128)(2,1)S(1)}, bf16[512,512]{1,0:T(8,128)(2,1)S(1)}) custom-call(bf16[512,1024]{1,0:T(8,128)(2,1)} %q_hbm.1, bf16[512,1024]{1,0:T(8,128)(2,1)} %g_hbm.1, bf16[2,128,512]{2,1,0:T(8,128)(2,1)S(1)} %bitcast.24, ...), custom_call_target="tpu_custom_call" | custom-call | flops 1073741824 | bytes 3145728 | tf_op jit(solution)/shard_map/pallas_call | solution.py:395
  27.0 2.7 %collective-permute-done.9.refs_5_ = bf16[3,2,2,16,512]{4,3,2,1,0:T(8,128)(2,1)S(1)} collective-permute-done((bf16[3,2,2,16,512]{4,3,2,1,0:T(8,128)(2,1)S(1)}, bf16[3,2,2,16,512]{4,3,2,1,0:T(8,128)(2,1)S(1)}, u32[]{:S(2)}, u32[]{:S(2)}) %collective-permute-start.9) | collective-permute-done | bytes 196640 | tf_op jit(solution)/shard_map/ppermute | solution.py:426
  29.7 0.7 %collective-permute-done.7.refs_3_ = bf16[3,2,2,16,512]{4,3,2,1,0:T(8,128)(2,1)S(1)} collective-permute-done((bf16[3,2,2,16,512]{4,3,2,1,0:T(8,128)(2,1)S(1)}, bf16[3,2,2,16,512]{4,3,2,1,0:T(8,128)(2,1)S(1)}, u32[]{:S(2)}, u32[]{:S(2)}) %collective-permute-start.7) | collective-permute-done | bytes 196640 | tf_op jit(solution)/shard_map/ppermute | solution.py:426
  30.5 0.7 %collective-permute-done.11.refs_6_ = bf16[2,2,16,512]{3,2,1,0:T(8,128)(2,1)S(1)} collective-permute-done((bf16[2,2,16,512]{3,2,1,0:T(8,128)(2,1)S(1)}, bf16[2,2,16,512]{3,2,1,0:T(8,128)(2,1)S(1)}, u32[]{:S(2)}, u32[]{:S(2)}) %collective-permute-start.11) | collective-permute-done | bytes 65568 | tf_op jit(solution)/shard_map/ppermute | solution.py:426
  31.2 0.7 %collective-permute-done.8.refs_2_ = bf16[2,2,16,512]{3,2,1,0:T(8,128)(2,1)S(1)} collective-permute-done((bf16[2,2,16,512]{3,2,1,0:T(8,128)(2,1)S(1)}, bf16[2,2,16,512]{3,2,1,0:T(8,128)(2,1)S(1)}, u32[]{:S(2)}, u32[]{:S(2)}) %collective-permute-start.8) | collective-permute-done | bytes 65568 | tf_op jit(solution)/shard_map/ppermute | solution.py:426
  31.9 4.0 %shard_map.86 = (bf16[512,512]{1,0:T(8,128)(2,1)S(1)}, f32[512,512]{1,0:T(8,128)S(1)}, f32[512,512]{1,0:T(8,128)S(1)}, f32[512,512]{1,0:T(8,128)S(1)}, bf16[4,2,...) custom-call(bf16[512,512]{1,0:T(8,128)(2,1)S(1)} %get-tuple-element.56.q_ref, ...), custom_call_target="tpu_custom_call" | custom-call | flops 2684354560 | bytes 4194304 | tf_op jit(solution)/shard_map/pallas_call | solution.py:395
  36.0 1.6 %collective-permute-start.13 = (bf16[3,2,2,16,512]{4,3,2,1,0:T(8,128)(2,1)S(1)}, bf16[3,2,2,16,512]{4,3,2,1,0:T(8,128)(2,1)S(1)}, u32[]{:S(2)}, u32[]{:S(2)}) collective-permute-start(bf16[3,2,2,16,512]{4,3,2,1,0:T(8,128)(2,1)S(1)} %slice.42), channel_id=1, source_target_pairs={{0,4},{1,5},{2,6},{3,7},{4,0},{5,1},{6,2},{7,3},{8,12},{9,13},{10,... | collective-permute-start | bytes 589832 | tf_op jit(solution)/shard_map/ppermute | solution.py:426
  37.5 2.5 %shard_map.87 = (f32[2,2,16,512]{3,2,1,0:T(8,128)S(1)}, bf16[256,512]{1,0:T(8,128)(2,1)S(1)}, bf16[512,512]{1,0:T(8,128)(2,1)S(1)}, bf16[256,512]{1,0:T(8,128)(2,1)S(1)}) custom-call(f32[8,128]{1,0:T(8,128)S(1)} %get-tuple-element.67.block_ref, f32[512,512]{1,0:T(8,128)S(1)} %get-tuple-element.68.bias_ref, bf16[512,512]{1,0:T(8,128)(2,1)S(1)} %get-tuple-element.56.q_ref, ...), custom_call_target="tpu_custom_call" | custom-call | flops 2147483648 | bytes 6295552 | tf_op jit(solution)/shard_map/pallas_call | solution.py:395
  40.1 3.3 %collective-permute-done.13 = bf16[3,2,2,16,512]{4,3,2,1,0:T(8,128)(2,1)S(1)} collective-permute-done((bf16[3,2,2,16,512]{4,3,2,1,0:T(8,128)(2,1)S(1)}, bf16[3,2,2,16,512]{4,3,2,1,0:T(8,128)(2,1)S(1)}, u32[]{:S(2)}, u32[]{:S(2)}) %collective-permute-start.13) | collective-permute-done | bytes 196640 | tf_op jit(solution)/shard_map/ppermute | solution.py:426
  43.5 0.6 collective-permute-start.15
  44.2 1.3 %collective-permute-start.18 = (bf16[2,2,16,512]{3,2,1,0:T(8,128)(2,1)S(1)}, bf16[2,2,16,512]{3,2,1,0:T(8,128)(2,1)S(1)}, u32[]{:S(2)}, u32[]{:S(2)}) collective-permute-start(bf16[2,2,16,512]{3,2,1,0:T(8,128)(2,1)S(1)} %get-tuple-element.92), channel_id=1, source_target_pairs={{24,0},{28,4},{25,1},{29,5},{26,2},{30,6},{27,3},{31,7}} | collective-permute-start | bytes 196616 | tf_op jit(solution)/shard_map/ppermute | solution.py:434
  45.5 1.3 %collective-permute-start.17 = (bf16[2,2,16,512]{3,2,1,0:T(8,128)(2,1)S(1)}, bf16[2,2,16,512]{3,2,1,0:T(8,128)(2,1)S(1)}, u32[]{:S(2)}, u32[]{:S(2)}) collective-permute-start(bf16[2,2,16,512]{3,2,1,0:T(8,128)(2,1)S(1)} %get-tuple-element.93), channel_id=1, source_target_pairs={{16,0},{20,4},{24,8},{28,12},{17,1},{21,5},{25,9},{29,13},{18,2},{... | collective-permute-start | bytes 196616 | tf_op jit(solution)/shard_map/ppermute | solution.py:434
  46.8 1.3 %collective-permute-start.16 = (bf16[2,2,16,512]{3,2,1,0:T(8,128)(2,1)S(1)}, bf16[2,2,16,512]{3,2,1,0:T(8,128)(2,1)S(1)}, u32[]{:S(2)}, u32[]{:S(2)}) collective-permute-start(bf16[2,2,16,512]{3,2,1,0:T(8,128)(2,1)S(1)} %get-tuple-element.94), channel_id=1, source_target_pairs={{8,0},{12,4},{16,8},{20,12},{24,16},{28,20},{9,1},{13,5},{17,9},{2... | collective-permute-start | bytes 196616 | tf_op jit(solution)/shard_map/ppermute | solution.py:434
  48.1 1.6 %collective-permute-start.19 = (bf16[1,2,2,16,512]{4,3,2,1,0:T(8,128)(2,1)S(1)}, bf16[1,2,2,16,512]{4,3,2,1,0:T(8,128)(2,1)S(1)}, u32[]{:S(2)}, u32[]{:S(2)}) collective-permute-start(bf16[1,2,2,16,512]{4,3,2,1,0:T(8,128)(2,1)S(1)} %slice.51), channel_id=1, source_target_pairs={{0,4},{1,5},{2,6},{3,7},{4,0},{5,1},{6,2},{7,3},{8,12},{9,13},{10,... | collective-permute-start | bytes 196616 | tf_op jit(solution)/shard_map/ppermute | solution.py:426
  49.6 1.5 %shard_map.88 = (bf16[512,1024]{1,0:T(8,128)(2,1)}, bf16[512,1024]{1,0:T(8,128)(2,1)}, bf16[128,1024]{1,0:T(8,128)(2,1)}, bf16[128,1024]{1,0:T(8,128)(2,1)}) custom-call(bf16[512,512]{1,0:T(8,128)(2,1)S(1)} %get-tuple-element.66.att_ref, bf16[512,512]{1,0:T(8,128)(2,1)S(1)} %collective-permute-done.12.att_far, ...), custom_call_target="tpu_custom_call" | custom-call | tf_op jit(solution)/shard_map/pallas_call | solution.py:107
  51.2 1.4 %collective-permute-done.18.refs_2_ = bf16[2,2,16,512]{3,2,1,0:T(8,128)(2,1)S(1)} collective-permute-done((bf16[2,2,16,512]{3,2,1,0:T(8,128)(2,1)S(1)}, bf16[2,2,16,512]{3,2,1,0:T(8,128)(2,1)S(1)}, u32[]{:S(2)}, u32[]{:S(2)}) %collective-permute-start.18) | collective-permute-done | bytes 65568 | tf_op jit(solution)/shard_map/ppermute | solution.py:434
  52.6 2.4 %collective-permute-done.17.refs_1_ = bf16[2,2,16,512]{3,2,1,0:T(8,128)(2,1)S(1)} collective-permute-done((bf16[2,2,16,512]{3,2,1,0:T(8,128)(2,1)S(1)}, bf16[2,2,16,512]{3,2,1,0:T(8,128)(2,1)S(1)}, u32[]{:S(2)}, u32[]{:S(2)}) %collective-permute-start.17) | collective-permute-done | bytes 65568 | tf_op jit(solution)/shard_map/ppermute | solution.py:434
  55.0 1.2 %collective-permute-done.20.far_ref = bf16[2,16,512]{2,1,0:T(8,128)(2,1)S(1)} collective-permute-done((bf16[2,16,512]{2,1,0:T(8,128)(2,1)S(1)}, bf16[2,16,512]{2,1,0:T(8,128)(2,1)S(1)}, u32[]{:S(2)}, u32[]{:S(2)}) %collective-permute-start.20) | collective-permute-done | bytes 32800 | tf_op jit(solution)/shard_map/ppermute | solution.py:426
  56.2 0.8 %shard_map.89 = (bf16[128,1024]{1,0:T(8,128)(2,1)}, bf16[128,1024]{1,0:T(8,128)(2,1)}) custom-call(f32[8,128]{1,0:T(8,128)S(1)} %get-tuple-element.67.block_ref, f32[2,2,16,512]{3,2,1,0:T(8,128)S(1)} %get-tuple-element.74.chosen_ref, bf16[2,16,512]{2,1,0:T(8,128)(2,1)S(1)} %collective-permute-done.20.far_ref, ...), custom_call_target="tpu_custom_call", output_to_operand_aliasing={{0}: (7, {}), {1}: (8, {})} | custom-call | tf_op jit(solution)/shard_map/pallas_call | solution.py:142
  (25 shorter events, 0.5 us)
Async XLA Ops:
  1.9 3.5 %collective-permute-start.4 = (bf16[2,8,16,512]{3,2,1,0:T(8,128)(2,1)S(1)}, bf16[2,8,16,512]{3,2,1,0:T(8,128)(2,1)S(1)}, u32[]{:S(2)}, u32[]{:S(2)}) collective-permute-start(bf16[2,8,16,512]{3,2,1,0:T(8,128)(2,1)S(1)} %get-tuple-element.51), channel_id=1, source_target_pairs={{0,1},{1,0},{2,3},{3,2},{4,5},{5,4},{6,7},{7,6},{8,9},{9,8},{10,11... | collective-permute-start | bytes 786440 | tf_op jit(solution)/shard_map/ppermute | solution.py:426
  2.4 4.1 %collective-permute-start = (bf16[2,16,512]{2,1,0:T(8,128)(2,1)S(1)}, bf16[2,16,512]{2,1,0:T(8,128)(2,1)S(1)}, u32[]{:S(2)}, u32[]{:S(2)}) collective-permute-start(bf16[2,16,512]{2,1,0:T(8,128)(2,1)S(1)} %get-tuple-element.49), channel_id=1, source_target_pairs={{0,1},{1,0},{2,3},{3,2},{4,5},{5,4},{6,7},{7,6},{8,9},{9,8},{10,11... | collective-permute-start | bytes 98312 | tf_op jit(solution)/shard_map/ppermute | solution.py:426
  2.5 15.2 %collective-permute-start.5 = (bf16[2,8,16,512]{3,2,1,0:T(8,128)(2,1)S(1)}, bf16[2,8,16,512]{3,2,1,0:T(8,128)(2,1)S(1)}, u32[]{:S(2)}, u32[]{:S(2)}) collective-permute-start(bf16[2,8,16,512]{3,2,1,0:T(8,128)(2,1)S(1)} %get-tuple-element.52), channel_id=1, source_target_pairs={{0,2},{1,3},{2,0},{3,1},{4,6},{5,7},{6,4},{7,5},{8,10},{9,11},{10,... | collective-permute-start | bytes 786440 | tf_op jit(solution)/shard_map/ppermute | solution.py:426
  5.4 12.3 %collective-permute-start.6 = (bf16[2,8,16,512]{3,2,1,0:T(8,128)(2,1)S(1)}, bf16[2,8,16,512]{3,2,1,0:T(8,128)(2,1)S(1)}, u32[]{:S(2)}, u32[]{:S(2)}) collective-permute-start(bf16[2,8,16,512]{3,2,1,0:T(8,128)(2,1)S(1)} %collective-permute-done.4), channel_id=1, source_target_pairs={{0,2},{1,3},{2,0},{3,1},{4,6},{5,7},{6,4},{7,5},{8,10},{9,11},{10,... | collective-permute-start | bytes 786440 | tf_op jit(solution)/shard_map/ppermute | solution.py:426
  6.4 9.3 %collective-permute-start.3 = (bf16[2,2,16,512]{3,2,1,0:T(8,128)(2,1)S(1)}, bf16[2,2,16,512]{3,2,1,0:T(8,128)(2,1)S(1)}, u32[]{:S(2)}, u32[]{:S(2)}) collective-permute-start(bf16[2,2,16,512]{3,2,1,0:T(8,128)(2,1)S(1)} %pad_maximum_fusion.1.refs_0_.refs_4_), channel_id=1, source_target_pairs={{0,24},{4,28},{1,25},{5,29},{2,26},{6,30},{3,27},{7,31}} | collective-permute-start | bytes 196616 | tf_op jit(solution)/shard_map/ppermute | solution.py:429
  12.0 3.8 %collective-permute-start.2 = (bf16[2,2,16,512]{3,2,1,0:T(8,128)(2,1)S(1)}, bf16[2,2,16,512]{3,2,1,0:T(8,128)(2,1)S(1)}, u32[]{:S(2)}, u32[]{:S(2)}) collective-permute-start(bf16[2,2,16,512]{3,2,1,0:T(8,128)(2,1)S(1)} %pad_maximum_fusion.1.refs_0_.refs_4_), channel_id=1, source_target_pairs={{0,16},{4,20},{8,24},{12,28},{1,17},{5,21},{9,25},{13,29},{2,18},{... | collective-permute-start | bytes 196616 | tf_op jit(solution)/shard_map/ppermute | solution.py:429
  13.3 4.4 %collective-permute-start.1 = (bf16[2,2,16,512]{3,2,1,0:T(8,128)(2,1)S(1)}, bf16[2,2,16,512]{3,2,1,0:T(8,128)(2,1)S(1)}, u32[]{:S(2)}, u32[]{:S(2)}) collective-permute-start(bf16[2,2,16,512]{3,2,1,0:T(8,128)(2,1)S(1)} %pad_maximum_fusion.1.refs_0_.refs_4_), channel_id=1, source_target_pairs={{0,8},{4,12},{8,16},{12,20},{16,24},{20,28},{1,9},{5,13},{9,17},{1... | collective-permute-start | bytes 196616 | tf_op jit(solution)/shard_map/ppermute | solution.py:429
  17.7 9.3 %collective-permute-start.10 = (bf16[3,2,2,16,512]{4,3,2,1,0:T(8,128)(2,1)S(1)}, bf16[3,2,2,16,512]{4,3,2,1,0:T(8,128)(2,1)S(1)}, u32[]{:S(2)}, u32[]{:S(2)}) collective-permute-start(bf16[3,2,2,16,512]{4,3,2,1,0:T(8,128)(2,1)S(1)} %pad_maximum_fusion.refs_1_), channel_id=1, source_target_pairs={{0,6},{1,7},{2,4},{3,5},{4,2},{5,3},{6,0},{7,1},{8,14},{9,15},{10,... | collective-permute-start | bytes 589832 | tf_op jit(solution)/shard_map/ppermute | solution.py:426
  20.2 9.5 %collective-permute-start.9 = (bf16[3,2,2,16,512]{4,3,2,1,0:T(8,128)(2,1)S(1)}, bf16[3,2,2,16,512]{4,3,2,1,0:T(8,128)(2,1)S(1)}, u32[]{:S(2)}, u32[]{:S(2)}) collective-permute-start(bf16[3,2,2,16,512]{4,3,2,1,0:T(8,128)(2,1)S(1)} %pad_maximum_fusion.refs_1_), channel_id=1, source_target_pairs={{0,2},{1,3},{2,0},{3,1},{4,6},{5,7},{6,4},{7,5},{8,10},{9,11},{10,... | collective-permute-start | bytes 589832 | tf_op jit(solution)/shard_map/ppermute | solution.py:426
  20.7 9.7 %collective-permute-start.7 = (bf16[3,2,2,16,512]{4,3,2,1,0:T(8,128)(2,1)S(1)}, bf16[3,2,2,16,512]{4,3,2,1,0:T(8,128)(2,1)S(1)}, u32[]{:S(2)}, u32[]{:S(2)}) collective-permute-start(bf16[3,2,2,16,512]{4,3,2,1,0:T(8,128)(2,1)S(1)} %pad_maximum_fusion.refs_1_), channel_id=1, source_target_pairs={{0,4},{1,5},{2,6},{3,7},{4,0},{5,1},{6,2},{7,3},{8,12},{9,13},{10,... | collective-permute-start | bytes 589832 | tf_op jit(solution)/shard_map/ppermute | solution.py:426
  21.2 9.9 %collective-permute-start.11 = (bf16[2,2,16,512]{3,2,1,0:T(8,128)(2,1)S(1)}, bf16[2,2,16,512]{3,2,1,0:T(8,128)(2,1)S(1)}, u32[]{:S(2)}, u32[]{:S(2)}) collective-permute-start(bf16[2,2,16,512]{3,2,1,0:T(8,128)(2,1)S(1)} %pad_maximum_fusion.1.refs_0_.refs_4_), channel_id=1, source_target_pairs={{0,6},{1,7},{2,4},{3,5},{4,2},{5,3},{6,0},{7,1},{8,14},{9,15},{10,... | collective-permute-start | bytes 196616 | tf_op jit(solution)/shard_map/ppermute | solution.py:426
  23.7 8.1 %collective-permute-start.8 = (bf16[2,2,16,512]{3,2,1,0:T(8,128)(2,1)S(1)}, bf16[2,2,16,512]{3,2,1,0:T(8,128)(2,1)S(1)}, u32[]{:S(2)}, u32[]{:S(2)}) collective-permute-start(bf16[2,2,16,512]{3,2,1,0:T(8,128)(2,1)S(1)} %pad_maximum_fusion.1.refs_0_.refs_4_), channel_id=1, source_target_pairs={{0,4},{1,5},{2,6},{3,7},{4,0},{5,1},{6,2},{7,3},{8,12},{9,13},{10,... | collective-permute-start | bytes 196616 | tf_op jit(solution)/shard_map/ppermute | solution.py:426
  35.9 7.5 %collective-permute-start.12 = (bf16[512,512]{1,0:T(8,128)(2,1)S(1)}, bf16[512,512]{1,0:T(8,128)(2,1)S(1)}, u32[]{:S(2)}, u32[]{:S(2)}) collective-permute-start(bf16[512,512]{1,0:T(8,128)(2,1)S(1)} %get-tuple-element.66.att_ref), channel_id=1, source_target_pairs={{0,1},{1,0},{2,3},{3,2},{4,5},{5,4},{6,7},{7,6},{8,9},{9,8},{10,11... | collective-permute-start | bytes 1572872 | tf_op jit(solution)/shard_map/ppermute | solution.py:426
  36.0 7.4 %collective-permute-start.13 = (bf16[3,2,2,16,512]{4,3,2,1,0:T(8,128)(2,1)S(1)}, bf16[3,2,2,16,512]{4,3,2,1,0:T(8,128)(2,1)S(1)}, u32[]{:S(2)}, u32[]{:S(2)}) collective-permute-start(bf16[3,2,2,16,512]{4,3,2,1,0:T(8,128)(2,1)S(1)} %slice.42), channel_id=1, source_target_pairs={{0,4},{1,5},{2,6},{3,7},{4,0},{5,1},{6,2},{7,3},{8,12},{9,13},{10,... | collective-permute-start | bytes 589832 | tf_op jit(solution)/shard_map/ppermute | solution.py:426
  43.4 6.2 %collective-permute-start.14 = (bf16[512,512]{1,0:T(8,128)(2,1)S(1)}, bf16[512,512]{1,0:T(8,128)(2,1)S(1)}, u32[]{:S(2)}, u32[]{:S(2)}) collective-permute-start(bf16[512,512]{1,0:T(8,128)(2,1)S(1)} %broadcast_add_fusion.gq_ref), channel_id=1, source_target_pairs={{0,1},{1,0},{2,3},{3,2},{4,5},{5,4},{6,7},{7,6},{8,9},{9,8},{10,11... | collective-permute-start | bytes 1572872 | tf_op jit(solution)/shard_map/ppermute | solution.py:426
  43.5 4.5 %collective-permute-start.15 = (bf16[256,512]{1,0:T(8,128)(2,1)S(1)}, bf16[256,512]{1,0:T(8,128)(2,1)S(1)}, u32[]{:S(2)}, u32[]{:S(2)}) collective-permute-start(bf16[256,512]{1,0:T(8,128)(2,1)S(1)} %broadcast_add_fusion.1), channel_id=1, source_target_pairs={{0,1},{1,0},{2,3},{3,2},{4,5},{5,4},{6,7},{7,6},{8,9},{9,8},{10,11... | collective-permute-start | bytes 786440 | tf_op jit(solution)/shard_map/ppermute | solution.py:426
  44.2 8.4 %collective-permute-start.18 = (bf16[2,2,16,512]{3,2,1,0:T(8,128)(2,1)S(1)}, bf16[2,2,16,512]{3,2,1,0:T(8,128)(2,1)S(1)}, u32[]{:S(2)}, u32[]{:S(2)}) collective-permute-start(bf16[2,2,16,512]{3,2,1,0:T(8,128)(2,1)S(1)} %get-tuple-element.92), channel_id=1, source_target_pairs={{24,0},{28,4},{25,1},{29,5},{26,2},{30,6},{27,3},{31,7}} | collective-permute-start | bytes 196616 | tf_op jit(solution)/shard_map/ppermute | solution.py:434
  45.5 9.5 %collective-permute-start.17 = (bf16[2,2,16,512]{3,2,1,0:T(8,128)(2,1)S(1)}, bf16[2,2,16,512]{3,2,1,0:T(8,128)(2,1)S(1)}, u32[]{:S(2)}, u32[]{:S(2)}) collective-permute-start(bf16[2,2,16,512]{3,2,1,0:T(8,128)(2,1)S(1)} %get-tuple-element.93), channel_id=1, source_target_pairs={{16,0},{20,4},{24,8},{28,12},{17,1},{21,5},{25,9},{29,13},{18,2},{... | collective-permute-start | bytes 196616 | tf_op jit(solution)/shard_map/ppermute | solution.py:434
  46.8 8.2 %collective-permute-start.16 = (bf16[2,2,16,512]{3,2,1,0:T(8,128)(2,1)S(1)}, bf16[2,2,16,512]{3,2,1,0:T(8,128)(2,1)S(1)}, u32[]{:S(2)}, u32[]{:S(2)}) collective-permute-start(bf16[2,2,16,512]{3,2,1,0:T(8,128)(2,1)S(1)} %get-tuple-element.94), channel_id=1, source_target_pairs={{8,0},{12,4},{16,8},{20,12},{24,16},{28,20},{9,1},{13,5},{17,9},{2... | collective-permute-start | bytes 196616 | tf_op jit(solution)/shard_map/ppermute | solution.py:434
  48.1 6.9 %collective-permute-start.19 = (bf16[1,2,2,16,512]{4,3,2,1,0:T(8,128)(2,1)S(1)}, bf16[1,2,2,16,512]{4,3,2,1,0:T(8,128)(2,1)S(1)}, u32[]{:S(2)}, u32[]{:S(2)}) collective-permute-start(bf16[1,2,2,16,512]{4,3,2,1,0:T(8,128)(2,1)S(1)} %slice.51), channel_id=1, source_target_pairs={{0,4},{1,5},{2,6},{3,7},{4,0},{5,1},{6,2},{7,3},{8,12},{9,13},{10,... | collective-permute-start | bytes 196616 | tf_op jit(solution)/shard_map/ppermute | solution.py:426
  55.0 1.3 %collective-permute-start.20 = (bf16[2,16,512]{2,1,0:T(8,128)(2,1)S(1)}, bf16[2,16,512]{2,1,0:T(8,128)(2,1)S(1)}, u32[]{:S(2)}, u32[]{:S(2)}) collective-permute-start(bf16[2,16,512]{2,1,0:T(8,128)(2,1)S(1)} %fusion.3), channel_id=1, source_target_pairs={{0,1},{1,0},{2,3},{3,2},{4,5},{5,4},{6,7},{7,6},{8,9},{9,8},{10,11... | collective-permute-start | bytes 98312 | tf_op jit(solution)/shard_map/ppermute | solution.py:426
